TPU v7x, 32 devices: a whole 2x2x4 slice. The times are simulated.
32 devices in a mesh: win: 2 (over y), pair: 4 (over z), stk: 2 (over x), lag: 2 (over core).
Axes of the slice: x: 2, y: 2, z: 4, core: 2. Of those that a mesh axis runs over, the one named last changes fastest.
Arguments:
- spectra: bfloat16 [32, 4, 256, 1024], P('win', 'pair', 'stk'), parts along dimension 0, may hold values from -40 to 40
- pair_blocks: int32 [8, 40, 2], P('win'), parts along dimension 0, may hold values from 0 to 63, as said below
- live_pairs: int32 [8], P('win'), parts along dimension 0, may hold values from 10 to 40, as said below
- stack_group: int32 [8, 40], P('win'), parts along dimension 0, may hold values from 0 to 3, as said below
Outputs:
- stacks: float32 [8, 256, 1024], P('win', 'stk', ('pair', 'lag')), parts along dimension 0
There are 2 independent parts, one for each index of `win`. A program takes and returns all parts, laid end to end along the dimension named above; each array names one. Nothing has to cross between parts.
Inputs may be any that keep to these rules, and one draw needn't show every extreme that they name: `pair_blocks`: every pair names a first block and a second block 1 to 8 higher. The pairs of all 40 slots of one owner span exactly 32 consecutive blocks, from the smallest first block to the largest second block. An owner's first live_pairs slots are used, the rest are not. Some owner uses all 40. `stack_group`: in the first 4 slots of every owner each group stands once.
All inputs are finite; a program needn't handle non-finite values.
Results may differ from a plain program's by a relative error of at most 0.0058.
Values may be sent and summed in bfloat16 or wider, within the bound.
No kernel may reach another device: no remote copies, remote signals or barrier semaphores. Data moves between devices by JAX's collectives and lax.ppermute only.
A program may use at most 128 MiB of HBM per device.

v0:
```python
import math

import jax
import jax.numpy as jnp
from jax import lax
from jax.sharding import PartitionSpec as P

NGRP = 4
HW = 15


AMP_FLOOR = 0.5
EPSILON = 1e-06
SLOT_GROUP = 8


def padded_2(cells, sides, width):
    for axis, dim in sides:
        count = lax.axis_size(axis)
        ends = count - 1
        head = lax.slice_in_dim(cells, 0, width, axis=dim)
        tail = lax.slice_in_dim(cells, cells.shape[dim] - width, cells.shape[dim], axis=dim)
        cells = jnp.concatenate(
            [
                lax.ppermute(tail, axis, [(i, (i + 1) % count) for i in range(ends)]),
                cells,
                lax.ppermute(head, axis, [((i + 1) % count, i) for i in range(ends)]),
            ],
            axis=dim,
        )
    return cells


def lag_table(lag_ids, num_bins):
    bin_index = jnp.arange(num_bins, dtype=jnp.int32)[:, None]
    phase_turns = bin_index * (lag_ids[None, :] + num_bins) % (2 * num_bins)
    angles = phase_turns.astype(jnp.float32) * (math.pi / num_bins)
    cosine = jnp.cos(angles)
    sine_part = jnp.sin(angles)
    amp_scale = math.sqrt(2.0 / num_bins)
    upper_rows = jnp.concatenate([cosine, sine_part], axis=1)
    lower_rows = jnp.concatenate([-sine_part, cosine], axis=1)
    return (jnp.concatenate([upper_rows, lower_rows], axis=0) * amp_scale).astype(jnp.bfloat16)


def whiten_blocks(spectra):
    values = spectra.astype(jnp.float32)
    channel_power = jnp.mean(values * values, axis=-1, keepdims=True) * 2.0
    return (values / jnp.sqrt(channel_power + EPSILON)).astype(jnp.bfloat16)


def cross_spectra(first_spec, second_spec, num_bins):
    first_spec = first_spec.astype(jnp.float32)
    second_spec = second_spec.astype(jnp.float32)
    real_a = first_spec[..., :num_bins]
    imag_a = first_spec[..., num_bins:]
    real_b = second_spec[..., :num_bins]
    imag_b = second_spec[..., num_bins:]
    real_part = real_a * real_b + imag_a * imag_b
    imag_part = imag_a * real_b - real_a * imag_b
    return jnp.concatenate([real_part, imag_part], axis=-1).astype(jnp.bfloat16)


def phase_terms(correlation, half_lags):
    direct = correlation[:, :half_lags]
    quadrature = correlation[:, half_lags:]
    divisor = jnp.maximum(jnp.sqrt(direct * direct + quadrature * quadrature), AMP_FLOOR)
    return jnp.stack([direct, direct / divisor, quadrature / divisor], axis=1)


def shards(spectra, pair_blocks, live_pairs, stack_group):
    owners = lax.axis_size("pair")
    owner_index = lax.axis_index("pair")
    lag_parts = lax.axis_size("lag")
    lag_index = lax.axis_index("lag")
    local_blocks = spectra.shape[0]
    channels = spectra.shape[2]
    row_width = spectra.shape[3]
    num_bins = row_width // 2
    lag_count = 2 * num_bins
    half_lags = lag_count // lag_parts
    piece_lags = half_lags // owners
    column = jnp.arange(half_lags, dtype=jnp.int32)
    lag_ids = (
        column // piece_lags * (lag_parts * piece_lags)
        + lag_index * piece_lags
        + column % piece_lags
    )
    lag_weights = lag_table(lag_ids, num_bins)
    whitened = whiten_blocks(spectra)
    all_blocks = local_blocks * owners
    gathered = lax.all_gather(whitened, "pair", axis=1, tiled=True)
    spectra_rows = gathered.reshape(all_blocks, channels, row_width)
    my_pairs = lax.dynamic_index_in_dim(pair_blocks, owner_index, 0, keepdims=False)
    my_groups = lax.dynamic_index_in_dim(stack_group, owner_index, 0, keepdims=False)
    my_live = lax.dynamic_index_in_dim(live_pairs, owner_index, 0, keepdims=False)
    first_rows = my_pairs[:, 0]
    second_rows = my_pairs[:, 1]
    slot_total = pair_blocks.shape[1]
    slot_index = jnp.arange(slot_total, dtype=jnp.int32)
    group_index = jnp.arange(NGRP, dtype=jnp.int32)
    weights_all = (
        (my_groups[:, None] == group_index[None, :]) & (slot_index < my_live)[:, None]
    ).astype(jnp.float32)

    def add_slots(step_index, group_sums):
        slot_start = step_index * SLOT_GROUP
        first_ids = lax.dynamic_slice_in_dim(first_rows, slot_start, SLOT_GROUP)
        second_ids = lax.dynamic_slice_in_dim(second_rows, slot_start, SLOT_GROUP)
        first_spec = jnp.take(spectra_rows, first_ids, axis=0)
        second_spec = jnp.take(spectra_rows, second_ids, axis=0)
        cross_rows = cross_spectra(first_spec, second_spec, num_bins).reshape(
            SLOT_GROUP * channels, row_width
        )
        correlation = jnp.dot(cross_rows, lag_weights, preferred_element_type=jnp.float32)
        phase_rows = phase_terms(correlation, half_lags).reshape(
            SLOT_GROUP, channels * 3 * half_lags
        )
        slot_weights = lax.dynamic_slice_in_dim(weights_all, slot_start, SLOT_GROUP)
        return group_sums + jnp.dot(slot_weights.T, phase_rows, precision=lax.Precision.HIGHEST)

    initial = jnp.zeros((NGRP, channels * 3 * half_lags), jnp.float32)
    group_sums = lax.fori_loop(0, slot_total // SLOT_GROUP, add_slots, initial)
    group_sums = group_sums.reshape(NGRP, channels, 3, half_lags)
    totals = lax.psum(group_sums, "pair")
    shares = lax.dynamic_slice_in_dim(totals, owner_index * piece_lags, piece_lags, 3)
    live_mask = jnp.arange(slot_total, dtype=jnp.int32)[None, :] < live_pairs[:, None]
    member = (stack_group[:, :, None] == group_index[None, None, :]) & live_mask[:, :, None]
    members = jnp.sum(member.astype(jnp.float32), axis=(0, 1))
    norm_root = jnp.sqrt(members)[:, None, None]
    linear = shares[:, :, 0] / norm_root
    coherence = (
        jnp.sqrt(shares[:, :, 1] * shares[:, :, 1] + shares[:, :, 2] * shares[:, :, 2]) / norm_root
    )
    padded = padded_2(coherence, ((("pair", "lag"), 2),), HW)
    smoothed = jnp.zeros_like(coherence)
    for offset_tap in range(2 * HW + 1):
        smoothed = smoothed + padded[:, :, offset_tap : offset_tap + piece_lags]
    smoothed = smoothed / (2 * HW + 1)
    return linear * smoothed * smoothed


def solution(mesh):
    return jax.shard_map(
        shards,
        mesh=mesh,
        in_specs=(P("win", "pair", "stk", None), P("win", None, None), P("win"), P("win", None)),
        out_specs=P("win", "stk", ("pair", "lag")),
        check_vma=False,
    )
```

profile of v0, /device:TPU:0, one launch (start us, length us, event | category | flops | bytes accessed | tf_op | source)
XLA Modules:
  0.0 756.5 jit_solution(4402624837217750955)
XLA Ops:
  6.5 3.2 fusion.7
  10.0 3.1 fusion.8
  15.8 4.1 fusion.16
  21.8 280.9 %all-gather.2.cloned.1.call-done = bf16[16,4,128,1024]{3,2,1,0:T(8,128)(2,1)} async-done(((bf16[16,1,128,1024]{3,2,1,0:T(8,128)(2,1)}), bf16[16,4,128,1024]{3,2,1,0:T(8,128)(2,1)}) %all-gather.2.cloned.1.call-update) | async-done | bytes 16777232 | tf_op jit(solution)/shard_map/all_gather | solution.py:92
  302.8 275.2 %while.14 = (s32[]{:T(128)}, f32[4,196608]{1,0:T(4,128)S(1)}, f32[40,4]{0,1:T(4,128)S(1)}, s32[40]{0:T(128)S(1)}, bf16[64,128,1024]{2,1,0:T(8,128)(2,1)}, /*inde...) while((s32[]{:T(128)}, f32[4,196608]{1,0:T(4,128)S(1)}, ...), condition=%wide.region_2.4_spmd.clone, body=%wide.region_1.3_spmd.clone.sunk | while | flops 2243430400 | bytes 125838472 | solution.py:123
  302.8 7.8 %gather_fusion.1 = bf16[8,128,1024]{2,1,0:T(8,128)(2,1)} fusion(bf16[64,128,1024]{2,1,0:T(8,128)(2,1)} %get-tuple-element.276, s32[1024]{0:T(1024)S(1)} %pad_clamp_fusion.5), kind=kCustom, calls=%fused_computation.clone.clone.1 | custom fusion | bytes 4194336 | tf_op jit(solution)/shard_map/while/body/eval_jaxpr/jit(_take)/gather | solution.py:110
  310.6 3.9 select_convert_fusion.5
  314.5 7.8 %gather_fusion = bf16[8,128,1024]{2,1,0:T(8,128)(2,1)} fusion(bf16[64,128,1024]{2,1,0:T(8,128)(2,1)} %get-tuple-element.276, s32[1024]{0:T(1024)S(1)} %pad_clamp_fusion.4), kind=kCustom, calls=%fused_computation.1.clone.clone.1 | custom fusion | bytes 4194336 | tf_op jit(solution)/shard_map/while/body/eval_jaxpr/jit(_take)/gather | solution.py:111
  322.3 2.1 select_convert_fusion.4
  326.7 2.3 fusion.108
  330.9 7.5 copy.11
  338.4 10.7 %reshape.136 = f32[8,196608]{1,0:T(8,128)} reshape(f32[1024,3,512]{2,1,0:T(4,128)} %copy.11) | data formatting | bytes 12582912 | tf_op jit(solution)/shard_map/while/body/eval_jaxpr/reshape | solution.py:116
  349.2 8.5 %convolution_add_fusion.2 = f32[4,196608]{1,0:T(4,128)S(1)} fusion(f32[8,196608]{1,0:T(8,128)} %reshape.136, f32[4,196608]{1,0:T(4,128)S(1)} %get-tuple-element.262, pred[]{:T(512)S(6)} %compare.9, f32[40,4]{0,1:T(4,128)S(1)} %get-tuple-element.274, s32[]{:T(128)S(6)} %select_n.99), kind=kOutput, calls=%fused_computation.2.clone.1 | convolution fusion | flops 77070336 | bytes 12583557 | tf_op jit(solution)/shard_map/while/body/eval_jaxpr/dot_general | solution.py:120
  357.8 7.8 %gather_fusion.1 = bf16[8,128,1024]{2,1,0:T(8,128)(2,1)} fusion(bf16[64,128,1024]{2,1,0:T(8,128)(2,1)} %get-tuple-element.276, s32[1024]{0:T(1024)S(1)} %pad_clamp_fusion.5), kind=kCustom, calls=%fused_computation.clone.clone.1 | custom fusion | bytes 4194336 | tf_op jit(solution)/shard_map/while/body/eval_jaxpr/jit(_take)/gather | solution.py:110
  365.6 3.9 select_convert_fusion.5
  369.5 7.8 %gather_fusion = bf16[8,128,1024]{2,1,0:T(8,128)(2,1)} fusion(bf16[64,128,1024]{2,1,0:T(8,128)(2,1)} %get-tuple-element.276, s32[1024]{0:T(1024)S(1)} %pad_clamp_fusion.4), kind=kCustom, calls=%fused_computation.1.clone.clone.1 | custom fusion | bytes 4194336 | tf_op jit(solution)/shard_map/while/body/eval_jaxpr/jit(_take)/gather | solution.py:111
  377.3 2.1 select_convert_fusion.4
  381.7 2.3 fusion.108
  385.9 7.5 copy.11
  393.4 10.7 %reshape.136 = f32[8,196608]{1,0:T(8,128)} reshape(f32[1024,3,512]{2,1,0:T(4,128)} %copy.11) | data formatting | bytes 12582912 | tf_op jit(solution)/shard_map/while/body/eval_jaxpr/reshape | solution.py:116
  404.2 8.5 %convolution_add_fusion.2 = f32[4,196608]{1,0:T(4,128)S(1)} fusion(f32[8,196608]{1,0:T(8,128)} %reshape.136, f32[4,196608]{1,0:T(4,128)S(1)} %get-tuple-element.262, pred[]{:T(512)S(6)} %compare.9, f32[40,4]{0,1:T(4,128)S(1)} %get-tuple-element.274, s32[]{:T(128)S(6)} %select_n.99), kind=kOutput, calls=%fused_computation.2.clone.1 | convolution fusion | flops 77070336 | bytes 12583557 | tf_op jit(solution)/shard_map/while/body/eval_jaxpr/dot_general | solution.py:120
  412.8 7.8 %gather_fusion.1 = bf16[8,128,1024]{2,1,0:T(8,128)(2,1)} fusion(bf16[64,128,1024]{2,1,0:T(8,128)(2,1)} %get-tuple-element.276, s32[1024]{0:T(1024)S(1)} %pad_clamp_fusion.5), kind=kCustom, calls=%fused_computation.clone.clone.1 | custom fusion | bytes 4194336 | tf_op jit(solution)/shard_map/while/body/eval_jaxpr/jit(_take)/gather | solution.py:110
  420.6 3.9 select_convert_fusion.5
  424.5 7.8 %gather_fusion = bf16[8,128,1024]{2,1,0:T(8,128)(2,1)} fusion(bf16[64,128,1024]{2,1,0:T(8,128)(2,1)} %get-tuple-element.276, s32[1024]{0:T(1024)S(1)} %pad_clamp_fusion.4), kind=kCustom, calls=%fused_computation.1.clone.clone.1 | custom fusion | bytes 4194336 | tf_op jit(solution)/shard_map/while/body/eval_jaxpr/jit(_take)/gather | solution.py:111
  432.3 2.1 select_convert_fusion.4
  436.7 2.3 fusion.108
  440.9 7.5 copy.11
  448.4 10.7 %reshape.136 = f32[8,196608]{1,0:T(8,128)} reshape(f32[1024,3,512]{2,1,0:T(4,128)} %copy.11) | data formatting | bytes 12582912 | tf_op jit(solution)/shard_map/while/body/eval_jaxpr/reshape | solution.py:116
  459.2 8.5 %convolution_add_fusion.2 = f32[4,196608]{1,0:T(4,128)S(1)} fusion(f32[8,196608]{1,0:T(8,128)} %reshape.136, f32[4,196608]{1,0:T(4,128)S(1)} %get-tuple-element.262, pred[]{:T(512)S(6)} %compare.9, f32[40,4]{0,1:T(4,128)S(1)} %get-tuple-element.274, s32[]{:T(128)S(6)} %select_n.99), kind=kOutput, calls=%fused_computation.2.clone.1 | convolution fusion | flops 77070336 | bytes 12583557 | tf_op jit(solution)/shard_map/while/body/eval_jaxpr/dot_general | solution.py:120
  467.8 7.8 %gather_fusion.1 = bf16[8,128,1024]{2,1,0:T(8,128)(2,1)} fusion(bf16[64,128,1024]{2,1,0:T(8,128)(2,1)} %get-tuple-element.276, s32[1024]{0:T(1024)S(1)} %pad_clamp_fusion.5), kind=kCustom, calls=%fused_computation.clone.clone.1 | custom fusion | bytes 4194336 | tf_op jit(solution)/shard_map/while/body/eval_jaxpr/jit(_take)/gather | solution.py:110
  475.6 3.9 select_convert_fusion.5
  479.5 7.8 %gather_fusion = bf16[8,128,1024]{2,1,0:T(8,128)(2,1)} fusion(bf16[64,128,1024]{2,1,0:T(8,128)(2,1)} %get-tuple-element.276, s32[1024]{0:T(1024)S(1)} %pad_clamp_fusion.4), kind=kCustom, calls=%fused_computation.1.clone.clone.1 | custom fusion | bytes 4194336 | tf_op jit(solution)/shard_map/while/body/eval_jaxpr/jit(_take)/gather | solution.py:111
  491.7 2.3 fusion.108
  495.9 7.5 copy.11
  503.4 10.7 %reshape.136 = f32[8,196608]{1,0:T(8,128)} reshape(f32[1024,3,512]{2,1,0:T(4,128)} %copy.11) | data formatting | bytes 12582912 | tf_op jit(solution)/shard_map/while/body/eval_jaxpr/reshape | solution.py:116
  514.2 8.5 %convolution_add_fusion.2 = f32[4,196608]{1,0:T(4,128)S(1)} fusion(f32[8,196608]{1,0:T(8,128)} %reshape.136, f32[4,196608]{1,0:T(4,128)S(1)} %get-tuple-element.262, pred[]{:T(512)S(6)} %compare.9, f32[40,4]{0,1:T(4,128)S(1)} %get-tuple-element.274, s32[]{:T(128)S(6)} %select_n.99), kind=kOutput, calls=%fused_computation.2.clone.1 | convolution fusion | flops 77070336 | bytes 12583557 | tf_op jit(solution)/shard_map/while/body/eval_jaxpr/dot_general | solution.py:120
  522.8 7.8 %gather_fusion.1 = bf16[8,128,1024]{2,1,0:T(8,128)(2,1)} fusion(bf16[64,128,1024]{2,1,0:T(8,128)(2,1)} %get-tuple-element.276, s32[1024]{0:T(1024)S(1)} %pad_clamp_fusion.5), kind=kCustom, calls=%fused_computation.clone.clone.1 | custom fusion | bytes 4194336 | tf_op jit(solution)/shard_map/while/body/eval_jaxpr/jit(_take)/gather | solution.py:110
  530.6 3.9 select_convert_fusion.5
  534.5 7.8 %gather_fusion = bf16[8,128,1024]{2,1,0:T(8,128)(2,1)} fusion(bf16[64,128,1024]{2,1,0:T(8,128)(2,1)} %get-tuple-element.276, s32[1024]{0:T(1024)S(1)} %pad_clamp_fusion.4), kind=kCustom, calls=%fused_computation.1.clone.clone.1 | custom fusion | bytes 4194336 | tf_op jit(solution)/shard_map/while/body/eval_jaxpr/jit(_take)/gather | solution.py:111
  546.7 2.3 fusion.108
  550.9 7.5 copy.11
  558.4 10.7 %reshape.136 = f32[8,196608]{1,0:T(8,128)} reshape(f32[1024,3,512]{2,1,0:T(4,128)} %copy.11) | data formatting | bytes 12582912 | tf_op jit(solution)/shard_map/while/body/eval_jaxpr/reshape | solution.py:116
  569.2 8.5 %convolution_add_fusion.2 = f32[4,196608]{1,0:T(4,128)S(1)} fusion(f32[8,196608]{1,0:T(8,128)} %reshape.136, f32[4,196608]{1,0:T(4,128)S(1)} %get-tuple-element.262, pred[]{:T(512)S(6)} %compare.9, f32[40,4]{0,1:T(4,128)S(1)} %get-tuple-element.274, s32[]{:T(128)S(6)} %select_n.99), kind=kOutput, calls=%fused_computation.2.clone.1 | convolution fusion | flops 77070336 | bytes 12583557 | tf_op jit(solution)/shard_map/while/body/eval_jaxpr/dot_general | solution.py:120
  577.9 4.8 reshape.103
  583.6 152.5 %all-reduce.2.cloned.1.call-done = f32[4,128,3,512]{3,2,1,0:T(4,128)} async-done(((f32[4,128,3,512]{3,2,1,0:T(4,128)}), f32[4,128,3,512]{3,2,1,0:T(4,128)}) %all-reduce.2.cloned.1.call-update) | async-done | bytes 3145744 | tf_op jit(solution)/shard_map/psum | solution.py:125
  736.1 3.3 constant_dynamic-slice_fusion
  742.8 2.1 collective-permute-done.1
  744.9 4.8 multiply_multiply_fusion
  (86 shorter events, 34.3 us)
Async XLA Ops:
  6.5 9.3 %copy-start = (s32[4,40,2]{1,2,0:T(2,128)S(1)}, s32[4,40,2]{1,2,0:T(2,128)}, u32[]{:S(2)}) copy-start(s32[4,40,2]{1,2,0:T(2,128)} %param.9) | copy-start | bytes 3844
  6.5 296.2 %all-gather.2.cloned.1.call-start = ((), (), s32[]{:S(2)}) async-start(), calls=%async_computation | async-start | bytes 20971520 | tf_op jit(solution)/shard_map/all_gather | solution.py:92
  6.5 3.5 copy-start.3
  13.1 0.7 copy-start.6
  13.1 723.0 %all-reduce.2.cloned.1.call-start = ((), (), s32[]{:S(2)}) async-start(), calls=%async_computation.1 | async-start | bytes 8388608 | tf_op jit(solution)/shard_map/psum | solution.py:125
  322.3 2.8 copy-start.2
  325.1 1.6 copy-start.4
  377.3 2.8 copy-start.2
  380.1 1.6 copy-start.4
  432.3 2.8 copy-start.2
  435.1 1.6 copy-start.4
  487.3 2.8 copy-start.2
  490.1 1.6 copy-start.4
  542.3 2.8 copy-start.2
  545.1 1.6 copy-start.4
  582.8 0.7 copy-start.7
  582.8 0.7 copy-start.5
  582.8 166.8 %copy-start.1 = (s32[4,40,2]{1,2,0:T(2,128)S(1)}, s32[4,40,2]{1,2,0:T(2,128)}, u32[]{:S(2)}) copy-start(s32[4,40,2]{1,2,0:T(2,128)} %param.9) | copy-start | bytes 3844
  739.7 3.1 collective-permute-start
  741.4 3.4 collective-permute-start.1
Sparse Core Ops, SparseCore 0:
  13.2 289.4 all-gather.1
  582.9 153.1 all-reduce.1
where the time goes:
time: 762 us; the launch traced here: 756 us
  waiting for transfers between devices  436 us (57%)
  local copies, waits for them, and re-layouts  182 us (24%)
  other arithmetic  67 us (9%)
  matrix products  54.3 us (7%)
  between operations  13.5 us (2%)
    all_gather x1, waiting for transfers between devices, shards(): gathered = lax.all_gather(whitened, 'pair', axis=1, tiled=True)  281 us
    psum x1, waiting for transfers between devices, shards(): totals = lax.psum(group_sums, 'pair')  152 us
    reshape x5, local copies, waits for them, and re-layouts, add_slots(): phase_terms(correlation, half_lags)  53.7 us
    dot_general x5, matrix products, add_slots(): jnp.dot(slot_weights.T, phase_rows, precision=lax.Precision.HIGHEST)  42.7 us
    gather x5, local copies, waits for them, and re-layouts, add_slots(): first_spec = jnp.take(spectra_rows, first_ids, axis=0)  39 us
    gather x5, local copies, waits for them, and re-layouts, add_slots(): second_spec = jnp.take(spectra_rows, second_ids, axis=0)  38.9 us
    another operation x5, local copies, waits for them, and re-layouts, phase_terms(): return jnp.stack([direct, direct / divisor, quadrature / divisor], axis=1)  37.7 us
    convert_element_type x5, other arithmetic, cross_spectra(): first_spec = first_spec.astype(jnp.float32)  19.4 us
  transfers between devices with their start and end apart: 4, of which 3 were waited for; matrix products, arithmetic and copies ran while one was open for 1% of the time, Pallas kernels for 0%

commit v1 on v0

v1 whole, which is shorter than its diff:
```python
import functools
import math

import jax
import jax.numpy as jnp
from jax import lax
from jax.experimental import pallas as pl
from jax.experimental.pallas import tpu as pltpu
from jax.sharding import PartitionSpec as P

NGRP = 4
HW = 15

AMP_FLOOR = 0.5
EPSILON = 1e-06
TILE_ROWS = 256
UNIT_ROWS = 16
LAG_TILE = 256
CHUNKS = 4


def lag_table(lag_count, num_bins):
    lag_ids = jnp.arange(lag_count, dtype=jnp.int32)
    bin_index = jnp.arange(num_bins, dtype=jnp.int32)[:, None]
    phase_turns = bin_index * (lag_ids[None, :] + num_bins) % (2 * num_bins)
    angles = phase_turns.astype(jnp.float32) * (math.pi / num_bins)
    cosine = jnp.cos(angles)
    sine_part = jnp.sin(angles)
    amp_scale = math.sqrt(2.0 / num_bins)
    upper_rows = jnp.concatenate([cosine, sine_part], axis=1)
    lower_rows = jnp.concatenate([-sine_part, cosine], axis=1)
    return (jnp.concatenate([upper_rows, lower_rows], axis=0) * amp_scale).astype(jnp.bfloat16)


def window_sum(values):
    rows, lags = values.shape
    edge = jnp.zeros((rows, 128), jnp.float32)
    one = jnp.concatenate([edge, values, edge], axis=1)
    width = one.shape[1]
    two = one + pltpu.roll(one, 1, 1)
    four = two + pltpu.roll(two, 2, 1)
    eight = four + pltpu.roll(four, 4, 1)
    back = eight + pltpu.roll(eight, 8, 1)
    ahead = eight + pltpu.roll(four, 8, 1) + pltpu.roll(two, 12, 1) + pltpu.roll(one, 14, 1)
    return (back + pltpu.roll(ahead, width - HW, 1))[:, 128 : 128 + lags]


def stack_kernel(num_parts, cell, tiles_ref, groups_ref, norm_ref, *refs):
    part_refs = refs[:num_parts]
    first_ref, second_ref, table_ref, out_ref, white_ref, sums_ref = refs[num_parts:]
    part_rows, width = part_refs[0].shape
    num_bins = width // 2
    lag_count = table_ref.shape[1] // 2
    units = TILE_ROWS // UNIT_ROWS

    for part, ref in enumerate(part_refs):
        values = ref[...].astype(jnp.float32)
        power = jnp.sum(values * values, axis=1, keepdims=True) * (2.0 / width)
        white = values * lax.rsqrt(power + EPSILON)
        white_ref[part * part_rows : (part + 1) * part_rows, :] = white.astype(jnp.bfloat16)
    sums_ref[...] = jnp.zeros_like(sums_ref)

    def tile_step(tile, carry):
        rows = pl.ds(pl.multiple_of(tile * TILE_ROWS, TILE_ROWS), TILE_ROWS)
        white = white_ref[...]
        first = jnp.dot(first_ref[rows, :], white, preferred_element_type=jnp.float32)
        second = jnp.dot(second_ref[rows, :], white, preferred_element_type=jnp.float32)
        real_a, imag_a = first[:, :num_bins], first[:, num_bins:]
        real_b, imag_b = second[:, :num_bins], second[:, num_bins:]
        real_part = (real_a * real_b + imag_a * imag_b).astype(jnp.bfloat16)
        imag_part = (imag_a * real_b - real_a * imag_b).astype(jnp.bfloat16)
        cross = jnp.concatenate([real_part, imag_part], axis=1)
        for lag in range(0, lag_count, LAG_TILE):
            lags = slice(lag, lag + LAG_TILE)
            quad_lags = slice(lag_count + lag, lag_count + lag + LAG_TILE)
            direct = jnp.dot(cross, table_ref[:, lags], preferred_element_type=jnp.float32)
            quad = jnp.dot(cross, table_ref[:, quad_lags], preferred_element_type=jnp.float32)
            inverse = jnp.minimum(lax.rsqrt(direct * direct + quad * quad), 1.0 / AMP_FLOOR)
            phase_c = direct * inverse
            phase_s = quad * inverse
            for unit in range(units):
                group = groups_ref[tile * units + unit]
                own = slice(unit * UNIT_ROWS, (unit + 1) * UNIT_ROWS)
                sums_ref[0, group, :, lags] += direct[own]
                sums_ref[1, group, :, lags] += phase_c[own]
                sums_ref[2, group, :, lags] += phase_s[own]
        return carry

    lax.fori_loop(0, tiles_ref[0], tile_step, 0)

    linear, coherence = [], []
    for group in range(NGRP):
        folded = []
        for kind in range(3):
            whole = sums_ref[kind, group]
            total = whole[:cell]
            for start in range(cell, UNIT_ROWS, cell):
                total = total + whole[start : start + cell]
            folded.append(total)
        scale = norm_ref[group]
        linear.append(folded[0] * scale)
        coherence.append(jnp.sqrt(folded[1] * folded[1] + folded[2] * folded[2]) * scale)
    coherence = jnp.concatenate(coherence, axis=0)
    smoothed = window_sum(coherence) * (1.0 / (2 * HW + 1))
    for group in range(NGRP):
        own = smoothed[group * cell : (group + 1) * cell]
        out_ref[group] = linear[group] * own * own


def pair_order(pair_blocks, live_pairs, stack_group, parts, part_blocks, cell):
    owners, slots, _ = pair_blocks.shape
    total = owners * slots
    unit_pairs = UNIT_ROWS // cell
    tile_pairs = TILE_ROWS // cell
    places = -(-(total + NGRP * (unit_pairs - 1)) // tile_pairs) * tile_pairs
    group_index = jnp.arange(NGRP, dtype=jnp.int32)
    live = jnp.arange(slots, dtype=jnp.int32)[None, :] < live_pairs[:, None]
    member = (stack_group[:, :, None] == group_index) & live[:, :, None]
    member = member.reshape(total, NGRP).astype(jnp.int32)
    members = jnp.sum(member, axis=0)
    filled = (members + unit_pairs - 1) // unit_pairs * unit_pairs
    ends = jnp.cumsum(filled)
    rank = jnp.cumsum(member, axis=0) - 1
    place = jnp.sum(member * (rank + (ends - filled)[None, :] + 1), axis=1) - 1
    here = jnp.arange(places, dtype=jnp.int32)
    match = here[:, None] == place[None, :]
    me = lax.axis_index("pair")
    blocks = pair_blocks.reshape(total, 2)
    held = lax.rem(me - lax.rem(blocks, parts) + parts, parts) * part_blocks + blocks // parts
    taken = jnp.sum(jnp.where(match[:, :, None], held[None] + 1, 0), axis=1) - 1
    row = jnp.where(taken[:, None, :] < 0, -1, taken[:, None, :] * cell + jnp.arange(cell, dtype=jnp.int32)[None, :, None])
    row = row.reshape(places * cell, 2)
    column = jnp.arange(parts * part_blocks * cell, dtype=jnp.int32)[None, :]
    first = (row[:, :1] == column).astype(jnp.bfloat16)
    second = (row[:, 1:] == column).astype(jnp.bfloat16)
    unit_start = jnp.arange(places // unit_pairs, dtype=jnp.int32) * unit_pairs
    unit_group = jnp.minimum(jnp.sum((unit_start[:, None] >= ends[None, :]).astype(jnp.int32), axis=1), NGRP - 1)
    tiles = ((ends[-1] + tile_pairs - 1) // tile_pairs).reshape(1)
    norm = 1.0 / jnp.sqrt(members.astype(jnp.float32))
    return tiles, unit_group, norm, first, second


def shards(spectra, pair_blocks, live_pairs, stack_group):
    parts = lax.axis_size("pair")
    me = lax.axis_index("pair")
    cores = lax.axis_size("lag")
    core = lax.axis_index("lag")
    part_blocks, _, channels, width = spectra.shape
    num_bins = width // 2
    lag_count = 2 * num_bins
    own_channels = channels // (parts * cores)
    chunks = CHUNKS if own_channels % CHUNKS == 0 else 1
    cell = own_channels // chunks

    tiles, unit_group, norm, first, second = pair_order(
        pair_blocks, live_pairs, stack_group, parts, part_blocks, cell
    )
    table = lag_table(lag_count, num_bins)

    rows = part_blocks * cell
    inputs = 1 if rows % UNIT_ROWS else parts
    call = pl.pallas_call(
        functools.partial(stack_kernel, inputs, cell),
        out_shape=jax.ShapeDtypeStruct((NGRP, cell, lag_count), jnp.float32),
        in_specs=[pl.BlockSpec(memory_space=pltpu.SMEM)] * 3
        + [pl.BlockSpec(memory_space=pltpu.VMEM)] * (inputs + 3),
        out_specs=pl.BlockSpec(memory_space=pltpu.VMEM),
        scratch_shapes=[
            pltpu.VMEM((parts * rows, width), jnp.bfloat16),
            pltpu.VMEM((3, NGRP, UNIT_ROWS, lag_count), jnp.float32),
        ],
        compiler_params=pltpu.CompilerParams(vmem_limit_bytes=40 * 1024 * 1024),
        name="stack",
    )

    stacks = []
    for chunk in range(chunks):
        received = []
        for shift in range(parts):
            target = lax.rem(me + shift, parts)
            start = (target * cores + core) * own_channels + chunk * cell
            piece = lax.dynamic_slice_in_dim(spectra, start, cell, 2).reshape(rows, width)
            if shift:
                piece = lax.ppermute(piece, "pair", [(i, (i + shift) % parts) for i in range(parts)])
            received.append(piece)
        if rows % UNIT_ROWS:
            received = [jnp.concatenate(received, axis=0)]
        stacks.append(call(tiles, unit_group, norm, *received, first, second, table))
    stacks = jnp.concatenate(stacks, axis=1)
    return lax.all_to_all(stacks, ("pair", "lag"), 2, 1, tiled=True)


def solution(mesh):
    return jax.shard_map(
        shards,
        mesh=mesh,
        in_specs=(P("win", "pair", "stk", None), P("win", None, None), P("win"), P("win", None)),
        out_specs=P("win", "stk", ("pair", "lag")),
        check_vma=False,
    )
```

time: 762 us -> 102 us (0.13)
  waiting for transfers between devices: 436 us -> 0.03 us
  local copies, waits for them, and re-layouts: 182 us -> 26.7 us
  matrix products: 54.3 us -> 0 us
  other arithmetic: 67 us -> 20.8 us
  Pallas kernels: 0 us -> 20.9 us
  starting transfers between devices: 3.09 us -> 18.8 us
  blocking collectives: 0 us -> 13.6 us
  between operations: 13.5 us -> 0.97 us
    all_gather x1 -> x0, waiting for transfers between devices: 281 us -> none  [shards(): gathered = lax.all_gather(whitened, 'pair', axis=1, tiled=True)]
    psum x1 -> x0, waiting for transfers between devices: 152 us -> none  [shards(): totals = lax.psum(group_sums, 'pair')]
    gather x10 -> x0, local copies, waits for them, and re-layouts: 77.9 us -> none  [the longest x5 39 us: add_slots(): first_spec = jnp.take(spectra_rows, first_ids, axis=0)]
    dot_general x10 -> x0, matrix products: 54.3 us -> none  [the longest x5 42.7 us: add_slots(): jnp.dot(slot_weights.T, phase_rows, precision=lax.Precision.HIGHEST)]
    reshape x6 -> x17, local copies, waits for them, and re-layouts: 58.6 us -> 12.4 us  [the longest x16 12.3 us: shards(): lax.dynamic_slice_in_dim(spectra, start, cell, 2).reshape(rows, width)]
    another operation x5 -> x3, local copies, waits for them, and re-layouts: 37.7 us -> 0.12 us  [phase_terms(): return jnp.stack([direct, direct / divisor, quadrature / divisor], axis=1)]
    convert_element_type x12 -> x1, other arithmetic: 32.9 us -> 0.27 us  [pair_order(): first = (row[:, :1] == column).astype(jnp.bfloat16)]
    pallas_call x0 -> x4, Pallas kernels: none -> 20.9 us  [shards(): call(tiles, unit_group, norm, *received, first, second, table)]
  transfers between devices with their start and end apart: 4 -> 12, of which waited for: 3 -> 0; matrix products, arithmetic and copies ran while one was open for 1% -> 32% of each run, Pallas kernels for 0% -> 15%
where the time goes in v1:
time: 102 us
  local copies, waits for them, and re-layouts  26.7 us (26%)
  Pallas kernels  20.9 us (20%)
  other arithmetic  20.8 us (20%)
  starting transfers between devices  18.8 us (18%)
  blocking collectives  13.6 us (13%)
    pallas_call x4, Pallas kernels, shards(): call(tiles, unit_group, norm, *received, first, second, table)  20.9 us
    ppermute x12, starting transfers between devices, shards(): lax.ppermute(piece, 'pair', [(i, (i + shift) % parts) for i in range(part...  18.8 us
    all_to_all x1, blocking collectives, shards(): return lax.all_to_all(stacks, ('pair', 'lag'), 2, 1, tiled=True)  13.6 us
    reshape x16, local copies, waits for them, and re-layouts, shards(): lax.dynamic_slice_in_dim(spectra, start, cell, 2).reshape(rows, width)  12.3 us
    sin x1, other arithmetic, lag_table(): sine_part = jnp.sin(angles)  9.35 us
    convert_element_type x1, other arithmetic, lag_table(): (jnp.concatenate([upper_rows, lower_rows], axis=0) * amp_scale).astype(jn...  7.67 us
    unnamed x16, local copies, waits for them, and re-layouts  5.28 us
    dynamic_slice x1, local copies, waits for them, and re-layouts, shards(): lax.dynamic_slice_in_dim(spectra, start, cell, 2).reshape(rows, width)  4.45 us
  transfers between devices with their start and end apart: 12, of which 0 were waited for; matrix products, arithmetic and copies ran while one was open for 32% of the time, Pallas kernels for 15%

profile of v1, /device:TPU:0, one launch (start us, length us, event | category | flops | bytes accessed | tf_op | source)
XLA Modules:
  0.0 101.8 jit_solution(17614155727725359230)
XLA Ops:
  0.0 4.4 %constant_dynamic-slice_fusion.12 = (bf16[16,1,4,1024]{3,2,1,0:T(4,128)(2,1)S(1)}, bf16[16,1,4,1024]{3,2,1,0:T(4,128)(2,1)}, bf16[16,1,4,1024]{3,2,1,0:T(4,128)(...) fusion(bf16[16,1,128,1024]{3,2,1,0:T(8,128)(2,1)} %param.4, ...), kind=kLoop, calls=%fused_computation.45 | loop fusion | bytes 4194368 | tf_op jit(solution)/shard_map/dynamic_slice | solution.py:182
  4.5 0.7 reshape.265
  5.1 3.1 %collective-permute-start = (bf16[64,1024]{1,0:T(8,128)(2,1)}, bf16[64,1024]{1,0:T(8,128)(2,1)S(1)}, u32[]{:S(2)}, u32[]{:S(2)}) collective-permute-start(bf16[64,1024]{1,0:T(8,128)(2,1)} %reshape.265), channel_id=1, source_target_pairs={{0,4},{4,8},{8,12},{12,0},{1,5},{5,9},{9,13},{13,1},{2,6},{6,10},{... | collective-permute-start | bytes 393224 | tf_op jit(solution)/shard_map/ppermute | solution.py:184
  8.3 0.7 reshape.266
  9.0 2.6 %collective-permute-start.1 = (bf16[64,1024]{1,0:T(8,128)(2,1)}, bf16[64,1024]{1,0:T(8,128)(2,1)S(1)}, u32[]{:S(2)}, u32[]{:S(2)}) collective-permute-start(bf16[64,1024]{1,0:T(8,128)(2,1)} %reshape.266), channel_id=1, source_target_pairs={{0,8},{4,12},{8,0},{12,4},{1,9},{5,13},{9,1},{13,5},{2,10},{6,14},... | collective-permute-start | bytes 393224 | tf_op jit(solution)/shard_map/ppermute | solution.py:184
  11.5 0.7 reshape.267
  12.2 1.3 %collective-permute-start.2 = (bf16[64,1024]{1,0:T(8,128)(2,1)}, bf16[64,1024]{1,0:T(8,128)(2,1)S(1)}, u32[]{:S(2)}, u32[]{:S(2)}) collective-permute-start(bf16[64,1024]{1,0:T(8,128)(2,1)} %reshape.267), channel_id=1, source_target_pairs={{0,12},{4,0},{8,4},{12,8},{1,13},{5,1},{9,5},{13,9},{2,14},{6,2},{... | collective-permute-start | bytes 393224 | tf_op jit(solution)/shard_map/ppermute | solution.py:184
  13.5 0.7 reshape.272
  14.2 0.7 collective-permute-start.3
  14.9 0.7 reshape.273
  15.6 0.4 collective-permute-start.4
  16.4 0.2 reduce-window.10
  16.6 1.2 %reduce-window.11 = s32[4,2,128]{2,1,0:T(2,128)S(1)} reduce-window(s32[4,2,128]{2,1,0:T(2,128)S(1)} %reshape.283, s32[]{:T(128)} %constant.113.clone.1), window={size=1x1x128 pad=0_0x0_0x127_0}, to_apply=%region_3.4 | reduce-window | flops 130048 | bytes 8196 | tf_op jit(solution)/shard_map/reduce-window.1
  18.8 0.2 add.308
  19.1 0.2 broadcast_in_dim.38
  19.4 9.4 %fusion.7 = (f32[512,1024]{1,0:T(8,128)S(1)}, f32[512,1024]{1,0:T(8,128)}, f32[512,1024]{1,0:T(8,128)}) fusion(s32[1024]{0:T(1024)S(1)} %iota_add_fusion), kind=kLoop, calls=%fused_computation.11 | loop fusion | flops 7864320 | bytes 6295552 | tf_op jit(solution)/shard_map/sin | solution.py:28
  28.8 0.7 reshape.274
  29.5 0.7 reshape.276
  30.1 0.3 fusion.10
  30.4 7.7 %fusion.refs_6_ = bf16[1024,2048]{1,0:T(8,128)(2,1)} fusion(f32[512,1024]{1,0:T(8,128)} %get-tuple-element.25, f32[512,1024]{1,0:T(8,128)} %get-tuple-element.24, f32[512,1024]{1,0:T(8,128)S(1)} %get-tuple-element.23), kind=kLoop, calls=%fused_computation.1 | loop fusion | flops 10485760 | bytes 10485760 | tf_op jit(solution)/shard_map/convert_element_type | solution.py:32
  38.1 2.8 %collective-permute-start.5 = (bf16[64,1024]{1,0:T(8,128)(2,1)}, bf16[64,1024]{1,0:T(8,128)(2,1)S(1)}, u32[]{:S(2)}, u32[]{:S(2)}) collective-permute-start(bf16[64,1024]{1,0:T(8,128)(2,1)} %reshape.274), channel_id=1, source_target_pairs={{0,12},{4,0},{8,4},{12,8},{1,13},{5,1},{9,5},{13,9},{2,14},{6,2},{... | collective-permute-start | bytes 393224 | tf_op jit(solution)/shard_map/ppermute | solution.py:184
  40.9 0.6 collective-permute-start.6
  41.6 0.6 slice.19
  42.8 0.9 reshape.264.refs_0_
  43.7 0.9 reshape.271.refs_0_
  44.7 0.9 reshape.277
  45.6 0.9 reshape.278
  46.6 0.9 reshape.275.refs_0_
  47.5 0.9 reshape.281
  48.5 0.9 reshape.282
  49.4 0.9 reshape.280
  50.5 1.5 %collective-permute-start.7 = (bf16[64,1024]{1,0:T(8,128)(2,1)S(1)}, bf16[64,1024]{1,0:T(8,128)(2,1)S(1)}, u32[]{:S(2)}, u32[]{:S(2)}) collective-permute-start(bf16[64,1024]{1,0:T(8,128)(2,1)S(1)} %reshape.277), channel_id=1, source_target_pairs={{0,8},{4,12},{8,0},{12,4},{1,9},{5,13},{9,1},{13,5},{2,10},{6,14},... | collective-permute-start | bytes 393224 | tf_op jit(solution)/shard_map/ppermute | solution.py:184
  51.9 2.9 %collective-permute-start.8 = (bf16[64,1024]{1,0:T(8,128)(2,1)S(1)}, bf16[64,1024]{1,0:T(8,128)(2,1)S(1)}, u32[]{:S(2)}, u32[]{:S(2)}) collective-permute-start(bf16[64,1024]{1,0:T(8,128)(2,1)S(1)} %reshape.278), channel_id=1, source_target_pairs={{0,12},{4,0},{8,4},{12,8},{1,13},{5,1},{9,5},{13,9},{2,14},{6,2},{... | collective-permute-start | bytes 393224 | tf_op jit(solution)/shard_map/ppermute | solution.py:184
  54.9 0.9 collective-permute-start.10
  55.8 1.0 collective-permute-start.11
  56.7 1.1 %collective-permute-start.9 = (bf16[64,1024]{1,0:T(8,128)(2,1)S(1)}, bf16[64,1024]{1,0:T(8,128)(2,1)S(1)}, u32[]{:S(2)}, u32[]{:S(2)}) collective-permute-start(bf16[64,1024]{1,0:T(8,128)(2,1)S(1)} %reshape.280), channel_id=1, source_target_pairs={{0,4},{4,8},{8,12},{12,0},{1,5},{5,9},{9,13},{13,1},{2,6},{6,10},{... | collective-permute-start | bytes 393224 | tf_op jit(solution)/shard_map/ppermute | solution.py:184
  57.8 2.2 %copy-done = bf16[1024,2048]{1,0:T(8,128)(2,1)S(1)} copy-done((bf16[1024,2048]{1,0:T(8,128)(2,1)S(1)}, bf16[1024,2048]{1,0:T(8,128)(2,1)}, u32[]{:S(2)}) %copy-start) | copy-done | bytes 4194328
  60.0 5.2 %stack.4 = f32[4,4,1024]{2,1,0:T(4,128)S(1)} custom-call(s32[1]{0:T(128)} %bitcast.2.tiles_ref, s32[48]{0:T(128)S(1)} %broadcast_minimum_fusion.groups_ref, f32[4]{0:T(128)S(1)} %convert_rsqrt_fusion.norm_ref, bf16[64,1024]{1,0:T(8,128)(2,1)S(1)} %reshape.264.refs_0_, bf16[64,1024]{1,0:T(8,128)(2,1)S(1)} %collective-permute-done.refs_1_, ...), custom_call_target="tpu_custom_call" | custom-call | tf_op jit(solution)/shard_map/stack/pallas_call | solution.py:188
  65.2 5.4 %stack.5 = f32[4,4,1024]{2,1,0:T(4,128)S(1)} custom-call(s32[1]{0:T(128)} %bitcast.2.tiles_ref, s32[48]{0:T(128)S(1)} %broadcast_minimum_fusion.groups_ref, f32[4]{0:T(128)S(1)} %convert_rsqrt_fusion.norm_ref, bf16[64,1024]{1,0:T(8,128)(2,1)S(1)} %reshape.271.refs_0_, bf16[64,1024]{1,0:T(8,128)(2,1)S(1)} %collective-permute-done.3.refs_1_, ...), custom_call_target="tpu_custom_call" | custom-call | tf_op jit(solution)/shard_map/stack/pallas_call | solution.py:188
  70.6 5.2 %stack.6 = f32[4,4,1024]{2,1,0:T(4,128)S(1)} custom-call(s32[1]{0:T(128)} %bitcast.2.tiles_ref, s32[48]{0:T(128)S(1)} %broadcast_minimum_fusion.groups_ref, f32[4]{0:T(128)S(1)} %convert_rsqrt_fusion.norm_ref, bf16[64,1024]{1,0:T(8,128)(2,1)S(1)} %reshape.275.refs_0_, bf16[64,1024]{1,0:T(8,128)(2,1)S(1)} %collective-permute-done.6.refs_1_, ...), custom_call_target="tpu_custom_call" | custom-call | tf_op jit(solution)/shard_map/stack/pallas_call | solution.py:188
  75.8 5.2 %stack.7 = f32[4,4,1024]{2,1,0:T(4,128)S(1)} custom-call(s32[1]{0:T(128)} %bitcast.2.tiles_ref, s32[48]{0:T(128)S(1)} %broadcast_minimum_fusion.groups_ref, f32[4]{0:T(128)S(1)} %convert_rsqrt_fusion.norm_ref, bf16[64,1024]{1,0:T(8,128)(2,1)S(1)} %reshape.279.refs_0_, bf16[64,1024]{1,0:T(8,128)(2,1)S(1)} %collective-permute-done.9.refs_1_, ...), custom_call_target="tpu_custom_call" | custom-call | tf_op jit(solution)/shard_map/stack/pallas_call | solution.py:188
  81.1 0.8 copy.27
  82.0 1.6 %reshape.286 = f32[8,1,8192]{2,1,0:T(1,128)S(1)} reshape(f32[1024,4,16]{2,1,0:T(4,128)S(1)} %bitcast.35) | data formatting | bytes 524288
  83.5 13.6 %all_to_all.18 = f32[8,1,8192]{2,1,0:T(1,128)S(1)} all-to-all(f32[8,1,8192]{2,1,0:T(1,128)S(1)} %reshape.286), channel_id=1, replica_groups=mesh['win'=2,'pair'=4,'stk'=2,'lag'=2] {'pair','lag'}, dimensions={0} | all-to-all | bytes 524288 | tf_op jit(solution)/shard_map/all_to_all | solution.py:190
  97.1 0.5 broadcast.322
  97.6 1.3 %reduce.4 = f32[8,8192]{1,0:T(8,128)S(1)} reduce(f32[8,1,8192]{2,1,0:T(1,128)S(1)} %all_to_all.18, f32[]{:T(128)} %broadcast.322), dimensions={1}, to_apply=%all_to_all.13.reduce_sub_computation | reduce | bytes 524292 | tf_op jit(solution)/shard_map/all_to_all | solution.py:190
  98.9 1.5 %reshape.287 = f32[1024,4,16]{2,1,0:T(4,128)S(1)} reshape(f32[8,8192]{1,0:T(8,128)S(1)} %reduce.4) | data formatting | bytes 524288
  100.4 1.4 %copy.28 = f32[4,8,16,128]{3,2,1,0:T(8,128)} copy(f32[4,8,16,128]{2,0,3,1:T(4,128)S(1)} %bitcast.36) | data formatting | bytes 524288 | tf_op jit(solution)/shard_map/all_to_all | solution.py:190
  (61 shorter events, 1.9 us)
Async XLA Ops:
  0.0 16.0 %copy-start.4 = (s32[4,40]{1,0:T(4,128)S(1)}, s32[4,40]{1,0:T(4,128)}, u32[]{:S(2)}) copy-start(s32[4,40]{1,0:T(4,128)} %param.7) | copy-start | bytes 1924
  0.0 16.0 %copy-start.5 = (s32[4]{0:T(128)S(1)}, s32[4]{0:T(128)}, u32[]{:S(2)}) copy-start(s32[4]{0:T(128)} %param.6) | copy-start | bytes 52
  0.0 18.4 %copy-start.3 = (s32[4,40,2]{1,2,0:T(2,128)S(1)}, s32[4,40,2]{1,2,0:T(2,128)}, u32[]{:S(2)}) copy-start(s32[4,40,2]{1,2,0:T(2,128)} %param.5) | copy-start | bytes 3844
  5.1 33.0 %collective-permute-start = (bf16[64,1024]{1,0:T(8,128)(2,1)}, bf16[64,1024]{1,0:T(8,128)(2,1)S(1)}, u32[]{:S(2)}, u32[]{:S(2)}) collective-permute-start(bf16[64,1024]{1,0:T(8,128)(2,1)} %reshape.265), channel_id=1, source_target_pairs={{0,4},{4,8},{8,12},{12,0},{1,5},{5,9},{9,13},{13,1},{2,6},{6,10},{... | collective-permute-start | bytes 393224 | tf_op jit(solution)/shard_map/ppermute | solution.py:184
  9.0 32.0 %collective-permute-start.1 = (bf16[64,1024]{1,0:T(8,128)(2,1)}, bf16[64,1024]{1,0:T(8,128)(2,1)S(1)}, u32[]{:S(2)}, u32[]{:S(2)}) collective-permute-start(bf16[64,1024]{1,0:T(8,128)(2,1)} %reshape.266), channel_id=1, source_target_pairs={{0,8},{4,12},{8,0},{12,4},{1,9},{5,13},{9,1},{13,5},{2,10},{6,14},... | collective-permute-start | bytes 393224 | tf_op jit(solution)/shard_map/ppermute | solution.py:184
  12.2 38.3 %collective-permute-start.2 = (bf16[64,1024]{1,0:T(8,128)(2,1)}, bf16[64,1024]{1,0:T(8,128)(2,1)S(1)}, u32[]{:S(2)}, u32[]{:S(2)}) collective-permute-start(bf16[64,1024]{1,0:T(8,128)(2,1)} %reshape.267), channel_id=1, source_target_pairs={{0,12},{4,0},{8,4},{12,8},{1,13},{5,1},{9,5},{13,9},{2,14},{6,2},{... | collective-permute-start | bytes 393224 | tf_op jit(solution)/shard_map/ppermute | solution.py:184
  14.2 37.7 %collective-permute-start.3 = (bf16[64,1024]{1,0:T(8,128)(2,1)}, bf16[64,1024]{1,0:T(8,128)(2,1)S(1)}, u32[]{:S(2)}, u32[]{:S(2)}) collective-permute-start(bf16[64,1024]{1,0:T(8,128)(2,1)} %reshape.272), channel_id=1, source_target_pairs={{0,4},{4,8},{8,12},{12,0},{1,5},{5,9},{9,13},{13,1},{2,6},{6,10},{... | collective-permute-start | bytes 393224 | tf_op jit(solution)/shard_map/ppermute | solution.py:184
  15.6 39.3 %collective-permute-start.4 = (bf16[64,1024]{1,0:T(8,128)(2,1)}, bf16[64,1024]{1,0:T(8,128)(2,1)S(1)}, u32[]{:S(2)}, u32[]{:S(2)}) collective-permute-start(bf16[64,1024]{1,0:T(8,128)(2,1)} %reshape.273), channel_id=1, source_target_pairs={{0,8},{4,12},{8,0},{12,4},{1,9},{5,13},{9,1},{13,5},{2,10},{6,14},... | collective-permute-start | bytes 393224 | tf_op jit(solution)/shard_map/ppermute | solution.py:184
  38.1 12.3 %copy-start.2 = (bf16[16,1,4,1024]{3,2,1,0:T(4,128)(2,1)S(1)}, bf16[16,1,4,1024]{3,2,1,0:T(4,128)(2,1)}, u32[]{:S(2)}) copy-start(bf16[16,1,4,1024]{3,2,1,0:T(4,128)(2,1)} %get-tuple-element.9) | copy-start | bytes 393220
  38.1 17.7 %collective-permute-start.5 = (bf16[64,1024]{1,0:T(8,128)(2,1)}, bf16[64,1024]{1,0:T(8,128)(2,1)S(1)}, u32[]{:S(2)}, u32[]{:S(2)}) collective-permute-start(bf16[64,1024]{1,0:T(8,128)(2,1)} %reshape.274), channel_id=1, source_target_pairs={{0,12},{4,0},{8,4},{12,8},{1,13},{5,1},{9,5},{13,9},{2,14},{6,2},{... | collective-permute-start | bytes 393224 | tf_op jit(solution)/shard_map/ppermute | solution.py:184
  40.9 15.8 %collective-permute-start.6 = (bf16[64,1024]{1,0:T(8,128)(2,1)}, bf16[64,1024]{1,0:T(8,128)(2,1)S(1)}, u32[]{:S(2)}, u32[]{:S(2)}) collective-permute-start(bf16[64,1024]{1,0:T(8,128)(2,1)} %reshape.276), channel_id=1, source_target_pairs={{0,4},{4,8},{8,12},{12,0},{1,5},{5,9},{9,13},{13,1},{2,6},{6,10},{... | collective-permute-start | bytes 393224 | tf_op jit(solution)/shard_map/ppermute | solution.py:184
  50.5 20.1 %collective-permute-start.7 = (bf16[64,1024]{1,0:T(8,128)(2,1)S(1)}, bf16[64,1024]{1,0:T(8,128)(2,1)S(1)}, u32[]{:S(2)}, u32[]{:S(2)}) collective-permute-start(bf16[64,1024]{1,0:T(8,128)(2,1)S(1)} %reshape.277), channel_id=1, source_target_pairs={{0,8},{4,12},{8,0},{12,4},{1,9},{5,13},{9,1},{13,5},{2,10},{6,14},... | collective-permute-start | bytes 393224 | tf_op jit(solution)/shard_map/ppermute | solution.py:184
  51.9 18.6 %collective-permute-start.8 = (bf16[64,1024]{1,0:T(8,128)(2,1)S(1)}, bf16[64,1024]{1,0:T(8,128)(2,1)S(1)}, u32[]{:S(2)}, u32[]{:S(2)}) collective-permute-start(bf16[64,1024]{1,0:T(8,128)(2,1)S(1)} %reshape.278), channel_id=1, source_target_pairs={{0,12},{4,0},{8,4},{12,8},{1,13},{5,1},{9,5},{13,9},{2,14},{6,2},{... | collective-permute-start | bytes 393224 | tf_op jit(solution)/shard_map/ppermute | solution.py:184
  54.9 20.9 %collective-permute-start.10 = (bf16[64,1024]{1,0:T(8,128)(2,1)S(1)}, bf16[64,1024]{1,0:T(8,128)(2,1)S(1)}, u32[]{:S(2)}, u32[]{:S(2)}) collective-permute-start(bf16[64,1024]{1,0:T(8,128)(2,1)S(1)} %reshape.281), channel_id=1, source_target_pairs={{0,8},{4,12},{8,0},{12,4},{1,9},{5,13},{9,1},{13,5},{2,10},{6,14},... | collective-permute-start | bytes 393224 | tf_op jit(solution)/shard_map/ppermute | solution.py:184
  55.8 20.0 %collective-permute-start.11 = (bf16[64,1024]{1,0:T(8,128)(2,1)S(1)}, bf16[64,1024]{1,0:T(8,128)(2,1)S(1)}, u32[]{:S(2)}, u32[]{:S(2)}) collective-permute-start(bf16[64,1024]{1,0:T(8,128)(2,1)S(1)} %reshape.282), channel_id=1, source_target_pairs={{0,12},{4,0},{8,4},{12,8},{1,13},{5,1},{9,5},{13,9},{2,14},{6,2},{... | collective-permute-start | bytes 393224 | tf_op jit(solution)/shard_map/ppermute | solution.py:184
  56.7 19.1 %collective-permute-start.9 = (bf16[64,1024]{1,0:T(8,128)(2,1)S(1)}, bf16[64,1024]{1,0:T(8,128)(2,1)S(1)}, u32[]{:S(2)}, u32[]{:S(2)}) collective-permute-start(bf16[64,1024]{1,0:T(8,128)(2,1)S(1)} %reshape.280), channel_id=1, source_target_pairs={{0,4},{4,8},{8,12},{12,0},{1,5},{5,9},{9,13},{13,1},{2,6},{6,10},{... | collective-permute-start | bytes 393224 | tf_op jit(solution)/shard_map/ppermute | solution.py:184
  57.8 2.2 %copy-start = (bf16[1024,2048]{1,0:T(8,128)(2,1)S(1)}, bf16[1024,2048]{1,0:T(8,128)(2,1)}, u32[]{:S(2)}) copy-start(bf16[1024,2048]{1,0:T(8,128)(2,1)} %fusion.refs_6_) | copy-start | bytes 12582916
  70.6 5.3 %copy-start.1 = (bf16[1024,2048]{1,0:T(8,128)(2,1)S(1)}, bf16[1024,2048]{1,0:T(8,128)(2,1)}, u32[]{:S(2)}) copy-start(bf16[1024,2048]{1,0:T(8,128)(2,1)} %fusion.refs_6_) | copy-start | bytes 12582916

commit v2 on v1

v2 whole, which is shorter than its diff:
```python
import functools
import math

import jax
import jax.numpy as jnp
from jax import lax
from jax.experimental import pallas as pl
from jax.experimental.pallas import tpu as pltpu
from jax.sharding import PartitionSpec as P

NGRP = 4
HW = 15

AMP_FLOOR = 0.5
EPSILON = 1e-06
TILE_ROWS = 256
PACK_ROWS = 16
SUB_ROWS = 8
LANES = 128
CLASSES = 4


def turn(steps, period):
    quarter = period // 4
    quadrant = (steps + quarter // 2) // quarter
    angle = (steps - quadrant * quarter).astype(jnp.float32) * (2.0 * math.pi / period)
    square = angle * angle
    cosine = 1.0 + square * (-1 / 2 + square * (1 / 24 + square * (-1 / 720 + square * (1 / 40320))))
    sine = angle * (1.0 + square * (-1 / 6 + square * (1 / 120 + square * (-1 / 5040 + square * (1 / 362880)))))
    odd = (quadrant & 1) == 1
    cosine, sine = jnp.where(odd, sine, cosine), jnp.where(odd, cosine, sine)
    cosine = jnp.where(((quadrant + 1) & 2) == 2, -cosine, cosine)
    sine = jnp.where((quadrant & 2) == 2, -sine, sine)
    return cosine, sine


def table_kernel(used_ref, out_ref):
    width, columns = out_ref.shape
    num_bins = width // 2
    period = 2 * num_bins
    scale = math.sqrt(2.0 / num_bins)
    class_bins = num_bins // CLASSES
    rows = lax.broadcasted_iota(jnp.int32, (class_bins, LANES), 0)
    lanes = lax.broadcasted_iota(jnp.int32, (class_bins, LANES), 1)
    for index in range(CLASSES):
        real_rows = slice(2 * index * class_bins, (2 * index + 1) * class_bins)
        imag_rows = slice((2 * index + 1) * class_bins, (2 * index + 2) * class_bins)
        for tile in range(columns // (2 * LANES)):
            lags = lanes + (tile * LANES + num_bins)
            cosine, sine = turn((rows * CLASSES + index) * lags & (period - 1), period)
            cosine, sine = cosine * scale, sine * scale
            direct = slice(2 * tile * LANES, (2 * tile + 1) * LANES)
            quad = slice((2 * tile + 1) * LANES, (2 * tile + 2) * LANES)
            out_ref[real_rows, direct] = cosine.astype(jnp.bfloat16)
            out_ref[imag_rows, direct] = (-sine).astype(jnp.bfloat16)
            out_ref[real_rows, quad] = sine.astype(jnp.bfloat16)
            out_ref[imag_rows, quad] = cosine.astype(jnp.bfloat16)


def lag_table(used, lag_count, num_bins):
    return pl.pallas_call(
        table_kernel,
        out_shape=jax.ShapeDtypeStruct((2 * num_bins, 2 * lag_count // CLASSES), jnp.bfloat16),
        in_specs=[pl.BlockSpec(memory_space=pltpu.SMEM)],
        out_specs=pl.BlockSpec(memory_space=pltpu.VMEM),
        compiler_params=pltpu.CompilerParams(vmem_limit_bytes=6 * 1024 * 1024),
        name="table",
    )(used)


def whiten(values):
    values = values.astype(jnp.float32)
    power = jnp.sum(values * values, axis=-1, keepdims=True) * (2.0 / values.shape[-1])
    return (values * lax.rsqrt(power + EPSILON)).astype(jnp.bfloat16)


def prepare_kernel(chunks, start_ref, spectra_ref, *refs):
    parts = start_ref.shape[0]
    out_refs = refs[: parts * len(chunks)]
    raw_ref, arrived = refs[parts * len(chunks) :]
    _, blocks, own_channels, width = raw_ref.shape
    num_bins = width // 2
    class_bins = num_bins // CLASSES
    order = (2, 3, 1, 0) if parts == 4 else tuple(range(parts))

    def fetch(step):
        start = pl.multiple_of(start_ref[step], 2 * SUB_ROWS)
        return pltpu.make_async_copy(
            spectra_ref.at[:, 0, pl.ds(start, own_channels), :], raw_ref.at[step], arrived.at[step]
        )

    for step in order:
        fetch(step).start()
    source = lax.broadcasted_iota(jnp.int32, (num_bins, num_bins), 0)
    target = lax.broadcasted_iota(jnp.int32, (num_bins, num_bins), 1)
    wanted = (target & (class_bins - 1)) * CLASSES + target // class_bins
    shuffle = jnp.where(source == wanted, 1.0, 0.0).astype(jnp.bfloat16)
    for step in order:
        fetch(step).wait()
        white = whiten(raw_ref[step].reshape(blocks * own_channels, width))
        halves = [
            jnp.dot(white[:, start : start + num_bins], shuffle, preferred_element_type=jnp.float32)
            for start in (0, num_bins)
        ]
        halves = [half.reshape(blocks, own_channels, num_bins) for half in halves]
        offset = 0
        for index, cells in enumerate(chunks):
            out_ref = out_refs[step * len(chunks) + index]
            row = 0
            for cell in cells:
                group = SUB_ROWS // cell
                for block in range(0, blocks, 2 * group):
                    for side, half in enumerate(halves):
                        rows = [half[block + k, offset : offset + cell] for k in range(2 * group)]
                        rows = jnp.concatenate(rows, axis=0).astype(jnp.bfloat16)
                        out_ref[row : row + PACK_ROWS, side * num_bins : (side + 1) * num_bins] = rows
                    row += PACK_ROWS
                offset += cell


def window_sum(values):
    rows, lags = values.shape
    edge = jnp.zeros((rows, 128), jnp.float32)
    one = jnp.concatenate([edge, values, edge], axis=1)
    width = one.shape[1]
    two = one + pltpu.roll(one, 1, 1)
    four = two + pltpu.roll(two, 2, 1)
    eight = four + pltpu.roll(four, 4, 1)
    back = eight + pltpu.roll(eight, 8, 1)
    ahead = eight + pltpu.roll(four, 8, 1) + pltpu.roll(two, 12, 1) + pltpu.roll(one, 14, 1)
    return (back + pltpu.roll(ahead, width - HW, 1))[:, 128 : 128 + lags]


def chunk_rows(cells, unit_pairs):
    return unit_pairs * sum(cells)


def quarter_turns(direct, quad):
    even_d, even_q = direct[0] + direct[2], quad[0] + quad[2]
    odd_d, odd_q = direct[1] + direct[3], quad[1] + quad[3]
    even_e, even_r = direct[0] - direct[2], quad[0] - quad[2]
    odd_e, odd_r = direct[1] - direct[3], quad[1] - quad[3]
    return (
        [even_d + odd_d, even_e - odd_r, even_d - odd_d, even_e + odd_r],
        [even_q + odd_q, even_r + odd_e, even_q - odd_q, even_r - odd_e],
    )


def phase_terms(direct, quad):
    inverse = jnp.minimum(lax.rsqrt(direct * direct + quad * quad), 1.0 / AMP_FLOOR)
    return [direct, direct * inverse, quad * inverse]


def stack_kernel(num_parts, cells, unit_pairs, tile_units, tiles_ref, place_ref, groups_ref, norm_ref, *refs):
    part_refs = refs[:num_parts]
    table_ref, out_ref = refs[num_parts : num_parts + 2]
    white_refs = refs[num_parts + 2 : num_parts + 2 + len(cells)]
    cross_ref, lag_ref, sums_ref = refs[num_parts + 2 + len(cells) :]
    part_rows, width = part_refs[0].shape
    num_bins = width // 2
    class_bins = num_bins // CLASSES
    quarter = width // CLASSES
    unit_rows = chunk_rows(cells, unit_pairs)
    part_blocks = part_rows // sum(cells)

    for part, ref in enumerate(part_refs):
        start = 0
        for cell, white_ref in zip(cells, white_refs):
            rows = part_blocks * cell
            copies = SUB_ROWS // cell
            white = ref[start : start + rows, :].astype(jnp.float32).reshape(rows // SUB_ROWS, SUB_ROWS, width)
            start += rows
            if copies == 1:
                white_ref[part * part_blocks : (part + 1) * part_blocks] = white
            else:
                for sub in range(rows // SUB_ROWS):
                    for copy in range(copies):
                        block = white[sub, copy * cell : (copy + 1) * cell]
                        white_ref[part * part_blocks + sub * copies + copy] = jnp.concatenate([block] * copies, axis=0)
    for white_ref in white_refs:
        white_ref[white_ref.shape[0] - 1] = jnp.zeros((SUB_ROWS, width), jnp.float32)
    sums_ref[...] = jnp.zeros_like(sums_ref)
    sub_row = lax.broadcasted_iota(jnp.int32, (SUB_ROWS, width), 0)

    def pick(white_ref, cell, side, place):
        rows = white_ref[place_ref[side, place]]
        for copy in range(1, SUB_ROWS // cell):
            other = white_ref[place_ref[side, place + copy]]
            rows = jnp.where(sub_row < copy * cell, rows, other)
        return rows

    subs = []
    for index, cell in enumerate(cells):
        subs += [(index, cell, pair) for pair in range(0, unit_pairs, SUB_ROWS // cell)]

    def tile_step(tile, carry):
        for unit in range(tile_units):
            for pack in range(0, len(subs), PACK_ROWS // SUB_ROWS):
                real_parts, imag_parts = [], []
                for index, cell, pair in subs[pack : pack + PACK_ROWS // SUB_ROWS]:
                    place = (tile * tile_units + unit) * unit_pairs + pair
                    first = pick(white_refs[index], cell, 0, place)
                    second = pick(white_refs[index], cell, 1, place)
                    real_a, imag_a = first[:, :num_bins], first[:, num_bins:]
                    real_b, imag_b = second[:, :num_bins], second[:, num_bins:]
                    real_parts.append(real_a * real_b + imag_a * imag_b)
                    imag_parts.append(imag_a * real_b - real_a * imag_b)
                start = unit * unit_rows + pack * SUB_ROWS
                own = slice(start, start + PACK_ROWS)
                real_part = jnp.concatenate(real_parts, axis=0).astype(jnp.bfloat16)
                imag_part = jnp.concatenate(imag_parts, axis=0).astype(jnp.bfloat16)
                for index in range(CLASSES):
                    bins = slice(index * class_bins, (index + 1) * class_bins)
                    middle = (2 * index + 1) * class_bins
                    cross_ref[own, middle - class_bins : middle] = real_part[:, bins]
                    cross_ref[own, middle : middle + class_bins] = imag_part[:, bins]
        for lag in range(quarter // LANES):
            for index in range(CLASSES):
                rows = slice(2 * index * class_bins, 2 * (index + 1) * class_bins)
                lag_ref[lag, index] = jnp.dot(
                    cross_ref[:, rows],
                    table_ref[rows, 2 * lag * LANES : 2 * (lag + 1) * LANES],
                    preferred_element_type=jnp.float32,
                )
        for lag in range(quarter // LANES):
            for unit in range(tile_units):
                group = groups_ref[tile * tile_units + unit]
                totals = [None] * len(cells)
                for sub, (index, _, _) in enumerate(subs):
                    start = unit * unit_rows + sub * SUB_ROWS
                    own = slice(start, start + SUB_ROWS)
                    direct = [lag_ref[lag, k, own, :LANES] for k in range(CLASSES)]
                    quad = [lag_ref[lag, k, own, LANES:] for k in range(CLASSES)]
                    terms = [phase_terms(d, q) for d, q in zip(*quarter_turns(direct, quad))]
                    if totals[index] is None:
                        totals[index] = terms
                    else:
                        totals[index] = [
                            [one + two for one, two in zip(old, new)] for old, new in zip(totals[index], terms)
                        ]
                for index, total in enumerate(totals):
                    for turn_index, kinds in enumerate(total):
                        lags = slice(turn_index * quarter + lag * LANES, turn_index * quarter + (lag + 1) * LANES)
                        for kind, value in enumerate(kinds):
                            sums_ref[kind, group, index, :, lags] += value
        return carry

    lax.fori_loop(0, tiles_ref[0], tile_step, 0)

    linear, coherence = [], []
    for group in range(NGRP):
        scale = norm_ref[group]
        for index, cell in enumerate(cells):
            folded = []
            for kind in range(3):
                whole = sums_ref[kind, group, index]
                total = whole[:cell]
                for start in range(cell, SUB_ROWS, cell):
                    total = total + whole[start : start + cell]
                folded.append(total)
            linear.append(folded[0] * scale)
            coherence.append(jnp.sqrt(folded[1] * folded[1] + folded[2] * folded[2]) * scale)
    smoothed = window_sum(jnp.concatenate(coherence, axis=0)) * (1.0 / (2 * HW + 1))
    stacks = jnp.concatenate(linear, axis=0) * smoothed * smoothed
    pieces, _, piece_lags = out_ref.shape
    for piece in range(pieces):
        out_ref[piece] = stacks[:, piece * piece_lags : (piece + 1) * piece_lags].astype(out_ref.dtype)


def pair_order(pair_blocks, live_pairs, stack_group, parts, part_blocks, unit_pairs, spare_units):
    owners, slots, _ = pair_blocks.shape
    total = owners * slots
    places = (-(-total // unit_pairs) + NGRP + spare_units) * unit_pairs
    group_index = jnp.arange(NGRP, dtype=jnp.int32)
    live = jnp.arange(slots, dtype=jnp.int32)[None, :] < live_pairs[:, None]
    member = (stack_group[:, :, None] == group_index) & live[:, :, None]
    member = member.reshape(total, NGRP).astype(jnp.int32)
    members = jnp.sum(member, axis=0)
    filled = (members + unit_pairs - 1) // unit_pairs * unit_pairs
    ends = jnp.cumsum(filled)
    rank = jnp.cumsum(member, axis=0) - 1
    place = jnp.sum(member * (rank + (ends - filled)[None, :] + 1), axis=1) - 1
    here = jnp.arange(places, dtype=jnp.int32)
    match = here[:, None] == place[None, :]
    me = lax.axis_index("pair")
    blocks = pair_blocks.reshape(total, 2).T
    held = (lax.rem(blocks, parts) ^ me) * part_blocks + blocks // parts
    empty = parts * part_blocks
    taken = jnp.sum(jnp.where(match[None], held[:, None, :] - empty, 0), axis=2) + empty
    unit_start = jnp.arange(places // unit_pairs, dtype=jnp.int32) * unit_pairs
    unit_group = jnp.minimum(jnp.sum((unit_start[:, None] >= ends[None, :]).astype(jnp.int32), axis=1), NGRP - 1)
    norm = 1.0 / jnp.sqrt(members.astype(jnp.float32))
    return ends[-1:] // unit_pairs, taken, unit_group, norm


def chunk_cells(own_channels):
    if own_channels != 2 * SUB_ROWS:
        return [[1] * own_channels]
    return [[8, 4], [4]]


def shards(spectra, pair_blocks, live_pairs, stack_group):
    parts = lax.axis_size("pair")
    me = lax.axis_index("pair")
    cores = lax.axis_size("lag")
    core = lax.axis_index("lag")
    part_blocks, _, channels, width = spectra.shape
    num_bins = width // 2
    lag_count = 2 * num_bins
    own_channels = channels // (parts * cores)
    chunks = chunk_cells(own_channels)
    unit_pairs = PACK_ROWS // min(chunks[-1])
    pieces = parts * cores
    tile_units = [max(1, rows // chunk_rows(cells, unit_pairs)) for cells, rows in zip(chunks, (288, 128))]

    used, taken, unit_group, norm = pair_order(
        pair_blocks, live_pairs, stack_group, parts, part_blocks, unit_pairs, max(tile_units)
    )

    def stack_call(cells, units, received):
        rows = part_blocks * sum(cells)
        if rows % PACK_ROWS:
            received = [jnp.concatenate(received, axis=0)]
        tiles = (used + units - 1) // units
        return pl.pallas_call(
            functools.partial(stack_kernel, len(received), cells, unit_pairs, units),
            out_shape=jax.ShapeDtypeStruct((pieces, NGRP * sum(cells), lag_count // pieces), jnp.float32),
            in_specs=[pl.BlockSpec(memory_space=pltpu.SMEM)] * 4
            + [pl.BlockSpec(memory_space=pltpu.VMEM)] * (len(received) + 1),
            out_specs=pl.BlockSpec(memory_space=pltpu.VMEM),
            scratch_shapes=[
                pltpu.VMEM((parts * part_blocks + 1, SUB_ROWS, width), jnp.float32) for _ in cells
            ]
            + [
                pltpu.VMEM((units * chunk_rows(cells, unit_pairs), width), jnp.bfloat16),
                pltpu.VMEM(
                    (lag_count // CLASSES // LANES, CLASSES, units * chunk_rows(cells, unit_pairs), 2 * LANES),
                    jnp.float32,
                ),
                pltpu.VMEM((3, NGRP, len(cells), SUB_ROWS, lag_count), jnp.float32),
            ],
            compiler_params=pltpu.CompilerParams(vmem_limit_bytes=20 * 1024 * 1024),
            name="stack",
        )(tiles, taken, unit_group, norm, *received, table)

    def move(value, shift):
        return lax.ppermute(value, "pair", [(i, i ^ shift) for i in range(parts)])

    starts = jnp.stack([((me ^ step) * cores + core) * own_channels for step in range(parts)])
    if own_channels % PACK_ROWS == 0:
        shapes = [jax.ShapeDtypeStruct((part_blocks * sum(cells), width), jnp.bfloat16) for cells in chunks]
        flat = pl.pallas_call(
            functools.partial(prepare_kernel, chunks),
            out_shape=shapes * parts,
            in_specs=[pl.BlockSpec(memory_space=pltpu.SMEM), pl.BlockSpec(memory_space=pltpu.HBM)],
            out_specs=[pl.BlockSpec(memory_space=pltpu.VMEM)] * (parts * len(chunks)),
            scratch_shapes=[
                pltpu.VMEM((parts, part_blocks, own_channels, width), jnp.bfloat16),
                pltpu.SemaphoreType.DMA((parts,)),
            ],
            compiler_params=pltpu.CompilerParams(vmem_limit_bytes=16 * 1024 * 1024),
            name="prepare",
        )(starts, spectra)
        pieces_of = [list(flat[index :: len(chunks)]) for index in range(len(chunks))]
    else:
        ordered = whiten(spectra).reshape(part_blocks, channels, 2, num_bins // CLASSES, CLASSES)
        ordered = ordered.swapaxes(3, 4).reshape(part_blocks, channels, width)
        pieces_of = [[]]
        for step in range(parts):
            piece = lax.dynamic_slice_in_dim(ordered, starts[step], own_channels, 1)
            pieces_of[0].append(piece.reshape(part_blocks * own_channels, width))

    received = []
    for index, chunk in enumerate(pieces_of):
        if index == 1:
            chunk[1:], received[0][2] = lax.optimization_barrier((chunk[1:], received[0][2]))
        received.append([chunk[0]] + [move(chunk[step], step) for step in range(1, parts)])
        if index == 0:
            used, received[0][2] = lax.optimization_barrier((used, received[0][2]))
            table = lag_table(used, lag_count, num_bins)
    stacks = [stack_call(cells, units, got) for cells, units, got in zip(chunks, tile_units, received)]

    stacks = jnp.concatenate(stacks, axis=1).astype(jnp.bfloat16)
    rows = stacks.shape[1]
    if cores == 2:
        stacks = stacks.reshape(parts, cores, rows, -1)
        mine = lax.dynamic_index_in_dim(stacks, core, 1, keepdims=False)
        other = lax.dynamic_index_in_dim(stacks, 1 - core, 1, keepdims=False)
        other = lax.ppermute(other, "lag", [(0, 1), (1, 0)])
        both = jnp.where(core == 0, jnp.stack([mine, other], 1), jnp.stack([other, mine], 1))
        got = []
        for step in range(parts):
            part = lax.dynamic_index_in_dim(both, me ^ step, 0, keepdims=False)
            got.append(move(part, step) if step else part)
        got = jnp.stack(got)[me ^ jnp.arange(parts, dtype=jnp.int32)]
    else:
        got = lax.all_to_all(stacks, ("pair", "lag"), 0, 0, tiled=True)
    got = got.reshape(pieces, rows, -1)
    blocks = []
    offset = 0
    for cell in map(sum, chunks):
        block = got[:, offset : offset + NGRP * cell].reshape(pieces, NGRP, cell, -1)
        blocks.append(block)
        offset += NGRP * cell
    whole = jnp.concatenate(blocks, axis=2)
    return whole.transpose(1, 0, 2, 3).reshape(NGRP, channels, -1).astype(jnp.float32)


def solution(mesh):
    return jax.shard_map(
        shards,
        mesh=mesh,
        in_specs=(P("win", "pair", "stk", None), P("win", None, None), P("win"), P("win", None)),
        out_specs=P("win", "stk", ("pair", "lag")),
        check_vma=False,
    )
```

time: 102 us -> 70.4 us (0.69)
  waiting for transfers between devices: 0.03 us -> 29.5 us
  local copies, waits for them, and re-layouts: 26.7 us -> 4.83 us
  other arithmetic: 20.8 us -> 2.36 us
  blocking collectives: 13.6 us -> 0 us
  Pallas kernels: 20.9 us -> 14 us
  between operations: 0.97 us -> 2.92 us
  starting transfers between devices: 18.8 us -> 17.3 us
    ppermute x12 -> x10, waiting for transfers between devices: 0.03 us -> 29.5 us  [the longest x9 28.3 us: move(): return lax.ppermute(value, 'pair', [(i, i ^ shift) for i in range(parts)])]
    all_to_all x1 -> x0, blocking collectives: 13.6 us -> none  [shards(): return lax.all_to_all(stacks, ('pair', 'lag'), 2, 1, tiled=True)]
    reshape x17 -> x1, local copies, waits for them, and re-layouts: 12.4 us -> 0.08 us  [pair_order(): blocks = pair_blocks.reshape(total, 2).T]
    sin x1 -> x0, other arithmetic: 9.35 us -> none  [lag_table(): sine_part = jnp.sin(angles)]
    convert_element_type x2 -> x1, other arithmetic: 7.94 us -> 0.02 us  [shards(): whole.transpose(1, 0, 2, 3).reshape(NGRP, channels, -1).astype(jnp.float32)]
    pallas_call x4, Pallas kernels: 20.9 us -> 14 us  [the longest x2 9.83 us: stack_call(): pl.pallas_call(functools.partial(stack_kernel, len(received), cells, unit...]
    dynamic_slice x1, local copies, waits for them, and re-layouts: 4.45 us -> 0.02 us  [shards(): part = lax.dynamic_index_in_dim(both, me ^ step, 0, keepdims=False)]
    unnamed x16 -> x10, local copies, waits for them, and re-layouts: 5.28 us -> 2.21 us
  transfers between devices with their start and end apart: 12 -> 10, of which waited for: 0 -> 6; matrix products, arithmetic and copies ran while one was open for 32% -> 5% of each run, Pallas kernels for 15% -> 11%
where the time goes in v2:
time: 70.4 us; the launch traced here: 71 us
  waiting for transfers between devices  29.5 us (42%)
  starting transfers between devices  17.3 us (25%)
  Pallas kernels  14 us (20%)
  local copies, waits for them, and re-layouts  4.83 us (7%)
  between operations  2.92 us (4%)
  other arithmetic  2.36 us (3%)
    ppermute x9, waiting for transfers between devices, move(): return lax.ppermute(value, 'pair', [(i, i ^ shift) for i in range(parts)])  28.3 us
    ppermute x9, starting transfers between devices, move(): return lax.ppermute(value, 'pair', [(i, i ^ shift) for i in range(parts)])  17.3 us
    pallas_call x2, Pallas kernels, stack_call(): pl.pallas_call(functools.partial(stack_kernel, len(received), cells, unit...  9.83 us
    pallas_call x1, Pallas kernels, shards(): pl.pallas_call(functools.partial(prepare_kernel, chunks), out_shape=shape...  3.08 us
    unnamed x10, local copies, waits for them, and re-layouts  2.21 us
    another operation x6, other arithmetic  1.47 us
  transfers between devices with their start and end apart: 10, of which 6 were waited for; matrix products, arithmetic and copies ran while one was open for 5% of the time, Pallas kernels for 11%

profile of v2, /device:TPU:0, one launch (start us, length us, event | category | flops | bytes accessed | tf_op | source)
XLA Modules:
  0.0 71.0 jit_solution(13736325910310498883)
XLA Ops:
  0.0 0.1 pad_add_fusion.start_ref
  0.1 2.2 %copy-done = bf16[16,1,128,1024]{3,2,1,0:T(8,128)(2,1)S(1)} copy-done((bf16[16,1,128,1024]{3,2,1,0:T(8,128)(2,1)S(1)}, bf16[16,1,128,1024]{3,2,1,0:T(8,128)(2,1)}, u32[]{:S(2)}) %copy-start) | copy-done | bytes 4194328
  2.3 3.1 %prepare.1 = (bf16[192,1024]{1,0:T(8,128)(2,1)S(1)}, bf16[64,1024]{1,0:T(8,128)(2,1)S(1)}, bf16[192,1024]{1,0:T(8,128)(2,1)S(1)}, bf16[64,1024]{1,0:T(8,128)(2,1...) custom-call(s32[4]{0:T(128)S(1)} %pad_add_fusion.start_ref, ...), custom_call_target="tpu_custom_call" | custom-call | tf_op jit(solution)/shard_map/prepare/pallas_call | solution.py:352
  5.4 4.1 %collective-permute-start = (bf16[192,1024]{1,0:T(8,128)(2,1)S(1)}, bf16[192,1024]{1,0:T(8,128)(2,1)S(1)}, u32[]{:S(2)}, u32[]{:S(2)}) collective-permute-start(bf16[192,1024]{1,0:T(8,128)(2,1)S(1)} %get-tuple-element.19), channel_id=1, source_target_pairs={{0,8},{4,12},{8,0},{12,4},{1,9},{5,13},{9,1},{13,5},{2,10},{6,14},... | collective-permute-start | bytes 1179656 | tf_op jit(solution)/shard_map/ppermute | solution.py:347
  9.5 1.6 %collective-permute-start.1 = (bf16[192,1024]{1,0:T(8,128)(2,1)S(1)}, bf16[192,1024]{1,0:T(8,128)(2,1)S(1)}, u32[]{:S(2)}, u32[]{:S(2)}) collective-permute-start(bf16[192,1024]{1,0:T(8,128)(2,1)S(1)} %get-tuple-element.22), channel_id=1, source_target_pairs={{0,4},{4,0},{8,12},{12,8},{1,5},{5,1},{9,13},{13,9},{2,6},{6,2},{1... | collective-permute-start | bytes 1179656 | tf_op jit(solution)/shard_map/ppermute | solution.py:347
  11.1 0.0 collective-permute-start.2
  11.1 0.0 copy-done.2
  11.1 0.1 eq.44
  11.2 0.0 copy-done.3
  11.2 0.1 iota_compare_fusion.3
  11.2 0.1 lt.53
  11.3 0.1 convert_reduce_fusion
  11.5 0.2 reduce-window.10
  11.7 1.2 %reduce-window.11 = s32[4,2,128]{2,1,0:T(2,128)S(1)} reduce-window(s32[4,2,128]{2,1,0:T(2,128)S(1)} %reshape.204, s32[]{:T(128)} %constant.119.clone.1), window={size=1x1x128 pad=0_0x0_0x127_0}, to_apply=%region_2.3 | reduce-window | flops 130048 | bytes 8196 | tf_op jit(solution)/shard_map/reduce-window.1
  12.9 0.1 slice.30
  13.0 0.1 copy.16
  13.1 0.1 copy.17
  13.2 0.1 add_bitcast_fusion
  13.3 0.1 fusion.6
  13.4 0.1 iota_compare_fusion
  13.5 0.0 copy-done.1
  13.5 0.1 reshape.200
  13.6 0.1 select_reduce_fusion
  13.8 0.6 slice.21
  17.0 0.1 convert_reduce_fusion.1
  17.1 11.7 %collective-permute-done.refs_2_ = bf16[192,1024]{1,0:T(8,128)(2,1)S(1)} collective-permute-done((bf16[192,1024]{1,0:T(8,128)(2,1)S(1)}, bf16[192,1024]{1,0:T(8,128)(2,1)S(1)}, u32[]{:S(2)}, u32[]{:S(2)}) %collective-permute-start) | collective-permute-done | bytes 393248 | tf_op jit(solution)/shard_map/ppermute | solution.py:347
  28.8 0.0 collective-permute-start.3
  28.8 3.6 %collective-permute-start.4 = (bf16[64,1024]{1,0:T(8,128)(2,1)S(1)}, bf16[64,1024]{1,0:T(8,128)(2,1)S(1)}, u32[]{:S(2)}, u32[]{:S(2)}) collective-permute-start(bf16[64,1024]{1,0:T(8,128)(2,1)S(1)} %get-tuple-element.31), channel_id=1, source_target_pairs={{0,8},{4,12},{8,0},{12,4},{1,9},{5,13},{9,1},{13,5},{2,10},{6,14},... | collective-permute-start | bytes 393224 | tf_op jit(solution)/shard_map/ppermute | solution.py:347
  32.4 0.8 %collective-permute-start.5 = (bf16[64,1024]{1,0:T(8,128)(2,1)S(1)}, bf16[64,1024]{1,0:T(8,128)(2,1)S(1)}, u32[]{:S(2)}, u32[]{:S(2)}) collective-permute-start(bf16[64,1024]{1,0:T(8,128)(2,1)S(1)} %get-tuple-element.32), channel_id=1, source_target_pairs={{0,12},{4,8},{8,4},{12,0},{1,13},{5,9},{9,5},{13,1},{2,14},{6,10},... | collective-permute-start | bytes 393224 | tf_op jit(solution)/shard_map/ppermute | solution.py:347
  33.2 1.1 %table.1.refs_4_ = bf16[1024,512]{1,0:T(8,128)(2,1)S(1)} custom-call(s32[1]{0:T(128)S(6)} %select_n.78.used_ref), custom_call_target="tpu_custom_call" | custom-call | tf_op jit(solution)/shard_map/table/pallas_call | solution.py:61
  34.4 0.0 collective-permute-done.1.refs_1_
  34.4 3.3 %collective-permute-done.2.refs_3_ = bf16[192,1024]{1,0:T(8,128)(2,1)S(1)} collective-permute-done((bf16[192,1024]{1,0:T(8,128)(2,1)S(1)}, bf16[192,1024]{1,0:T(8,128)(2,1)S(1)}, u32[]{:S(2)}, u32[]{:S(2)}) %collective-permute-start.2) | collective-permute-done | bytes 393248 | tf_op jit(solution)/shard_map/ppermute | solution.py:347
  37.7 6.5 %stack.54 = f32[8,48,128]{2,1,0:T(8,128)S(1)} custom-call(s32[1]{0:T(128)S(6)} %select_n.79.tiles_ref, s32[2,208]{1,0:T(2,128)S(1)} %broadcast_add_fusion.place_ref, s32[52]{0:T(128)S(1)} %broadcast_minimum_fusion.groups_ref, f32[4]{0:T(128)S(1)} %convert_rsqrt_fusion.norm_ref, bf16[192,1024]{1,0:T(8,128)(2,1)S(1)} %get-tuple-element.21.refs_0_, ...), custom_call_target="tpu_custom_call" | custom-call | tf_op jit(solution)/shard_map/stack/pallas_call | solution.py:325
  44.3 0.0 collective-permute-done.3.refs_1_
  44.3 8.9 %collective-permute-done.4.refs_2_ = bf16[64,1024]{1,0:T(8,128)(2,1)S(1)} collective-permute-done((bf16[64,1024]{1,0:T(8,128)(2,1)S(1)}, bf16[64,1024]{1,0:T(8,128)(2,1)S(1)}, u32[]{:S(2)}, u32[]{:S(2)}) %collective-permute-start.4) | collective-permute-done | bytes 131104 | tf_op jit(solution)/shard_map/ppermute | solution.py:347
  53.2 0.0 collective-permute-done.5.refs_3_
  53.2 3.3 %stack.55 = f32[8,16,128]{2,1,0:T(8,128)S(1)} custom-call(s32[1]{0:T(128)S(6)} %select_n.83.tiles_ref, s32[2,208]{1,0:T(2,128)S(1)} %broadcast_add_fusion.place_ref, s32[52]{0:T(128)S(1)} %broadcast_minimum_fusion.groups_ref, f32[4]{0:T(128)S(1)} %convert_rsqrt_fusion.norm_ref, bf16[64,1024]{1,0:T(8,128)(2,1)S(1)} %get-tuple-element.29.refs_0_, ...), custom_call_target="tpu_custom_call" | custom-call | tf_op jit(solution)/shard_map/stack/pallas_call | solution.py:325
  56.6 0.1 collective-permute-start.6
  56.7 1.2 %collective-permute-done.6 = bf16[4,64,128]{2,1,0:T(8,128)(2,1)S(1)} collective-permute-done((bf16[4,64,128]{2,1,0:T(8,128)(2,1)S(1)}, bf16[4,64,128]{2,1,0:T(8,128)(2,1)S(1)}, u32[]{:S(2)}, u32[]{:S(2)}) %collective-permute-start.6) | collective-permute-done | bytes 65568 | tf_op jit(solution)/shard_map/ppermute | solution.py:389
  57.9 4.4 %collective-permute-start.7 = (bf16[2,64,128]{2,1,0:T(8,128)(2,1)S(1)}, bf16[2,64,128]{2,1,0:T(8,128)(2,1)S(1)}, u32[]{:S(2)}, u32[]{:S(2)}) collective-permute-start(bf16[2,64,128]{2,1,0:T(8,128)(2,1)S(1)} %get-tuple-element.36), channel_id=1, source_target_pairs={{0,4},{4,0},{8,12},{12,8},{1,5},{5,1},{9,13},{13,9},{2,6},{6,2},{1... | collective-permute-start | bytes 98312 | tf_op jit(solution)/shard_map/ppermute | solution.py:347
  62.3 1.4 %collective-permute-start.8 = (bf16[2,64,128]{2,1,0:T(8,128)(2,1)S(1)}, bf16[2,64,128]{2,1,0:T(8,128)(2,1)S(1)}, u32[]{:S(2)}, u32[]{:S(2)}) collective-permute-start(bf16[2,64,128]{2,1,0:T(8,128)(2,1)S(1)} %get-tuple-element.35), channel_id=1, source_target_pairs={{0,8},{4,12},{8,0},{12,4},{1,9},{5,13},{9,1},{13,5},{2,10},{6,14},... | collective-permute-start | bytes 98312 | tf_op jit(solution)/shard_map/ppermute | solution.py:347
  63.7 1.4 %collective-permute-start.9 = (bf16[2,64,128]{2,1,0:T(8,128)(2,1)S(1)}, bf16[2,64,128]{2,1,0:T(8,128)(2,1)S(1)}, u32[]{:S(2)}, u32[]{:S(2)}) collective-permute-start(bf16[2,64,128]{2,1,0:T(8,128)(2,1)S(1)} %get-tuple-element.34), channel_id=1, source_target_pairs={{0,12},{4,8},{8,4},{12,0},{1,13},{5,9},{9,5},{13,1},{2,14},{6,10},... | collective-permute-start | bytes 98312 | tf_op jit(solution)/shard_map/ppermute | solution.py:347
  65.1 0.0 collective-permute-done.7
  65.1 2.5 %collective-permute-done.8 = bf16[2,64,128]{2,1,0:T(8,128)(2,1)S(1)} collective-permute-done((bf16[2,64,128]{2,1,0:T(8,128)(2,1)S(1)}, bf16[2,64,128]{2,1,0:T(8,128)(2,1)S(1)}, u32[]{:S(2)}, u32[]{:S(2)}) %collective-permute-start.8) | collective-permute-done | bytes 32800 | tf_op jit(solution)/shard_map/ppermute | solution.py:347
  67.6 1.8 %collective-permute-done.9 = bf16[2,64,128]{2,1,0:T(8,128)(2,1)S(1)} collective-permute-done((bf16[2,64,128]{2,1,0:T(8,128)(2,1)S(1)}, bf16[2,64,128]{2,1,0:T(8,128)(2,1)S(1)}, u32[]{:S(2)}, u32[]{:S(2)}) %collective-permute-start.9) | collective-permute-done | bytes 32800 | tf_op jit(solution)/shard_map/ppermute | solution.py:347
  69.4 0.6 gather_fusion
  70.0 0.1 copy.19
  70.2 0.8 %copy.20 = f32[4,8,16,128]{3,2,1,0:T(8,128)} copy(f32[4,8,16,128]{3,1,2,0:T(8,128)S(1)} %convert_bitcast_fusion) | data formatting | bytes 524288 | tf_op jit(solution)/shard_map/convert_element_type | solution.py:406
  (30 shorter events, 0.3 us)
Async XLA Ops:
  0.0 11.1 %copy-start.2 = (s32[4,40]{1,0:T(4,128)S(1)}, s32[4,40]{1,0:T(4,128)}, u32[]{:S(2)}) copy-start(s32[4,40]{1,0:T(4,128)} %param.7) | copy-start | bytes 1924
  0.0 11.2 %copy-start.3 = (s32[4]{0:T(128)S(1)}, s32[4]{0:T(128)}, u32[]{:S(2)}) copy-start(s32[4]{0:T(128)} %param.6) | copy-start | bytes 52
  0.0 13.5 %copy-start.1 = (s32[4,40,2]{1,2,0:T(2,128)S(1)}, s32[4,40,2]{1,2,0:T(2,128)}, u32[]{:S(2)}) copy-start(s32[4,40,2]{1,2,0:T(2,128)} %param.5) | copy-start | bytes 3844
  0.1 2.2 %copy-start = (bf16[16,1,128,1024]{3,2,1,0:T(8,128)(2,1)S(1)}, bf16[16,1,128,1024]{3,2,1,0:T(8,128)(2,1)}, u32[]{:S(2)}) copy-start(bf16[16,1,128,1024]{3,2,1,0:T(8,128)(2,1)} %spectra_ref.1) | copy-start | bytes 12582916
  5.4 23.4 %collective-permute-start = (bf16[192,1024]{1,0:T(8,128)(2,1)S(1)}, bf16[192,1024]{1,0:T(8,128)(2,1)S(1)}, u32[]{:S(2)}, u32[]{:S(2)}) collective-permute-start(bf16[192,1024]{1,0:T(8,128)(2,1)S(1)} %get-tuple-element.19), channel_id=1, source_target_pairs={{0,8},{4,12},{8,0},{12,4},{1,9},{5,13},{9,1},{13,5},{2,10},{6,14},... | collective-permute-start | bytes 1179656 | tf_op jit(solution)/shard_map/ppermute | solution.py:347
  9.5 24.9 %collective-permute-start.1 = (bf16[192,1024]{1,0:T(8,128)(2,1)S(1)}, bf16[192,1024]{1,0:T(8,128)(2,1)S(1)}, u32[]{:S(2)}, u32[]{:S(2)}) collective-permute-start(bf16[192,1024]{1,0:T(8,128)(2,1)S(1)} %get-tuple-element.22), channel_id=1, source_target_pairs={{0,4},{4,0},{8,12},{12,8},{1,5},{5,1},{9,13},{13,9},{2,6},{6,2},{1... | collective-permute-start | bytes 1179656 | tf_op jit(solution)/shard_map/ppermute | solution.py:347
  11.1 26.6 %collective-permute-start.2 = (bf16[192,1024]{1,0:T(8,128)(2,1)S(1)}, bf16[192,1024]{1,0:T(8,128)(2,1)S(1)}, u32[]{:S(2)}, u32[]{:S(2)}) collective-permute-start(bf16[192,1024]{1,0:T(8,128)(2,1)S(1)} %get-tuple-element.28), channel_id=1, source_target_pairs={{0,12},{4,8},{8,4},{12,0},{1,13},{5,9},{9,5},{13,1},{2,14},{6,10},... | collective-permute-start | bytes 1179656 | tf_op jit(solution)/shard_map/ppermute | solution.py:347
  28.8 15.5 %collective-permute-start.3 = (bf16[64,1024]{1,0:T(8,128)(2,1)S(1)}, bf16[64,1024]{1,0:T(8,128)(2,1)S(1)}, u32[]{:S(2)}, u32[]{:S(2)}) collective-permute-start(bf16[64,1024]{1,0:T(8,128)(2,1)S(1)} %get-tuple-element.30), channel_id=1, source_target_pairs={{0,4},{4,0},{8,12},{12,8},{1,5},{5,1},{9,13},{13,9},{2,6},{6,2},{1... | collective-permute-start | bytes 393224 | tf_op jit(solution)/shard_map/ppermute | solution.py:347
  28.8 24.4 %collective-permute-start.4 = (bf16[64,1024]{1,0:T(8,128)(2,1)S(1)}, bf16[64,1024]{1,0:T(8,128)(2,1)S(1)}, u32[]{:S(2)}, u32[]{:S(2)}) collective-permute-start(bf16[64,1024]{1,0:T(8,128)(2,1)S(1)} %get-tuple-element.31), channel_id=1, source_target_pairs={{0,8},{4,12},{8,0},{12,4},{1,9},{5,13},{9,1},{13,5},{2,10},{6,14},... | collective-permute-start | bytes 393224 | tf_op jit(solution)/shard_map/ppermute | solution.py:347
  32.4 20.8 %collective-permute-start.5 = (bf16[64,1024]{1,0:T(8,128)(2,1)S(1)}, bf16[64,1024]{1,0:T(8,128)(2,1)S(1)}, u32[]{:S(2)}, u32[]{:S(2)}) collective-permute-start(bf16[64,1024]{1,0:T(8,128)(2,1)S(1)} %get-tuple-element.32), channel_id=1, source_target_pairs={{0,12},{4,8},{8,4},{12,0},{1,13},{5,9},{9,5},{13,1},{2,14},{6,10},... | collective-permute-start | bytes 393224 | tf_op jit(solution)/shard_map/ppermute | solution.py:347
  56.6 1.3 %collective-permute-start.6 = (bf16[4,64,128]{2,1,0:T(8,128)(2,1)S(1)}, bf16[4,64,128]{2,1,0:T(8,128)(2,1)S(1)}, u32[]{:S(2)}, u32[]{:S(2)}) collective-permute-start(bf16[4,64,128]{2,1,0:T(8,128)(2,1)S(1)} %get-tuple-element.38), channel_id=1, source_target_pairs={{0,1},{1,0},{2,3},{3,2},{4,5},{5,4},{6,7},{7,6},{8,9},{9,8},{10,11... | collective-permute-start | bytes 196616 | tf_op jit(solution)/shard_map/ppermute | solution.py:389
  57.9 7.2 %collective-permute-start.7 = (bf16[2,64,128]{2,1,0:T(8,128)(2,1)S(1)}, bf16[2,64,128]{2,1,0:T(8,128)(2,1)S(1)}, u32[]{:S(2)}, u32[]{:S(2)}) collective-permute-start(bf16[2,64,128]{2,1,0:T(8,128)(2,1)S(1)} %get-tuple-element.36), channel_id=1, source_target_pairs={{0,4},{4,0},{8,12},{12,8},{1,5},{5,1},{9,13},{13,9},{2,6},{6,2},{1... | collective-permute-start | bytes 98312 | tf_op jit(solution)/shard_map/ppermute | solution.py:347
  62.3 5.2 %collective-permute-start.8 = (bf16[2,64,128]{2,1,0:T(8,128)(2,1)S(1)}, bf16[2,64,128]{2,1,0:T(8,128)(2,1)S(1)}, u32[]{:S(2)}, u32[]{:S(2)}) collective-permute-start(bf16[2,64,128]{2,1,0:T(8,128)(2,1)S(1)} %get-tuple-element.35), channel_id=1, source_target_pairs={{0,8},{4,12},{8,0},{12,4},{1,9},{5,13},{9,1},{13,5},{2,10},{6,14},... | collective-permute-start | bytes 98312 | tf_op jit(solution)/shard_map/ppermute | solution.py:347
  63.7 5.7 %collective-permute-start.9 = (bf16[2,64,128]{2,1,0:T(8,128)(2,1)S(1)}, bf16[2,64,128]{2,1,0:T(8,128)(2,1)S(1)}, u32[]{:S(2)}, u32[]{:S(2)}) collective-permute-start(bf16[2,64,128]{2,1,0:T(8,128)(2,1)S(1)} %get-tuple-element.34), channel_id=1, source_target_pairs={{0,12},{4,8},{8,4},{12,0},{1,13},{5,9},{9,5},{13,1},{2,14},{6,10},... | collective-permute-start | bytes 98312 | tf_op jit(solution)/shard_map/ppermute | solution.py:347

commit v3 on v2

--- a/solution.py
+++ b/solution.py
@@ -74,30 +74,19 @@
     return (values * lax.rsqrt(power + EPSILON)).astype(jnp.bfloat16)
 
 
-def prepare_kernel(chunks, start_ref, spectra_ref, *refs):
-    parts = start_ref.shape[0]
-    out_refs = refs[: parts * len(chunks)]
-    raw_ref, arrived = refs[parts * len(chunks) :]
-    _, blocks, own_channels, width = raw_ref.shape
+def prepare_kernel(chunks, wanted, *refs):
+    order = list(dict.fromkeys(step for step, _ in wanted))
+    raw_refs = dict(zip(order, refs))
+    out_refs = dict(zip(wanted, refs[len(order) :]))
+    blocks, _, own_channels, width = refs[0].shape
     num_bins = width // 2
     class_bins = num_bins // CLASSES
-    order = (2, 3, 1, 0) if parts == 4 else tuple(range(parts))
-
-    def fetch(step):
-        start = pl.multiple_of(start_ref[step], 2 * SUB_ROWS)
-        return pltpu.make_async_copy(
-            spectra_ref.at[:, 0, pl.ds(start, own_channels), :], raw_ref.at[step], arrived.at[step]
-        )
-
-    for step in order:
-        fetch(step).start()
     source = lax.broadcasted_iota(jnp.int32, (num_bins, num_bins), 0)
     target = lax.broadcasted_iota(jnp.int32, (num_bins, num_bins), 1)
-    wanted = (target & (class_bins - 1)) * CLASSES + target // class_bins
-    shuffle = jnp.where(source == wanted, 1.0, 0.0).astype(jnp.bfloat16)
+    moved = (target & (class_bins - 1)) * CLASSES + target // class_bins
+    shuffle = jnp.where(source == moved, 1.0, 0.0).astype(jnp.bfloat16)
     for step in order:
-        fetch(step).wait()
-        white = whiten(raw_ref[step].reshape(blocks * own_channels, width))
+        white = whiten(raw_refs[step][...].reshape(blocks * own_channels, width))
         halves = [
             jnp.dot(white[:, start : start + num_bins], shuffle, preferred_element_type=jnp.float32)
             for start in (0, num_bins)
@@ -105,7 +94,10 @@
         halves = [half.reshape(blocks, own_channels, num_bins) for half in halves]
         offset = 0
         for index, cells in enumerate(chunks):
-            out_ref = out_refs[step * len(chunks) + index]
+            if (step, index) not in out_refs:
+                offset += sum(cells)
+                continue
+            out_ref = out_refs[step, index]
             row = 0
             for cell in cells:
                 group = SUB_ROWS // cell
@@ -151,11 +143,18 @@
     return [direct, direct * inverse, quad * inverse]
 
 
-def stack_kernel(num_parts, cells, unit_pairs, tile_units, tiles_ref, place_ref, groups_ref, norm_ref, *refs):
-    part_refs = refs[:num_parts]
-    table_ref, out_ref = refs[num_parts : num_parts + 2]
-    white_refs = refs[num_parts + 2 : num_parts + 2 + len(cells)]
-    cross_ref, lag_ref, sums_ref = refs[num_parts + 2 + len(cells) :]
+def stack_kernel(num_parts, cells, unit_pairs, tile_units, num_done, tiles_ref, place_ref, groups_ref, norm_ref, *refs):
+    refs = list(refs)
+    part_refs = [refs.pop(0) for _ in range(num_parts)]
+    table_ref = refs.pop(0)
+    if num_done:
+        piece_ref = refs.pop(0)
+        done_refs = [refs.pop(0) for _ in range(num_done)]
+        near_ref, far_ref = refs.pop(0), refs.pop(0)
+    else:
+        out_ref = refs.pop(0)
+    white_refs = [refs.pop(0) for _ in cells]
+    cross_ref, lag_ref, sums_ref = refs[:3]
     part_rows, width = part_refs[0].shape
     num_bins = width // 2
     class_bins = num_bins // CLASSES
@@ -262,9 +261,34 @@
             coherence.append(jnp.sqrt(folded[1] * folded[1] + folded[2] * folded[2]) * scale)
     smoothed = window_sum(jnp.concatenate(coherence, axis=0)) * (1.0 / (2 * HW + 1))
     stacks = jnp.concatenate(linear, axis=0) * smoothed * smoothed
-    pieces, _, piece_lags = out_ref.shape
-    for piece in range(pieces):
-        out_ref[piece] = stacks[:, piece * piece_lags : (piece + 1) * piece_lags].astype(out_ref.dtype)
+    channels = sum(cells)
+    if not num_done:
+        for group in range(NGRP):
+            out_ref[group] = stacks[group * channels : (group + 1) * channels]
+        return
+    whole_ref = refs[3]
+    for group in range(NGRP):
+        rows = [ref[group] for ref in done_refs] + [stacks[group * channels : (group + 1) * channels]]
+        rows = jnp.concatenate(rows, axis=0)
+        whole_ref[group * rows.shape[0] : (group + 1) * rows.shape[0], :] = rows
+    parts, _, piece_lags = near_ref.shape
+    for step in range(parts):
+        for flip, out_ref in enumerate((near_ref, far_ref)):
+            piece = piece_ref[0] ^ (2 * step + flip)
+            lags = pl.ds(pl.multiple_of(piece * piece_lags, LANES), piece_lags)
+            out_ref[step] = whole_ref[:, lags].astype(out_ref.dtype)
+
+
+def place_kernel(piece_ref, *refs):
+    *step_refs, out_ref, held_ref = refs
+    for step, ref in enumerate(step_refs):
+        held_ref[2 * step : 2 * step + 2] = ref[...]
+    pieces = held_ref.shape[0]
+    cell = held_ref.shape[1] // NGRP
+    for source in range(pieces):
+        block = held_ref[piece_ref[0] ^ source].astype(jnp.float32)
+        for group in range(NGRP):
+            out_ref[group, source * cell : (source + 1) * cell, :] = block[group * cell : (group + 1) * cell]
 
 
 def pair_order(pair_blocks, live_pairs, stack_group, parts, part_blocks, unit_pairs, spare_units):
@@ -293,10 +317,10 @@
     return ends[-1:] // unit_pairs, taken, unit_group, norm
 
 
-def chunk_cells(own_channels):
-    if own_channels != 2 * SUB_ROWS:
+def chunk_cells(own_channels, parts, cores):
+    if (own_channels, parts, cores) != (2 * SUB_ROWS, 4, 2):
         return [[1] * own_channels]
-    return [[8, 4], [4]]
+    return [[8], [4], [4]]
 
 
 def shards(spectra, pair_blocks, live_pairs, stack_group):
@@ -308,60 +332,77 @@
     num_bins = width // 2
     lag_count = 2 * num_bins
     own_channels = channels // (parts * cores)
-    chunks = chunk_cells(own_channels)
+    chunks = chunk_cells(own_channels, parts, cores)
     unit_pairs = PACK_ROWS // min(chunks[-1])
     pieces = parts * cores
-    tile_units = [max(1, rows // chunk_rows(cells, unit_pairs)) for cells, rows in zip(chunks, (288, 128))]
+    here = (me * cores + core).reshape(1)
+    tile_units = [max(1, rows // chunk_rows(cells, unit_pairs)) for cells, rows in zip(chunks, (256, 128, 128))]
 
     used, taken, unit_group, norm = pair_order(
         pair_blocks, live_pairs, stack_group, parts, part_blocks, unit_pairs, max(tile_units)
     )
 
-    def stack_call(cells, units, received):
+    def stack_call(cells, units, received, done):
         rows = part_blocks * sum(cells)
         if rows % PACK_ROWS:
             received = [jnp.concatenate(received, axis=0)]
         tiles = (used + units - 1) // units
+        smem, vmem = pl.BlockSpec(memory_space=pltpu.SMEM), pl.BlockSpec(memory_space=pltpu.VMEM)
+        tile_rows = units * chunk_rows(cells, unit_pairs)
+        in_specs = [smem] * 4 + [vmem] * (len(received) + 1)
+        args = [tiles, taken, unit_group, norm, *received, table]
+        out_shape = jax.ShapeDtypeStruct((NGRP, sum(cells), lag_count), jnp.float32)
+        scratch = [pltpu.VMEM((parts * part_blocks + 1, SUB_ROWS, width), jnp.float32) for _ in cells]
+        scratch += [
+            pltpu.VMEM((tile_rows, width), jnp.bfloat16),
+            pltpu.VMEM((lag_count // CLASSES // LANES, CLASSES, tile_rows, 2 * LANES), jnp.float32),
+            pltpu.VMEM((3, NGRP, len(cells), SUB_ROWS, lag_count), jnp.float32),
+        ]
+        out_specs = vmem
+        if done:
+            in_specs += [smem] + [vmem] * len(done)
+            args += [here, *done]
+            piece = jax.ShapeDtypeStruct((parts, NGRP * own_channels, lag_count // pieces), jnp.bfloat16)
+            out_shape, out_specs = [piece, piece], [vmem, vmem]
+            scratch.append(pltpu.VMEM((NGRP * own_channels, lag_count), jnp.float32))
         return pl.pallas_call(
-            functools.partial(stack_kernel, len(received), cells, unit_pairs, units),
-            out_shape=jax.ShapeDtypeStruct((pieces, NGRP * sum(cells), lag_count // pieces), jnp.float32),
-            in_specs=[pl.BlockSpec(memory_space=pltpu.SMEM)] * 4
-            + [pl.BlockSpec(memory_space=pltpu.VMEM)] * (len(received) + 1),
-            out_specs=pl.BlockSpec(memory_space=pltpu.VMEM),
-            scratch_shapes=[
-                pltpu.VMEM((parts * part_blocks + 1, SUB_ROWS, width), jnp.float32) for _ in cells
-            ]
-            + [
-                pltpu.VMEM((units * chunk_rows(cells, unit_pairs), width), jnp.bfloat16),
-                pltpu.VMEM(
-                    (lag_count // CLASSES // LANES, CLASSES, units * chunk_rows(cells, unit_pairs), 2 * LANES),
-                    jnp.float32,
-                ),
-                pltpu.VMEM((3, NGRP, len(cells), SUB_ROWS, lag_count), jnp.float32),
-            ],
+            functools.partial(stack_kernel, len(received), cells, unit_pairs, units, len(done)),
+            out_shape=out_shape,
+            in_specs=in_specs,
+            out_specs=out_specs,
+            scratch_shapes=scratch,
             compiler_params=pltpu.CompilerParams(vmem_limit_bytes=20 * 1024 * 1024),
             name="stack",
-        )(tiles, taken, unit_group, norm, *received, table)
+        )(*args)
 
     def move(value, shift):
         return lax.ppermute(value, "pair", [(i, i ^ shift) for i in range(parts)])
 
-    starts = jnp.stack([((me ^ step) * cores + core) * own_channels for step in range(parts)])
-    if own_channels % PACK_ROWS == 0:
-        shapes = [jax.ShapeDtypeStruct((part_blocks * sum(cells), width), jnp.bfloat16) for cells in chunks]
-        flat = pl.pallas_call(
-            functools.partial(prepare_kernel, chunks),
-            out_shape=shapes * parts,
-            in_specs=[pl.BlockSpec(memory_space=pltpu.SMEM), pl.BlockSpec(memory_space=pltpu.HBM)],
-            out_specs=[pl.BlockSpec(memory_space=pltpu.VMEM)] * (parts * len(chunks)),
-            scratch_shapes=[
-                pltpu.VMEM((parts, part_blocks, own_channels, width), jnp.bfloat16),
-                pltpu.SemaphoreType.DMA((parts,)),
-            ],
-            compiler_params=pltpu.CompilerParams(vmem_limit_bytes=16 * 1024 * 1024),
-            name="prepare",
-        )(starts, spectra)
-        pieces_of = [list(flat[index :: len(chunks)]) for index in range(len(chunks))]
+    starts = [((me ^ step) * cores + core) * own_channels for step in range(parts)]
+    if len(chunks) > 1:
+        pieces_of = [[None] * parts for _ in chunks]
+        raw = {}
+        calls = [[(2, 0)], [(3, 0), (1, 0)], [(0, 0)] + [(step, index) for index in range(1, len(chunks)) for step in range(parts)]]
+        for wanted in calls:
+            steps = list(dict.fromkeys(step for step, _ in wanted))
+            for step in steps:
+                if step not in raw:
+                    raw[step] = lax.dynamic_slice_in_dim(spectra, starts[step], own_channels, 2)
+            flat = pl.pallas_call(
+                functools.partial(prepare_kernel, chunks, wanted),
+                out_shape=[
+                    jax.ShapeDtypeStruct((part_blocks * sum(chunks[index]), width), jnp.bfloat16)
+                    for _, index in wanted
+                ],
+                in_specs=[pl.BlockSpec(memory_space=pltpu.VMEM)] * len(steps),
+                out_specs=[pl.BlockSpec(memory_space=pltpu.VMEM)] * len(wanted),
+                compiler_params=pltpu.CompilerParams(vmem_limit_bytes=16 * 1024 * 1024),
+                name="prepare",
+            )(*[raw[step] for step in steps])
+            flat = list(flat)
+            flat[0], starts = lax.optimization_barrier((flat[0], starts))
+            for (step, index), piece in zip(wanted, flat):
+                pieces_of[index][step] = piece
     else:
         ordered = whiten(spectra).reshape(part_blocks, channels, 2, num_bins // CLASSES, CLASSES)
         ordered = ordered.swapaxes(3, 4).reshape(part_blocks, channels, width)
@@ -370,40 +411,35 @@
             piece = lax.dynamic_slice_in_dim(ordered, starts[step], own_channels, 1)
             pieces_of[0].append(piece.reshape(part_blocks * own_channels, width))
 
-    received = []
-    for index, chunk in enumerate(pieces_of):
+    received, done = [], []
+    for index, (cells, units, chunk) in enumerate(zip(chunks, tile_units, pieces_of)):
         if index == 1:
             chunk[1:], received[0][2] = lax.optimization_barrier((chunk[1:], received[0][2]))
+        if index > 1:
+            chunk[1:], done[index - 2] = lax.optimization_barrier((chunk[1:], done[index - 2]))
         received.append([chunk[0]] + [move(chunk[step], step) for step in range(1, parts)])
         if index == 0:
-            used, received[0][2] = lax.optimization_barrier((used, received[0][2]))
+            if parts > 2:
+                used, received[0][2] = lax.optimization_barrier((used, received[0][2]))
             table = lag_table(used, lag_count, num_bins)
-    stacks = [stack_call(cells, units, got) for cells, units, got in zip(chunks, tile_units, received)]
-
-    stacks = jnp.concatenate(stacks, axis=1).astype(jnp.bfloat16)
-    rows = stacks.shape[1]
-    if cores == 2:
-        stacks = stacks.reshape(parts, cores, rows, -1)
-        mine = lax.dynamic_index_in_dim(stacks, core, 1, keepdims=False)
-        other = lax.dynamic_index_in_dim(stacks, 1 - core, 1, keepdims=False)
-        other = lax.ppermute(other, "lag", [(0, 1), (1, 0)])
-        both = jnp.where(core == 0, jnp.stack([mine, other], 1), jnp.stack([other, mine], 1))
-        got = []
-        for step in range(parts):
-            part = lax.dynamic_index_in_dim(both, me ^ step, 0, keepdims=False)
-            got.append(move(part, step) if step else part)
-        got = jnp.stack(got)[me ^ jnp.arange(parts, dtype=jnp.int32)]
-    else:
-        got = lax.all_to_all(stacks, ("pair", "lag"), 0, 0, tiled=True)
-    got = got.reshape(pieces, rows, -1)
-    blocks = []
-    offset = 0
-    for cell in map(sum, chunks):
-        block = got[:, offset : offset + NGRP * cell].reshape(pieces, NGRP, cell, -1)
-        blocks.append(block)
-        offset += NGRP * cell
-    whole = jnp.concatenate(blocks, axis=2)
-    return whole.transpose(1, 0, 2, 3).reshape(NGRP, channels, -1).astype(jnp.float32)
+        if len(chunks) == 1:
+            return lax.all_to_all(stack_call(cells, units, received[0], []), ("pair", "lag"), 2, 1, tiled=True)
+        if index < len(chunks) - 1:
+            done.append(stack_call(cells, units, received[index], []))
+
+    near, far = stack_call(chunks[-1], tile_units[-1], received[-1], done)
+    other = lax.ppermute(far, "lag", [(i, i ^ 1) for i in range(cores)])
+    both = jnp.stack([near, other], 1)
+    arrived = [both[0]] + [move(both[step], step) for step in range(1, parts)]
+    return pl.pallas_call(
+        place_kernel,
+        out_shape=jax.ShapeDtypeStruct((NGRP, channels, lag_count // pieces), jnp.float32),
+        in_specs=[pl.BlockSpec(memory_space=pltpu.SMEM)] + [pl.BlockSpec(memory_space=pltpu.VMEM)] * parts,
+        out_specs=pl.BlockSpec(memory_space=pltpu.VMEM),
+        scratch_shapes=[pltpu.VMEM((pieces, NGRP * own_channels, lag_count // pieces), jnp.bfloat16)],
+        compiler_params=pltpu.CompilerParams(vmem_limit_bytes=8 * 1024 * 1024),
+        name="place",
+    )(here, *arrived)
 
 
 def solution(mesh):

time: 70.4 us -> 65.5 us (0.930); the launches traced: 71 us -> 65 us
  waiting for transfers between devices: 29.5 us -> 19.6 us
  starting transfers between devices: 17.3 us -> 20.7 us
    ppermute x9 -> x12, waiting for transfers between devices: 28.3 us -> 18.4 us  [move(): return lax.ppermute(value, 'pair', [(i, i ^ shift) for i in range(parts)])]
    dynamic_slice x1 -> x3, local copies, waits for them, and re-layouts: 0.02 us -> 4.34 us  [shards(): raw[step] = lax.dynamic_slice_in_dim(spectra, starts[step], own_channels, 2)]
    ppermute x9 -> x12, starting transfers between devices: 17.3 us -> 20.6 us  [move(): return lax.ppermute(value, 'pair', [(i, i ^ shift) for i in range(parts)])]
    unnamed x10 -> x8, local copies, waits for them, and re-layouts: 2.21 us -> 0.02 us
    convert_element_type x1 -> x0, local copies, waits for them, and re-layouts: 0.75 us -> none  [shards(): whole.transpose(1, 0, 2, 3).reshape(NGRP, channels, -1).astype(jnp.float32)]
    gather x2 -> x0, local copies, waits for them, and re-layouts: 0.71 us -> none  [shards(): got = jnp.stack(got)[me ^ jnp.arange(parts, dtype=jnp.int32)]]
    pallas_call x1 -> x4, Pallas kernels: 3.08 us -> 3.66 us  [the longest x3 2.93 us: shards(): pl.pallas_call(functools.partial(prepare_kernel, chunks, wanted), out_sha...]
    pallas_call x2 -> x3, Pallas kernels: 9.83 us -> 9.43 us  [stack_call(): pl.pallas_call(functools.partial(stack_kernel, len(received), cells, unit...]
  transfers between devices with their start and end apart: 10 -> 13, of which waited for: 6 -> 6; matrix products, arithmetic and copies ran while one was open for 5% -> 10% of each run, Pallas kernels for 11% -> 15%
where the time goes in v3:
time: 65.5 us; the launch traced here: 65 us
  starting transfers between devices  20.7 us (32%)
  waiting for transfers between devices  19.6 us (30%)
  Pallas kernels  14.2 us (22%)
  local copies, waits for them, and re-layouts  5.49 us (8%)
  between operations  2.83 us (4%)
  other arithmetic  2.19 us (3%)
    ppermute x12, starting transfers between devices, move(): return lax.ppermute(value, 'pair', [(i, i ^ shift) for i in range(parts)])  20.6 us
    ppermute x12, waiting for transfers between devices, move(): return lax.ppermute(value, 'pair', [(i, i ^ shift) for i in range(parts)])  18.4 us
    pallas_call x3, Pallas kernels, stack_call(): pl.pallas_call(functools.partial(stack_kernel, len(received), cells, unit...  9.43 us
    dynamic_slice x3, local copies, waits for them, and re-layouts, shards(): raw[step] = lax.dynamic_slice_in_dim(spectra, starts[step], own_channels, 2)  4.34 us
    pallas_call x3, Pallas kernels, shards(): pl.pallas_call(functools.partial(prepare_kernel, chunks, wanted), out_sha...  2.93 us
    another operation x4, other arithmetic  1.45 us
  transfers between devices with their start and end apart: 13, of which 6 were waited for; matrix products, arithmetic and copies ran while one was open for 10% of the time, Pallas kernels for 15%

profile of v3, /device:TPU:0, one launch (start us, length us, event | category | flops | bytes accessed | tf_op | source)
XLA Modules:
  0.0 65.0 jit_solution(1070672259531894018)
XLA Ops:
  0.0 1.1 %constant_dynamic-slice_fusion.3.refs_0_.refs_2_ = bf16[16,1,16,1024]{3,2,1,0:T(8,128)(2,1)S(1)} fusion(bf16[16,1,128,1024]{3,2,1,0:T(8,128)(2,1)} %param.4, s32[]{:T(128)S(6)} %select_n.51), kind=kLoop, calls=%fused_computation.50 | loop fusion | bytes 1048580 | tf_op jit(solution)/shard_map/dynamic_slice | solution.py:390
  1.1 0.6 prepare.3
  1.8 4.1 %collective-permute-start = (bf16[128,1024]{1,0:T(8,128)(2,1)S(1)}, bf16[128,1024]{1,0:T(8,128)(2,1)S(1)}, u32[]{:S(2)}, u32[]{:S(2)}) collective-permute-start(bf16[128,1024]{1,0:T(8,128)(2,1)S(1)} %prepare.3), channel_id=1, source_target_pairs={{0,8},{4,12},{8,0},{12,4},{1,9},{5,13},{9,1},{13,5},{2,10},{6,14},... | collective-permute-start | bytes 786440 | tf_op jit(solution)/shard_map/ppermute | solution.py:379
  5.9 1.9 %constant_dynamic-slice_fusion = (bf16[16,1,16,1024]{3,2,1,0:T(8,128)(2,1)S(1)}, bf16[16,1,16,1024]{3,2,1,0:T(8,128)(2,1)S(1)}) fusion(bf16[16,1,128,1024]{3,2,1,0:T(8,128)(2,1)} %param.4, s32[]{:T(128)S(6)} %select_n.57, s32[]{:T(128)S(6)} %select_n.56), kind=kLoop, calls=%fused_computation.47 | loop fusion | bytes 2097160 | tf_op jit(solution)/shard_map/dynamic_slice | solution.py:390
  7.7 0.9 %prepare.4 = (bf16[128,1024]{1,0:T(8,128)(2,1)S(1)}, bf16[128,1024]{1,0:T(8,128)(2,1)S(1)}) custom-call(bf16[16,1,16,1024]{3,2,1,0:T(8,128)(2,1)S(1)} %get-tuple-element.64.refs_0_.refs_3_, bf16[16,1,16,1024]{3,2,1,0:T(8,128)(2,1)S(1)} %get-tuple-element.63.refs_1_), custom_call_target="tpu_custom_call" | custom-call | tf_op jit(solution)/shard_map/prepare/pallas_call | solution.py:391
  8.6 1.4 %collective-permute-start.2 = (bf16[128,1024]{1,0:T(8,128)(2,1)S(1)}, bf16[128,1024]{1,0:T(8,128)(2,1)S(1)}, u32[]{:S(2)}, u32[]{:S(2)}) collective-permute-start(bf16[128,1024]{1,0:T(8,128)(2,1)S(1)} %get-tuple-element.49), channel_id=1, source_target_pairs={{0,12},{4,8},{8,4},{12,0},{1,13},{5,9},{9,5},{13,1},{2,14},{6,10},... | collective-permute-start | bytes 786440 | tf_op jit(solution)/shard_map/ppermute | solution.py:379
  10.0 0.3 collective-permute-start.1
  10.3 0.1 eq.40
  10.4 0.1 iota_compare_fusion.3
  10.5 0.1 lt.35
  10.6 0.1 convert_reduce_fusion
  10.7 0.2 reduce-window.10
  10.9 1.2 %reduce-window.11 = s32[4,2,128]{2,1,0:T(2,128)S(1)} reduce-window(s32[4,2,128]{2,1,0:T(2,128)S(1)} %reshape.172, s32[]{:T(128)} %constant.99.clone.1), window={size=1x1x128 pad=0_0x0_0x127_0}, to_apply=%region_2.3 | reduce-window | flops 130048 | bytes 8196 | tf_op jit(solution)/shard_map/reduce-window.1
  12.2 0.1 slice.36
  12.2 0.1 copy.10
  12.4 0.1 copy.11
  12.5 0.1 add_bitcast_fusion
  12.6 0.1 fusion.10
  12.7 0.1 iota_compare_fusion
  12.8 0.1 reshape.171
  12.9 0.1 select_reduce_fusion
  13.0 1.4 %constant_dynamic-slice_fusion.2.refs_0_ = bf16[16,1,16,1024]{3,2,1,0:T(8,128)(2,1)S(1)} fusion(bf16[16,1,128,1024]{3,2,1,0:T(8,128)(2,1)} %param.4, s32[]{:T(128)S(6)} %select_n.58), kind=kLoop, calls=%fused_computation.49 | loop fusion | bytes 1048580 | tf_op jit(solution)/shard_map/dynamic_slice | solution.py:390
  14.4 0.1 convert_reduce_fusion.1
  14.5 0.6 slice.27
  16.4 1.5 %prepare.5 = (bf16[128,1024]{1,0:T(8,128)(2,1)S(1)}, bf16[64,1024]{1,0:T(8,128)(2,1)S(1)}, bf16[64,1024]{1,0:T(8,128)(2,1)S(1)}, bf16[64,1024]{1,0:T(8,128)(2,1)...) custom-call(bf16[16,1,16,1024]{3,2,1,0:T(8,128)(2,1)S(1)} %constant_, ...), custom_call_target="tpu_custom_call" | custom-call | tf_op jit(solution)/shard_map/prepare/pallas_call | solution.py:391
  19.2 5.1 %collective-permute-done.refs_2_ = bf16[128,1024]{1,0:T(8,128)(2,1)S(1)} collective-permute-done((bf16[128,1024]{1,0:T(8,128)(2,1)S(1)}, bf16[128,1024]{1,0:T(8,128)(2,1)S(1)}, u32[]{:S(2)}, u32[]{:S(2)}) %collective-permute-start) | collective-permute-done | bytes 262176 | tf_op jit(solution)/shard_map/ppermute | solution.py:379
  24.3 0.0 collective-permute-start.6
  24.3 1.1 %table.1.refs_4_ = bf16[1024,512]{1,0:T(8,128)(2,1)S(1)} custom-call(s32[1]{0:T(128)S(6)} %select_n.50.used_ref), custom_call_target="tpu_custom_call" | custom-call | tf_op jit(solution)/shard_map/table/pallas_call | solution.py:61
  25.4 3.4 %collective-permute-start.7 = (bf16[64,1024]{1,0:T(8,128)(2,1)S(1)}, bf16[64,1024]{1,0:T(8,128)(2,1)S(1)}, u32[]{:S(2)}, u32[]{:S(2)}) collective-permute-start(bf16[64,1024]{1,0:T(8,128)(2,1)S(1)} %get-tuple-element.59), channel_id=1, source_target_pairs={{0,8},{4,12},{8,0},{12,4},{1,9},{5,13},{9,1},{13,5},{2,10},{6,14},... | collective-permute-start | bytes 393224 | tf_op jit(solution)/shard_map/ppermute | solution.py:379
  28.9 1.0 %collective-permute-start.8 = (bf16[64,1024]{1,0:T(8,128)(2,1)S(1)}, bf16[64,1024]{1,0:T(8,128)(2,1)S(1)}, u32[]{:S(2)}, u32[]{:S(2)}) collective-permute-start(bf16[64,1024]{1,0:T(8,128)(2,1)S(1)} %get-tuple-element.60), channel_id=1, source_target_pairs={{0,12},{4,8},{8,4},{12,0},{1,13},{5,9},{9,5},{13,1},{2,14},{6,10},... | collective-permute-start | bytes 393224 | tf_op jit(solution)/shard_map/ppermute | solution.py:379
  29.9 3.8 %stack.15.refs_6_ = f32[4,8,1024]{2,1,0:T(8,128)S(1)} custom-call(s32[1]{0:T(128)S(6)} %select_n.52.tiles_ref, s32[2,208]{1,0:T(2,128)S(1)} %broadcast_add_fusion.place_ref, s32[52]{0:T(128)S(1)} %broadcast_minimum_fusion.groups_ref, f32[4]{0:T(128)S(1)} %convert_rsqrt_fusion.norm_ref, bf16[128,1024]{1,0:T(8,128)(2,1)S(1)} %get-tuple-element.46.refs_0_, ...), custom_call_target="tpu_custom_call" | custom-call | tf_op jit(solution)/shard_map/stack/pallas_call | solution.py:368
  33.7 0.1 collective-permute-start.3
  33.7 3.4 %collective-permute-start.4 = (bf16[64,1024]{1,0:T(8,128)(2,1)S(1)}, bf16[64,1024]{1,0:T(8,128)(2,1)S(1)}, u32[]{:S(2)}, u32[]{:S(2)}) collective-permute-start(bf16[64,1024]{1,0:T(8,128)(2,1)S(1)} %get-tuple-element.51), channel_id=1, source_target_pairs={{0,8},{4,12},{8,0},{12,4},{1,9},{5,13},{9,1},{13,5},{2,10},{6,14},... | collective-permute-start | bytes 393224 | tf_op jit(solution)/shard_map/ppermute | solution.py:379
  37.1 0.0 collective-permute-done.6.refs_1_
  37.1 1.0 %collective-permute-start.5 = (bf16[64,1024]{1,0:T(8,128)(2,1)S(1)}, bf16[64,1024]{1,0:T(8,128)(2,1)S(1)}, u32[]{:S(2)}, u32[]{:S(2)}) collective-permute-start(bf16[64,1024]{1,0:T(8,128)(2,1)S(1)} %get-tuple-element.52), channel_id=1, source_target_pairs={{0,12},{4,8},{8,4},{12,0},{1,13},{5,9},{9,5},{13,1},{2,14},{6,10},... | collective-permute-start | bytes 393224 | tf_op jit(solution)/shard_map/ppermute | solution.py:379
  38.1 0.5 collective-permute-done.7.refs_2_
  38.6 0.0 collective-permute-done.8.refs_3_
  38.6 2.8 %stack.16.refs_7_ = f32[4,4,1024]{2,1,0:T(4,128)S(1)} custom-call(s32[1]{0:T(128)S(6)} %select_n.52.tiles_ref, s32[2,208]{1,0:T(2,128)S(1)} %broadcast_add_fusion.place_ref, s32[52]{0:T(128)S(1)} %broadcast_minimum_fusion.groups_ref, f32[4]{0:T(128)S(1)} %convert_rsqrt_fusion.norm_ref, bf16[64,1024]{1,0:T(8,128)(2,1)S(1)} %get-tuple-element.54.refs_0_, ...), custom_call_target="tpu_custom_call" | custom-call | tf_op jit(solution)/shard_map/stack/pallas_call | solution.py:368
  41.5 8.4 %collective-permute-done.4.refs_2_ = bf16[64,1024]{1,0:T(8,128)(2,1)S(1)} collective-permute-done((bf16[64,1024]{1,0:T(8,128)(2,1)S(1)}, bf16[64,1024]{1,0:T(8,128)(2,1)S(1)}, u32[]{:S(2)}, u32[]{:S(2)}) %collective-permute-start.4) | collective-permute-done | bytes 131104 | tf_op jit(solution)/shard_map/ppermute | solution.py:379
  49.9 2.8 %stack.17 = (bf16[4,64,128]{2,1,0:T(8,128)(2,1)S(1)}, bf16[4,64,128]{2,1,0:T(8,128)(2,1)S(1)}) custom-call(s32[1]{0:T(128)S(6)} %select_n.52.tiles_ref, s32[2,208]{1,0:T(2,128)S(1)} %broadcast_add_fusion.place_ref, s32[52]{0:T(128)S(1)} %broadcast_minimum_fusion.groups_ref, f32[4]{0:T(128)S(1)} %convert_rsqrt_fusion.norm_ref, ...), custom_call_target="tpu_custom_call" | custom-call | tf_op jit(solution)/shard_map/stack/pallas_call | solution.py:368
  52.7 0.1 collective-permute-start.9
  52.8 1.2 %collective-permute-done.9 = bf16[4,64,128]{2,1,0:T(8,128)(2,1)S(1)} collective-permute-done((bf16[4,64,128]{2,1,0:T(8,128)(2,1)S(1)}, bf16[4,64,128]{2,1,0:T(8,128)(2,1)S(1)}, u32[]{:S(2)}, u32[]{:S(2)}) %collective-permute-start.9) | collective-permute-done | bytes 65568 | tf_op jit(solution)/shard_map/ppermute | solution.py:431
  54.1 2.6 %collective-permute-start.10 = (bf16[2,64,128]{2,1,0:T(8,128)(2,1)S(1)}, bf16[2,64,128]{2,1,0:T(8,128)(2,1)S(1)}, u32[]{:S(2)}, u32[]{:S(2)}) collective-permute-start(bf16[2,64,128]{2,1,0:T(8,128)(2,1)S(1)} %get-tuple-element.67), channel_id=1, source_target_pairs={{0,4},{4,0},{8,12},{12,8},{1,5},{5,1},{9,13},{13,9},{2,6},{6,2},{1... | collective-permute-start | bytes 98312 | tf_op jit(solution)/shard_map/ppermute | solution.py:379
  56.7 1.9 %collective-permute-start.11 = (bf16[2,64,128]{2,1,0:T(8,128)(2,1)S(1)}, bf16[2,64,128]{2,1,0:T(8,128)(2,1)S(1)}, u32[]{:S(2)}, u32[]{:S(2)}) collective-permute-start(bf16[2,64,128]{2,1,0:T(8,128)(2,1)S(1)} %get-tuple-element.68), channel_id=1, source_target_pairs={{0,8},{4,12},{8,0},{12,4},{1,9},{5,13},{9,1},{13,5},{2,10},{6,14},... | collective-permute-start | bytes 98312 | tf_op jit(solution)/shard_map/ppermute | solution.py:379
  58.6 1.4 %collective-permute-start.12 = (bf16[2,64,128]{2,1,0:T(8,128)(2,1)S(1)}, bf16[2,64,128]{2,1,0:T(8,128)(2,1)S(1)}, u32[]{:S(2)}, u32[]{:S(2)}) collective-permute-start(bf16[2,64,128]{2,1,0:T(8,128)(2,1)S(1)} %get-tuple-element.65), channel_id=1, source_target_pairs={{0,12},{4,8},{8,4},{12,0},{1,13},{5,9},{9,5},{13,1},{2,14},{6,10},... | collective-permute-start | bytes 98312 | tf_op jit(solution)/shard_map/ppermute | solution.py:379
  59.9 1.8 %collective-permute-done.11.refs_2_ = bf16[2,64,128]{2,1,0:T(8,128)(2,1)S(1)} collective-permute-done((bf16[2,64,128]{2,1,0:T(8,128)(2,1)S(1)}, bf16[2,64,128]{2,1,0:T(8,128)(2,1)S(1)}, u32[]{:S(2)}, u32[]{:S(2)}) %collective-permute-start.11) | collective-permute-done | bytes 32800 | tf_op jit(solution)/shard_map/ppermute | solution.py:379
  61.7 2.6 %collective-permute-done.12.refs_3_ = bf16[2,64,128]{2,1,0:T(8,128)(2,1)S(1)} collective-permute-done((bf16[2,64,128]{2,1,0:T(8,128)(2,1)S(1)}, bf16[2,64,128]{2,1,0:T(8,128)(2,1)S(1)}, u32[]{:S(2)}, u32[]{:S(2)}) %collective-permute-start.12) | collective-permute-done | bytes 32800 | tf_op jit(solution)/shard_map/ppermute | solution.py:379
  64.3 0.7 %place.1 = f32[4,128,128]{2,1,0:T(8,128)} custom-call(s32[1]{0:T(128)} %bitcast.refs_5_.piece_ref, bf16[2,64,128]{2,1,0:T(8,128)(2,1)S(1)} %get-tuple-element.66.refs_0_, bf16[2,64,128]{2,1,0:T(8,128)(2,1)S(1)} %collective-permute-done.10.refs_1_, bf16[2,64,128]{2,1,0:T(8,128)(2,1)S(1)} %collective-permute-done.11.refs_2_, ...), custom_call_target="tpu_custom_call" | custom-call | tf_op jit(solution)/shard_map/place/pallas_call | solution.py:434
  (27 shorter events, 0.2 us)
Async XLA Ops:
  0.0 10.3 %copy-start.1 = (s32[4,40]{1,0:T(4,128)S(1)}, s32[4,40]{1,0:T(4,128)}, u32[]{:S(2)}) copy-start(s32[4,40]{1,0:T(4,128)} %param.7) | copy-start | bytes 1924
  0.0 10.4 %copy-start.2 = (s32[4]{0:T(128)S(1)}, s32[4]{0:T(128)}, u32[]{:S(2)}) copy-start(s32[4]{0:T(128)} %param.6) | copy-start | bytes 52
  0.0 12.8 %copy-start = (s32[4,40,2]{1,2,0:T(2,128)S(1)}, s32[4,40,2]{1,2,0:T(2,128)}, u32[]{:S(2)}) copy-start(s32[4,40,2]{1,2,0:T(2,128)} %param.5) | copy-start | bytes 3844
  1.8 22.5 %collective-permute-start = (bf16[128,1024]{1,0:T(8,128)(2,1)S(1)}, bf16[128,1024]{1,0:T(8,128)(2,1)S(1)}, u32[]{:S(2)}, u32[]{:S(2)}) collective-permute-start(bf16[128,1024]{1,0:T(8,128)(2,1)S(1)} %prepare.3), channel_id=1, source_target_pairs={{0,8},{4,12},{8,0},{12,4},{1,9},{5,13},{9,1},{13,5},{2,10},{6,14},... | collective-permute-start | bytes 786440 | tf_op jit(solution)/shard_map/ppermute | solution.py:379
  8.6 21.3 %collective-permute-start.2 = (bf16[128,1024]{1,0:T(8,128)(2,1)S(1)}, bf16[128,1024]{1,0:T(8,128)(2,1)S(1)}, u32[]{:S(2)}, u32[]{:S(2)}) collective-permute-start(bf16[128,1024]{1,0:T(8,128)(2,1)S(1)} %get-tuple-element.49), channel_id=1, source_target_pairs={{0,12},{4,8},{8,4},{12,0},{1,13},{5,9},{9,5},{13,1},{2,14},{6,10},... | collective-permute-start | bytes 786440 | tf_op jit(solution)/shard_map/ppermute | solution.py:379
  10.0 19.9 %collective-permute-start.1 = (bf16[128,1024]{1,0:T(8,128)(2,1)S(1)}, bf16[128,1024]{1,0:T(8,128)(2,1)S(1)}, u32[]{:S(2)}, u32[]{:S(2)}) collective-permute-start(bf16[128,1024]{1,0:T(8,128)(2,1)S(1)} %get-tuple-element.47), channel_id=1, source_target_pairs={{0,4},{4,0},{8,12},{12,8},{1,5},{5,1},{9,13},{13,9},{2,6},{6,2},{1... | collective-permute-start | bytes 786440 | tf_op jit(solution)/shard_map/ppermute | solution.py:379
  24.3 12.8 %collective-permute-start.6 = (bf16[64,1024]{1,0:T(8,128)(2,1)S(1)}, bf16[64,1024]{1,0:T(8,128)(2,1)S(1)}, u32[]{:S(2)}, u32[]{:S(2)}) collective-permute-start(bf16[64,1024]{1,0:T(8,128)(2,1)S(1)} %get-tuple-element.58), channel_id=1, source_target_pairs={{0,4},{4,0},{8,12},{12,8},{1,5},{5,1},{9,13},{13,9},{2,6},{6,2},{1... | collective-permute-start | bytes 393224 | tf_op jit(solution)/shard_map/ppermute | solution.py:379
  25.4 13.2 %collective-permute-start.7 = (bf16[64,1024]{1,0:T(8,128)(2,1)S(1)}, bf16[64,1024]{1,0:T(8,128)(2,1)S(1)}, u32[]{:S(2)}, u32[]{:S(2)}) collective-permute-start(bf16[64,1024]{1,0:T(8,128)(2,1)S(1)} %get-tuple-element.59), channel_id=1, source_target_pairs={{0,8},{4,12},{8,0},{12,4},{1,9},{5,13},{9,1},{13,5},{2,10},{6,14},... | collective-permute-start | bytes 393224 | tf_op jit(solution)/shard_map/ppermute | solution.py:379
  28.9 9.8 %collective-permute-start.8 = (bf16[64,1024]{1,0:T(8,128)(2,1)S(1)}, bf16[64,1024]{1,0:T(8,128)(2,1)S(1)}, u32[]{:S(2)}, u32[]{:S(2)}) collective-permute-start(bf16[64,1024]{1,0:T(8,128)(2,1)S(1)} %get-tuple-element.60), channel_id=1, source_target_pairs={{0,12},{4,8},{8,4},{12,0},{1,13},{5,9},{9,5},{13,1},{2,14},{6,10},... | collective-permute-start | bytes 393224 | tf_op jit(solution)/shard_map/ppermute | solution.py:379
  33.7 7.8 %collective-permute-start.3 = (bf16[64,1024]{1,0:T(8,128)(2,1)S(1)}, bf16[64,1024]{1,0:T(8,128)(2,1)S(1)}, u32[]{:S(2)}, u32[]{:S(2)}) collective-permute-start(bf16[64,1024]{1,0:T(8,128)(2,1)S(1)} %get-tuple-element.50), channel_id=1, source_target_pairs={{0,4},{4,0},{8,12},{12,8},{1,5},{5,1},{9,13},{13,9},{2,6},{6,2},{1... | collective-permute-start | bytes 393224 | tf_op jit(solution)/shard_map/ppermute | solution.py:379
  33.7 16.1 %collective-permute-start.4 = (bf16[64,1024]{1,0:T(8,128)(2,1)S(1)}, bf16[64,1024]{1,0:T(8,128)(2,1)S(1)}, u32[]{:S(2)}, u32[]{:S(2)}) collective-permute-start(bf16[64,1024]{1,0:T(8,128)(2,1)S(1)} %get-tuple-element.51), channel_id=1, source_target_pairs={{0,8},{4,12},{8,0},{12,4},{1,9},{5,13},{9,1},{13,5},{2,10},{6,14},... | collective-permute-start | bytes 393224 | tf_op jit(solution)/shard_map/ppermute | solution.py:379
  37.1 12.8 %collective-permute-start.5 = (bf16[64,1024]{1,0:T(8,128)(2,1)S(1)}, bf16[64,1024]{1,0:T(8,128)(2,1)S(1)}, u32[]{:S(2)}, u32[]{:S(2)}) collective-permute-start(bf16[64,1024]{1,0:T(8,128)(2,1)S(1)} %get-tuple-element.52), channel_id=1, source_target_pairs={{0,12},{4,8},{8,4},{12,0},{1,13},{5,9},{9,5},{13,1},{2,14},{6,10},... | collective-permute-start | bytes 393224 | tf_op jit(solution)/shard_map/ppermute | solution.py:379
  52.7 1.3 %collective-permute-start.9 = (bf16[4,64,128]{2,1,0:T(8,128)(2,1)S(1)}, bf16[4,64,128]{2,1,0:T(8,128)(2,1)S(1)}, u32[]{:S(2)}, u32[]{:S(2)}) collective-permute-start(bf16[4,64,128]{2,1,0:T(8,128)(2,1)S(1)} %get-tuple-element.62), channel_id=1, source_target_pairs={{0,1},{1,0},{2,3},{3,2},{4,5},{5,4},{6,7},{7,6},{8,9},{9,8},{10,11... | collective-permute-start | bytes 196616 | tf_op jit(solution)/shard_map/ppermute | solution.py:431
  54.1 5.9 %collective-permute-start.10 = (bf16[2,64,128]{2,1,0:T(8,128)(2,1)S(1)}, bf16[2,64,128]{2,1,0:T(8,128)(2,1)S(1)}, u32[]{:S(2)}, u32[]{:S(2)}) collective-permute-start(bf16[2,64,128]{2,1,0:T(8,128)(2,1)S(1)} %get-tuple-element.67), channel_id=1, source_target_pairs={{0,4},{4,0},{8,12},{12,8},{1,5},{5,1},{9,13},{13,9},{2,6},{6,2},{1... | collective-permute-start | bytes 98312 | tf_op jit(solution)/shard_map/ppermute | solution.py:379
  56.7 5.0 %collective-permute-start.11 = (bf16[2,64,128]{2,1,0:T(8,128)(2,1)S(1)}, bf16[2,64,128]{2,1,0:T(8,128)(2,1)S(1)}, u32[]{:S(2)}, u32[]{:S(2)}) collective-permute-start(bf16[2,64,128]{2,1,0:T(8,128)(2,1)S(1)} %get-tuple-element.68), channel_id=1, source_target_pairs={{0,8},{4,12},{8,0},{12,4},{1,9},{5,13},{9,1},{13,5},{2,10},{6,14},... | collective-permute-start | bytes 98312 | tf_op jit(solution)/shard_map/ppermute | solution.py:379
  58.6 5.7 %collective-permute-start.12 = (bf16[2,64,128]{2,1,0:T(8,128)(2,1)S(1)}, bf16[2,64,128]{2,1,0:T(8,128)(2,1)S(1)}, u32[]{:S(2)}, u32[]{:S(2)}) collective-permute-start(bf16[2,64,128]{2,1,0:T(8,128)(2,1)S(1)} %get-tuple-element.65), channel_id=1, source_target_pairs={{0,12},{4,8},{8,4},{12,0},{1,13},{5,9},{9,5},{13,1},{2,14},{6,10},... | collective-permute-start | bytes 98312 | tf_op jit(solution)/shard_map/ppermute | solution.py:379

commit v4 on v3

--- a/solution.py
+++ b/solution.py
@@ -281,7 +281,7 @@
 
 def place_kernel(piece_ref, *refs):
     *step_refs, out_ref, held_ref = refs
-    for step, ref in enumerate(step_refs):
+    for step, ref in enumerate(reversed(step_refs)):
         held_ref[2 * step : 2 * step + 2] = ref[...]
     pieces = held_ref.shape[0]
     cell = held_ref.shape[1] // NGRP
@@ -439,7 +439,7 @@
         scratch_shapes=[pltpu.VMEM((pieces, NGRP * own_channels, lag_count // pieces), jnp.bfloat16)],
         compiler_params=pltpu.CompilerParams(vmem_limit_bytes=8 * 1024 * 1024),
         name="place",
-    )(here, *arrived)
+    )(here, *reversed(arrived))
 
 
 def solution(mesh):

time: 65.5 us -> 63.7 us (0.973)
  waiting for transfers between devices: 19.6 us -> 17.3 us
  Pallas kernels: 14.2 us -> 16.2 us
  starting transfers between devices: 20.7 us -> 19.8 us
    ppermute x12, waiting for transfers between devices: 18.4 us -> 16 us  [move(): return lax.ppermute(value, 'pair', [(i, i ^ shift) for i in range(parts)])]
    pallas_call x3, Pallas kernels: 9.43 us -> 11.4 us  [stack_call(): pl.pallas_call(functools.partial(stack_kernel, len(received), cells, unit...]
    ppermute x12, starting transfers between devices: 20.6 us -> 19.7 us  [move(): return lax.ppermute(value, 'pair', [(i, i ^ shift) for i in range(parts)])]
  transfers between devices with their start and end apart: 13 -> 13, of which waited for: 6 -> 6; matrix products, arithmetic and copies ran while one was open for 10% -> 10% of each run, Pallas kernels for 15% -> 18%
where the time goes in v4:
time: 63.7 us
  starting transfers between devices  19.8 us (31%)
  waiting for transfers between devices  17.3 us (27%)
  Pallas kernels  16.2 us (25%)
  local copies, waits for them, and re-layouts  5.49 us (9%)
  between operations  2.83 us (4%)
  other arithmetic  2.19 us (3%)
    ppermute x12, starting transfers between devices, move(): return lax.ppermute(value, 'pair', [(i, i ^ shift) for i in range(parts)])  19.7 us
    ppermute x12, waiting for transfers between devices, move(): return lax.ppermute(value, 'pair', [(i, i ^ shift) for i in range(parts)])  16 us
    pallas_call x3, Pallas kernels, stack_call(): pl.pallas_call(functools.partial(stack_kernel, len(received), cells, unit...  11.4 us
    dynamic_slice x3, local copies, waits for them, and re-layouts, shards(): raw[step] = lax.dynamic_slice_in_dim(spectra, starts[step], own_channels, 2)  4.34 us
    pallas_call x3, Pallas kernels, shards(): pl.pallas_call(functools.partial(prepare_kernel, chunks, wanted), out_sha...  2.93 us
    another operation x4, other arithmetic  1.45 us
  transfers between devices with their start and end apart: 13, of which 6 were waited for; matrix products, arithmetic and copies ran while one was open for 10% of the time, Pallas kernels for 18%

profile of v4, /device:TPU:0, one launch (start us, length us, event | category | flops | bytes accessed | tf_op | source)
XLA Modules:
  0.0 63.7 jit_solution(2820086438224060617)
XLA Ops:
  0.0 1.1 %constant_dynamic-slice_fusion.3.refs_0_.refs_2_ = bf16[16,1,16,1024]{3,2,1,0:T(8,128)(2,1)S(1)} fusion(bf16[16,1,128,1024]{3,2,1,0:T(8,128)(2,1)} %param.4, s32[]{:T(128)S(6)} %select_n.51), kind=kLoop, calls=%fused_computation.50 | loop fusion | bytes 1048580 | tf_op jit(solution)/shard_map/dynamic_slice | solution.py:390
  1.1 0.6 prepare.3
  1.8 4.1 %collective-permute-start = (bf16[128,1024]{1,0:T(8,128)(2,1)S(1)}, bf16[128,1024]{1,0:T(8,128)(2,1)S(1)}, u32[]{:S(2)}, u32[]{:S(2)}) collective-permute-start(bf16[128,1024]{1,0:T(8,128)(2,1)S(1)} %prepare.3), channel_id=1, source_target_pairs={{0,8},{4,12},{8,0},{12,4},{1,9},{5,13},{9,1},{13,5},{2,10},{6,14},... | collective-permute-start | bytes 786440 | tf_op jit(solution)/shard_map/ppermute | solution.py:379
  5.9 1.9 %constant_dynamic-slice_fusion = (bf16[16,1,16,1024]{3,2,1,0:T(8,128)(2,1)S(1)}, bf16[16,1,16,1024]{3,2,1,0:T(8,128)(2,1)S(1)}) fusion(bf16[16,1,128,1024]{3,2,1,0:T(8,128)(2,1)} %param.4, s32[]{:T(128)S(6)} %select_n.57, s32[]{:T(128)S(6)} %select_n.56), kind=kLoop, calls=%fused_computation.47 | loop fusion | bytes 2097160 | tf_op jit(solution)/shard_map/dynamic_slice | solution.py:390
  7.7 0.9 %prepare.4 = (bf16[128,1024]{1,0:T(8,128)(2,1)S(1)}, bf16[128,1024]{1,0:T(8,128)(2,1)S(1)}) custom-call(bf16[16,1,16,1024]{3,2,1,0:T(8,128)(2,1)S(1)} %get-tuple-element.64.refs_0_.refs_3_, bf16[16,1,16,1024]{3,2,1,0:T(8,128)(2,1)S(1)} %get-tuple-element.63.refs_1_), custom_call_target="tpu_custom_call" | custom-call | tf_op jit(solution)/shard_map/prepare/pallas_call | solution.py:391
  8.6 1.4 %collective-permute-start.2 = (bf16[128,1024]{1,0:T(8,128)(2,1)S(1)}, bf16[128,1024]{1,0:T(8,128)(2,1)S(1)}, u32[]{:S(2)}, u32[]{:S(2)}) collective-permute-start(bf16[128,1024]{1,0:T(8,128)(2,1)S(1)} %get-tuple-element.49), channel_id=1, source_target_pairs={{0,12},{4,8},{8,4},{12,0},{1,13},{5,9},{9,5},{13,1},{2,14},{6,10},... | collective-permute-start | bytes 786440 | tf_op jit(solution)/shard_map/ppermute | solution.py:379
  10.0 0.3 collective-permute-start.1
  10.3 0.1 eq.40
  10.4 0.1 iota_compare_fusion.3
  10.5 0.1 lt.35
  10.6 0.1 convert_reduce_fusion
  10.7 0.2 reduce-window.10
  10.9 1.2 %reduce-window.11 = s32[4,2,128]{2,1,0:T(2,128)S(1)} reduce-window(s32[4,2,128]{2,1,0:T(2,128)S(1)} %reshape.172, s32[]{:T(128)} %constant.99.clone.1), window={size=1x1x128 pad=0_0x0_0x127_0}, to_apply=%region_2.3 | reduce-window | flops 130048 | bytes 8196 | tf_op jit(solution)/shard_map/reduce-window.1
  12.2 0.1 slice.36
  12.2 0.1 copy.10
  12.4 0.1 copy.11
  12.5 0.1 add_bitcast_fusion
  12.6 0.1 fusion.10
  12.7 0.1 iota_compare_fusion
  12.8 0.1 reshape.171
  12.9 0.1 select_reduce_fusion
  13.0 1.4 %constant_dynamic-slice_fusion.2.refs_0_ = bf16[16,1,16,1024]{3,2,1,0:T(8,128)(2,1)S(1)} fusion(bf16[16,1,128,1024]{3,2,1,0:T(8,128)(2,1)} %param.4, s32[]{:T(128)S(6)} %select_n.58), kind=kLoop, calls=%fused_computation.49 | loop fusion | bytes 1048580 | tf_op jit(solution)/shard_map/dynamic_slice | solution.py:390
  14.4 0.1 convert_reduce_fusion.1
  14.5 0.6 slice.27
  16.4 1.5 %prepare.5 = (bf16[128,1024]{1,0:T(8,128)(2,1)S(1)}, bf16[64,1024]{1,0:T(8,128)(2,1)S(1)}, bf16[64,1024]{1,0:T(8,128)(2,1)S(1)}, bf16[64,1024]{1,0:T(8,128)(2,1)...) custom-call(bf16[16,1,16,1024]{3,2,1,0:T(8,128)(2,1)S(1)} %constant_, ...), custom_call_target="tpu_custom_call" | custom-call | tf_op jit(solution)/shard_map/prepare/pallas_call | solution.py:391
  19.2 5.1 %collective-permute-done.refs_2_ = bf16[128,1024]{1,0:T(8,128)(2,1)S(1)} collective-permute-done((bf16[128,1024]{1,0:T(8,128)(2,1)S(1)}, bf16[128,1024]{1,0:T(8,128)(2,1)S(1)}, u32[]{:S(2)}, u32[]{:S(2)}) %collective-permute-start) | collective-permute-done | bytes 262176 | tf_op jit(solution)/shard_map/ppermute | solution.py:379
  24.3 1.1 %table.1.refs_4_ = bf16[1024,512]{1,0:T(8,128)(2,1)S(1)} custom-call(s32[1]{0:T(128)S(6)} %select_n.50.used_ref), custom_call_target="tpu_custom_call" | custom-call | tf_op jit(solution)/shard_map/table/pallas_call | solution.py:61
  25.4 3.4 %collective-permute-start.7 = (bf16[64,1024]{1,0:T(8,128)(2,1)S(1)}, bf16[64,1024]{1,0:T(8,128)(2,1)S(1)}, u32[]{:S(2)}, u32[]{:S(2)}) collective-permute-start(bf16[64,1024]{1,0:T(8,128)(2,1)S(1)} %get-tuple-element.59), channel_id=1, source_target_pairs={{0,8},{4,12},{8,0},{12,4},{1,9},{5,13},{9,1},{13,5},{2,10},{6,14},... | collective-permute-start | bytes 393224 | tf_op jit(solution)/shard_map/ppermute | solution.py:379
  28.9 1.0 %collective-permute-start.8 = (bf16[64,1024]{1,0:T(8,128)(2,1)S(1)}, bf16[64,1024]{1,0:T(8,128)(2,1)S(1)}, u32[]{:S(2)}, u32[]{:S(2)}) collective-permute-start(bf16[64,1024]{1,0:T(8,128)(2,1)S(1)} %get-tuple-element.60), channel_id=1, source_target_pairs={{0,12},{4,8},{8,4},{12,0},{1,13},{5,9},{9,5},{13,1},{2,14},{6,10},... | collective-permute-start | bytes 393224 | tf_op jit(solution)/shard_map/ppermute | solution.py:379
  29.9 0.0 collective-permute-done.2.refs_3_
  29.9 4.6 %stack.15.refs_6_ = f32[4,8,1024]{2,1,0:T(8,128)S(1)} custom-call(s32[1]{0:T(128)S(6)} %select_n.52.tiles_ref, s32[2,208]{1,0:T(2,128)S(1)} %broadcast_add_fusion.place_ref, s32[52]{0:T(128)S(1)} %broadcast_minimum_fusion.groups_ref, f32[4]{0:T(128)S(1)} %convert_rsqrt_fusion.norm_ref, bf16[128,1024]{1,0:T(8,128)(2,1)S(1)} %get-tuple-element.46.refs_0_, ...), custom_call_target="tpu_custom_call" | custom-call | tf_op jit(solution)/shard_map/stack/pallas_call | solution.py:368
  34.5 0.1 collective-permute-start.3
  34.6 3.4 %collective-permute-start.4 = (bf16[64,1024]{1,0:T(8,128)(2,1)S(1)}, bf16[64,1024]{1,0:T(8,128)(2,1)S(1)}, u32[]{:S(2)}, u32[]{:S(2)}) collective-permute-start(bf16[64,1024]{1,0:T(8,128)(2,1)S(1)} %get-tuple-element.51), channel_id=1, source_target_pairs={{0,8},{4,12},{8,0},{12,4},{1,9},{5,13},{9,1},{13,5},{2,10},{6,14},... | collective-permute-start | bytes 393224 | tf_op jit(solution)/shard_map/ppermute | solution.py:379
  37.9 0.0 collective-permute-done.6.refs_1_
  37.9 1.0 %collective-permute-start.5 = (bf16[64,1024]{1,0:T(8,128)(2,1)S(1)}, bf16[64,1024]{1,0:T(8,128)(2,1)S(1)}, u32[]{:S(2)}, u32[]{:S(2)}) collective-permute-start(bf16[64,1024]{1,0:T(8,128)(2,1)S(1)} %get-tuple-element.52), channel_id=1, source_target_pairs={{0,12},{4,8},{8,4},{12,0},{1,13},{5,9},{9,5},{13,1},{2,14},{6,10},... | collective-permute-start | bytes 393224 | tf_op jit(solution)/shard_map/ppermute | solution.py:379
  39.0 0.0 collective-permute-done.8.refs_3_
  39.0 3.4 %stack.16.refs_7_ = f32[4,4,1024]{2,1,0:T(4,128)S(1)} custom-call(s32[1]{0:T(128)S(6)} %select_n.52.tiles_ref, s32[2,208]{1,0:T(2,128)S(1)} %broadcast_add_fusion.place_ref, s32[52]{0:T(128)S(1)} %broadcast_minimum_fusion.groups_ref, f32[4]{0:T(128)S(1)} %convert_rsqrt_fusion.norm_ref, bf16[64,1024]{1,0:T(8,128)(2,1)S(1)} %get-tuple-element.54.refs_0_, ...), custom_call_target="tpu_custom_call" | custom-call | tf_op jit(solution)/shard_map/stack/pallas_call | solution.py:368
  42.3 7.5 %collective-permute-done.4.refs_2_ = bf16[64,1024]{1,0:T(8,128)(2,1)S(1)} collective-permute-done((bf16[64,1024]{1,0:T(8,128)(2,1)S(1)}, bf16[64,1024]{1,0:T(8,128)(2,1)S(1)}, u32[]{:S(2)}, u32[]{:S(2)}) %collective-permute-start.4) | collective-permute-done | bytes 131104 | tf_op jit(solution)/shard_map/ppermute | solution.py:379
  49.8 3.4 %stack.17 = (bf16[4,64,128]{2,1,0:T(8,128)(2,1)S(1)}, bf16[4,64,128]{2,1,0:T(8,128)(2,1)S(1)}) custom-call(s32[1]{0:T(128)S(6)} %select_n.52.tiles_ref, s32[2,208]{1,0:T(2,128)S(1)} %broadcast_add_fusion.place_ref, s32[52]{0:T(128)S(1)} %broadcast_minimum_fusion.groups_ref, f32[4]{0:T(128)S(1)} %convert_rsqrt_fusion.norm_ref, ...), custom_call_target="tpu_custom_call" | custom-call | tf_op jit(solution)/shard_map/stack/pallas_call | solution.py:368
  53.2 0.1 collective-permute-start.9
  53.3 1.2 %collective-permute-done.9 = bf16[4,64,128]{2,1,0:T(8,128)(2,1)S(1)} collective-permute-done((bf16[4,64,128]{2,1,0:T(8,128)(2,1)S(1)}, bf16[4,64,128]{2,1,0:T(8,128)(2,1)S(1)}, u32[]{:S(2)}, u32[]{:S(2)}) %collective-permute-start.9) | collective-permute-done | bytes 65568 | tf_op jit(solution)/shard_map/ppermute | solution.py:431
  54.6 2.8 %collective-permute-start.10 = (bf16[2,64,128]{2,1,0:T(8,128)(2,1)S(1)}, bf16[2,64,128]{2,1,0:T(8,128)(2,1)S(1)}, u32[]{:S(2)}, u32[]{:S(2)}) collective-permute-start(bf16[2,64,128]{2,1,0:T(8,128)(2,1)S(1)} %get-tuple-element.66), channel_id=1, source_target_pairs={{0,12},{4,8},{8,4},{12,0},{1,13},{5,9},{9,5},{13,1},{2,14},{6,10},... | collective-permute-start | bytes 98312 | tf_op jit(solution)/shard_map/ppermute | solution.py:379
  57.3 1.8 %collective-permute-start.11 = (bf16[2,64,128]{2,1,0:T(8,128)(2,1)S(1)}, bf16[2,64,128]{2,1,0:T(8,128)(2,1)S(1)}, u32[]{:S(2)}, u32[]{:S(2)}) collective-permute-start(bf16[2,64,128]{2,1,0:T(8,128)(2,1)S(1)} %get-tuple-element.67), channel_id=1, source_target_pairs={{0,8},{4,12},{8,0},{12,4},{1,9},{5,13},{9,1},{13,5},{2,10},{6,14},... | collective-permute-start | bytes 98312 | tf_op jit(solution)/shard_map/ppermute | solution.py:379
  59.1 0.5 collective-permute-start.12
  59.6 0.8 %collective-permute-done.10.refs_0_ = bf16[2,64,128]{2,1,0:T(8,128)(2,1)S(1)} collective-permute-done((bf16[2,64,128]{2,1,0:T(8,128)(2,1)S(1)}, bf16[2,64,128]{2,1,0:T(8,128)(2,1)S(1)}, u32[]{:S(2)}, u32[]{:S(2)}) %collective-permute-start.10) | collective-permute-done | bytes 32800 | tf_op jit(solution)/shard_map/ppermute | solution.py:379
  60.4 1.9 %collective-permute-done.11.refs_1_ = bf16[2,64,128]{2,1,0:T(8,128)(2,1)S(1)} collective-permute-done((bf16[2,64,128]{2,1,0:T(8,128)(2,1)S(1)}, bf16[2,64,128]{2,1,0:T(8,128)(2,1)S(1)}, u32[]{:S(2)}, u32[]{:S(2)}) %collective-permute-start.11) | collective-permute-done | bytes 32800 | tf_op jit(solution)/shard_map/ppermute | solution.py:379
  62.3 0.7 %collective-permute-done.12.refs_2_ = bf16[2,64,128]{2,1,0:T(8,128)(2,1)S(1)} collective-permute-done((bf16[2,64,128]{2,1,0:T(8,128)(2,1)S(1)}, bf16[2,64,128]{2,1,0:T(8,128)(2,1)S(1)}, u32[]{:S(2)}, u32[]{:S(2)}) %collective-permute-start.12) | collective-permute-done | bytes 32800 | tf_op jit(solution)/shard_map/ppermute | solution.py:379
  63.0 0.7 %place.1 = f32[4,128,128]{2,1,0:T(8,128)} custom-call(s32[1]{0:T(128)} %bitcast.refs_5_.piece_ref, bf16[2,64,128]{2,1,0:T(8,128)(2,1)S(1)} %collective-permute-done.10.refs_0_, bf16[2,64,128]{2,1,0:T(8,128)(2,1)S(1)} %collective-permute-done.11.refs_1_, bf16[2,64,128]{2,1,0:T(8,128)(2,1)S(1)} %collective-permute-done.12.refs_2_, ...), custom_call_target="tpu_custom_call" | custom-call | tf_op jit(solution)/shard_map/place/pallas_call | solution.py:434
  (27 shorter events, 0.2 us)
Async XLA Ops:
  0.0 10.3 %copy-start.1 = (s32[4,40]{1,0:T(4,128)S(1)}, s32[4,40]{1,0:T(4,128)}, u32[]{:S(2)}) copy-start(s32[4,40]{1,0:T(4,128)} %param.7) | copy-start | bytes 1924
  0.0 10.4 %copy-start.2 = (s32[4]{0:T(128)S(1)}, s32[4]{0:T(128)}, u32[]{:S(2)}) copy-start(s32[4]{0:T(128)} %param.6) | copy-start | bytes 52
  0.0 12.8 %copy-start = (s32[4,40,2]{1,2,0:T(2,128)S(1)}, s32[4,40,2]{1,2,0:T(2,128)}, u32[]{:S(2)}) copy-start(s32[4,40,2]{1,2,0:T(2,128)} %param.5) | copy-start | bytes 3844
  1.8 22.5 %collective-permute-start = (bf16[128,1024]{1,0:T(8,128)(2,1)S(1)}, bf16[128,1024]{1,0:T(8,128)(2,1)S(1)}, u32[]{:S(2)}, u32[]{:S(2)}) collective-permute-start(bf16[128,1024]{1,0:T(8,128)(2,1)S(1)} %prepare.3), channel_id=1, source_target_pairs={{0,8},{4,12},{8,0},{12,4},{1,9},{5,13},{9,1},{13,5},{2,10},{6,14},... | collective-permute-start | bytes 786440 | tf_op jit(solution)/shard_map/ppermute | solution.py:379
  8.6 21.3 %collective-permute-start.2 = (bf16[128,1024]{1,0:T(8,128)(2,1)S(1)}, bf16[128,1024]{1,0:T(8,128)(2,1)S(1)}, u32[]{:S(2)}, u32[]{:S(2)}) collective-permute-start(bf16[128,1024]{1,0:T(8,128)(2,1)S(1)} %get-tuple-element.49), channel_id=1, source_target_pairs={{0,12},{4,8},{8,4},{12,0},{1,13},{5,9},{9,5},{13,1},{2,14},{6,10},... | collective-permute-start | bytes 786440 | tf_op jit(solution)/shard_map/ppermute | solution.py:379
  10.0 19.9 %collective-permute-start.1 = (bf16[128,1024]{1,0:T(8,128)(2,1)S(1)}, bf16[128,1024]{1,0:T(8,128)(2,1)S(1)}, u32[]{:S(2)}, u32[]{:S(2)}) collective-permute-start(bf16[128,1024]{1,0:T(8,128)(2,1)S(1)} %get-tuple-element.47), channel_id=1, source_target_pairs={{0,4},{4,0},{8,12},{12,8},{1,5},{5,1},{9,13},{13,9},{2,6},{6,2},{1... | collective-permute-start | bytes 786440 | tf_op jit(solution)/shard_map/ppermute | solution.py:379
  24.3 13.7 %collective-permute-start.6 = (bf16[64,1024]{1,0:T(8,128)(2,1)S(1)}, bf16[64,1024]{1,0:T(8,128)(2,1)S(1)}, u32[]{:S(2)}, u32[]{:S(2)}) collective-permute-start(bf16[64,1024]{1,0:T(8,128)(2,1)S(1)} %get-tuple-element.58), channel_id=1, source_target_pairs={{0,4},{4,0},{8,12},{12,8},{1,5},{5,1},{9,13},{13,9},{2,6},{6,2},{1... | collective-permute-start | bytes 393224 | tf_op jit(solution)/shard_map/ppermute | solution.py:379
  25.4 13.5 %collective-permute-start.7 = (bf16[64,1024]{1,0:T(8,128)(2,1)S(1)}, bf16[64,1024]{1,0:T(8,128)(2,1)S(1)}, u32[]{:S(2)}, u32[]{:S(2)}) collective-permute-start(bf16[64,1024]{1,0:T(8,128)(2,1)S(1)} %get-tuple-element.59), channel_id=1, source_target_pairs={{0,8},{4,12},{8,0},{12,4},{1,9},{5,13},{9,1},{13,5},{2,10},{6,14},... | collective-permute-start | bytes 393224 | tf_op jit(solution)/shard_map/ppermute | solution.py:379
  28.9 10.1 %collective-permute-start.8 = (bf16[64,1024]{1,0:T(8,128)(2,1)S(1)}, bf16[64,1024]{1,0:T(8,128)(2,1)S(1)}, u32[]{:S(2)}, u32[]{:S(2)}) collective-permute-start(bf16[64,1024]{1,0:T(8,128)(2,1)S(1)} %get-tuple-element.60), channel_id=1, source_target_pairs={{0,12},{4,8},{8,4},{12,0},{1,13},{5,9},{9,5},{13,1},{2,14},{6,10},... | collective-permute-start | bytes 393224 | tf_op jit(solution)/shard_map/ppermute | solution.py:379
  34.5 7.8 %collective-permute-start.3 = (bf16[64,1024]{1,0:T(8,128)(2,1)S(1)}, bf16[64,1024]{1,0:T(8,128)(2,1)S(1)}, u32[]{:S(2)}, u32[]{:S(2)}) collective-permute-start(bf16[64,1024]{1,0:T(8,128)(2,1)S(1)} %get-tuple-element.50), channel_id=1, source_target_pairs={{0,4},{4,0},{8,12},{12,8},{1,5},{5,1},{9,13},{13,9},{2,6},{6,2},{1... | collective-permute-start | bytes 393224 | tf_op jit(solution)/shard_map/ppermute | solution.py:379
  34.6 15.3 %collective-permute-start.4 = (bf16[64,1024]{1,0:T(8,128)(2,1)S(1)}, bf16[64,1024]{1,0:T(8,128)(2,1)S(1)}, u32[]{:S(2)}, u32[]{:S(2)}) collective-permute-start(bf16[64,1024]{1,0:T(8,128)(2,1)S(1)} %get-tuple-element.51), channel_id=1, source_target_pairs={{0,8},{4,12},{8,0},{12,4},{1,9},{5,13},{9,1},{13,5},{2,10},{6,14},... | collective-permute-start | bytes 393224 | tf_op jit(solution)/shard_map/ppermute | solution.py:379
  37.9 11.9 %collective-permute-start.5 = (bf16[64,1024]{1,0:T(8,128)(2,1)S(1)}, bf16[64,1024]{1,0:T(8,128)(2,1)S(1)}, u32[]{:S(2)}, u32[]{:S(2)}) collective-permute-start(bf16[64,1024]{1,0:T(8,128)(2,1)S(1)} %get-tuple-element.52), channel_id=1, source_target_pairs={{0,12},{4,8},{8,4},{12,0},{1,13},{5,9},{9,5},{13,1},{2,14},{6,10},... | collective-permute-start | bytes 393224 | tf_op jit(solution)/shard_map/ppermute | solution.py:379
  53.2 1.3 %collective-permute-start.9 = (bf16[4,64,128]{2,1,0:T(8,128)(2,1)S(1)}, bf16[4,64,128]{2,1,0:T(8,128)(2,1)S(1)}, u32[]{:S(2)}, u32[]{:S(2)}) collective-permute-start(bf16[4,64,128]{2,1,0:T(8,128)(2,1)S(1)} %get-tuple-element.62), channel_id=1, source_target_pairs={{0,1},{1,0},{2,3},{3,2},{4,5},{5,4},{6,7},{7,6},{8,9},{9,8},{10,11... | collective-permute-start | bytes 196616 | tf_op jit(solution)/shard_map/ppermute | solution.py:431
  54.6 5.8 %collective-permute-start.10 = (bf16[2,64,128]{2,1,0:T(8,128)(2,1)S(1)}, bf16[2,64,128]{2,1,0:T(8,128)(2,1)S(1)}, u32[]{:S(2)}, u32[]{:S(2)}) collective-permute-start(bf16[2,64,128]{2,1,0:T(8,128)(2,1)S(1)} %get-tuple-element.66), channel_id=1, source_target_pairs={{0,12},{4,8},{8,4},{12,0},{1,13},{5,9},{9,5},{13,1},{2,14},{6,10},... | collective-permute-start | bytes 98312 | tf_op jit(solution)/shard_map/ppermute | solution.py:379
  57.3 4.9 %collective-permute-start.11 = (bf16[2,64,128]{2,1,0:T(8,128)(2,1)S(1)}, bf16[2,64,128]{2,1,0:T(8,128)(2,1)S(1)}, u32[]{:S(2)}, u32[]{:S(2)}) collective-permute-start(bf16[2,64,128]{2,1,0:T(8,128)(2,1)S(1)} %get-tuple-element.67), channel_id=1, source_target_pairs={{0,8},{4,12},{8,0},{12,4},{1,9},{5,13},{9,1},{13,5},{2,10},{6,14},... | collective-permute-start | bytes 98312 | tf_op jit(solution)/shard_map/ppermute | solution.py:379
  59.1 3.9 %collective-permute-start.12 = (bf16[2,64,128]{2,1,0:T(8,128)(2,1)S(1)}, bf16[2,64,128]{2,1,0:T(8,128)(2,1)S(1)}, u32[]{:S(2)}, u32[]{:S(2)}) collective-permute-start(bf16[2,64,128]{2,1,0:T(8,128)(2,1)S(1)} %get-tuple-element.68), channel_id=1, source_target_pairs={{0,4},{4,0},{8,12},{12,8},{1,5},{5,1},{9,13},{13,9},{2,6},{6,2},{1... | collective-permute-start | bytes 98312 | tf_op jit(solution)/shard_map/ppermute | solution.py:379

commit v5 on v4

--- a/solution.py
+++ b/solution.py
@@ -74,40 +74,53 @@
     return (values * lax.rsqrt(power + EPSILON)).astype(jnp.bfloat16)
 
 
-def prepare_kernel(chunks, wanted, *refs):
-    order = list(dict.fromkeys(step for step, _ in wanted))
-    raw_refs = dict(zip(order, refs))
-    out_refs = dict(zip(wanted, refs[len(order) :]))
-    blocks, _, own_channels, width = refs[0].shape
+def prepare_kernel(cells_of, *refs):
+    in_refs = refs[: len(cells_of)]
+    out_refs = list(refs[len(cells_of) :])
+    rows, width = in_refs[0].shape
     num_bins = width // 2
     class_bins = num_bins // CLASSES
     source = lax.broadcasted_iota(jnp.int32, (num_bins, num_bins), 0)
     target = lax.broadcasted_iota(jnp.int32, (num_bins, num_bins), 1)
     moved = (target & (class_bins - 1)) * CLASSES + target // class_bins
     shuffle = jnp.where(source == moved, 1.0, 0.0).astype(jnp.bfloat16)
-    for step in order:
-        white = whiten(raw_refs[step][...].reshape(blocks * own_channels, width))
-        halves = [
-            jnp.dot(white[:, start : start + num_bins], shuffle, preferred_element_type=jnp.float32)
-            for start in (0, num_bins)
-        ]
-        halves = [half.reshape(blocks, own_channels, num_bins) for half in halves]
-        offset = 0
-        for index, cells in enumerate(chunks):
-            if (step, index) not in out_refs:
-                offset += sum(cells)
+    for in_ref, cells in zip(in_refs, cells_of):
+        white = whiten(in_ref[...])
+        cell_refs = [out_refs.pop(0) for _ in cells]
+        for start in (0, num_bins):
+            half = jnp.dot(white[:, start : start + num_bins], shuffle, preferred_element_type=jnp.float32)
+            bins = slice(start, start + num_bins)
+            if len(cells) == 1:
+                cell_refs[0][:, bins] = half.astype(jnp.bfloat16)
                 continue
-            out_ref = out_refs[step, index]
-            row = 0
-            for cell in cells:
-                group = SUB_ROWS // cell
-                for block in range(0, blocks, 2 * group):
-                    for side, half in enumerate(halves):
-                        rows = [half[block + k, offset : offset + cell] for k in range(2 * group)]
-                        rows = jnp.concatenate(rows, axis=0).astype(jnp.bfloat16)
-                        out_ref[row : row + PACK_ROWS, side * num_bins : (side + 1) * num_bins] = rows
-                    row += PACK_ROWS
+            half = half.reshape(rows // SUB_ROWS, SUB_ROWS, num_bins)
+            offset = 0
+            for cell, out_ref in zip(cells, cell_refs):
+                blocks = PACK_ROWS // cell
+                for first in range(0, rows // SUB_ROWS, blocks):
+                    pack = [half[first + k, offset : offset + cell] for k in range(blocks)]
+                    out_ref[first * cell : first * cell + PACK_ROWS, bins] = jnp.concatenate(pack, axis=0).astype(
+                        jnp.bfloat16
+                    )
                 offset += cell
+
+
+def prepare(pieces, cells_of):
+    rows, width = pieces[0].shape
+    vmem = pl.BlockSpec(memory_space=pltpu.VMEM)
+    shapes = [
+        jax.ShapeDtypeStruct((rows // SUB_ROWS * cell, width), jnp.bfloat16) for cells in cells_of for cell in cells
+    ]
+    return list(
+        pl.pallas_call(
+            functools.partial(prepare_kernel, cells_of),
+            out_shape=shapes,
+            in_specs=[vmem] * len(pieces),
+            out_specs=[vmem] * len(shapes),
+            compiler_params=pltpu.CompilerParams(vmem_limit_bytes=16 * 1024 * 1024),
+            name="prepare",
+        )(*pieces)
+    )
 
 
 def window_sum(values):
@@ -380,29 +393,23 @@
 
     starts = [((me ^ step) * cores + core) * own_channels for step in range(parts)]
     if len(chunks) > 1:
+        def raw(step, half):
+            start = starts[step] + half * SUB_ROWS
+            piece = lax.dynamic_slice_in_dim(spectra, start, SUB_ROWS, 2)
+            return piece.reshape(part_blocks * SUB_ROWS, width)
+
         pieces_of = [[None] * parts for _ in chunks]
-        raw = {}
-        calls = [[(2, 0)], [(3, 0), (1, 0)], [(0, 0)] + [(step, index) for index in range(1, len(chunks)) for step in range(parts)]]
-        for wanted in calls:
-            steps = list(dict.fromkeys(step for step, _ in wanted))
-            for step in steps:
-                if step not in raw:
-                    raw[step] = lax.dynamic_slice_in_dim(spectra, starts[step], own_channels, 2)
-            flat = pl.pallas_call(
-                functools.partial(prepare_kernel, chunks, wanted),
-                out_shape=[
-                    jax.ShapeDtypeStruct((part_blocks * sum(chunks[index]), width), jnp.bfloat16)
-                    for _, index in wanted
-                ],
-                in_specs=[pl.BlockSpec(memory_space=pltpu.VMEM)] * len(steps),
-                out_specs=[pl.BlockSpec(memory_space=pltpu.VMEM)] * len(wanted),
-                compiler_params=pltpu.CompilerParams(vmem_limit_bytes=16 * 1024 * 1024),
-                name="prepare",
-            )(*[raw[step] for step in steps])
-            flat = list(flat)
-            flat[0], starts = lax.optimization_barrier((flat[0], starts))
-            for (step, index), piece in zip(wanted, flat):
-                pieces_of[index][step] = piece
+        pieces_of[0][2] = raw(2, 0)
+        pieces_of[0][2], starts = lax.optimization_barrier((pieces_of[0][2], starts))
+        flat = prepare([raw(3, 0), raw(1, 0)], [[SUB_ROWS]] * 2)
+        flat, starts = lax.optimization_barrier((flat, starts))
+        pieces_of[0][3], pieces_of[0][1] = flat
+        later = [cell for cells in chunks[1:] for cell in cells]
+        flat = prepare([raw(0, 0)] + [raw(step, 1) for step in range(parts)], [[SUB_ROWS]] + [later] * parts)
+        pieces_of[0][0] = flat.pop(0)
+        for step in range(parts):
+            for index in range(1, len(chunks)):
+                pieces_of[index][step] = flat.pop(0)
     else:
         ordered = whiten(spectra).reshape(part_blocks, channels, 2, num_bins // CLASSES, CLASSES)
         ordered = ordered.swapaxes(3, 4).reshape(part_blocks, channels, width)
@@ -414,14 +421,23 @@
     received, done = [], []
     for index, (cells, units, chunk) in enumerate(zip(chunks, tile_units, pieces_of)):
         if index == 1:
-            chunk[1:], received[0][2] = lax.optimization_barrier((chunk[1:], received[0][2]))
+            chunk[1:], first_arrived = lax.optimization_barrier((chunk[1:], first_arrived))
+            chunk[1], table, received[0][2] = lax.optimization_barrier((chunk[1], table, received[0][2]))
         if index > 1:
-            chunk[1:], done[index - 2] = lax.optimization_barrier((chunk[1:], done[index - 2]))
-        received.append([chunk[0]] + [move(chunk[step], step) for step in range(1, parts)])
+            chunk[1:], received[0][3] = lax.optimization_barrier((chunk[1:], received[0][3]))
+        got = [chunk[0]] + [None] * (parts - 1)
+        for step in sorted(range(1, parts), reverse=index == 0):
+            if index == 0 and step == 1 and len(chunks) > 1:
+                chunk[1], pieces_of[1][0] = lax.optimization_barrier((chunk[1], pieces_of[1][0]))
+            got[step] = move(chunk[step], step)
+        received.append(got)
         if index == 0:
             if parts > 2:
                 used, received[0][2] = lax.optimization_barrier((used, received[0][2]))
+                first_arrived = received[0][2]
             table = lag_table(used, lag_count, num_bins)
+            if len(chunks) > 1:
+                received[0][2] = prepare([received[0][2]], [[SUB_ROWS]])[0]
         if len(chunks) == 1:
             return lax.all_to_all(stack_call(cells, units, received[0], []), ("pair", "lag"), 2, 1, tiled=True)
         if index < len(chunks) - 1:

time: 63.7 us -> 62.9 us (0.987)
  waiting for transfers between devices: 17.3 us -> 8.07 us
  starting transfers between devices: 19.8 us -> 28.8 us
  Pallas kernels: 16.2 us -> 15.2 us
    ppermute x12, waiting for transfers between devices: 16 us -> 6.83 us  [move(): return lax.ppermute(value, 'pair', [(i, i ^ shift) for i in range(parts)])]
    ppermute x12, starting transfers between devices: 19.7 us -> 28.8 us  [move(): return lax.ppermute(value, 'pair', [(i, i ^ shift) for i in range(parts)])]
    reshape x0 -> x3, local copies, waits for them, and re-layouts: none -> 4.67 us  [raw(): return piece.reshape(part_blocks * SUB_ROWS, width)]
    dynamic_slice x3 -> x0, local copies, waits for them, and re-layouts: 4.34 us -> none  [shards(): raw[step] = lax.dynamic_slice_in_dim(spectra, starts[step], own_channels, 2)]
    pallas_call x3, Pallas kernels: 2.93 us -> 2.1 us  [prepare(): pl.pallas_call(functools.partial(prepare_kernel, cells_of), out_shape=sha...]
  transfers between devices with their start and end apart: 13 -> 13, of which waited for: 6 -> 6; matrix products, arithmetic and copies ran while one was open for 10% -> 11% of each run, Pallas kernels for 18% -> 18%
where the time goes in v5:
time: 62.9 us
  starting transfers between devices  28.8 us (46%)
  Pallas kernels  15.2 us (24%)
  waiting for transfers between devices  8.07 us (13%)
  local copies, waits for them, and re-layouts  5.81 us (9%)
  between operations  2.82 us (4%)
  other arithmetic  2.19 us (3%)
    ppermute x12, starting transfers between devices, move(): return lax.ppermute(value, 'pair', [(i, i ^ shift) for i in range(parts)])  28.8 us
    pallas_call x3, Pallas kernels, stack_call(): pl.pallas_call(functools.partial(stack_kernel, len(received), cells, unit...  11.2 us
    ppermute x12, waiting for transfers between devices, move(): return lax.ppermute(value, 'pair', [(i, i ^ shift) for i in range(parts)])  6.83 us
    reshape x3, local copies, waits for them, and re-layouts, raw(): return piece.reshape(part_blocks * SUB_ROWS, width)  4.67 us
    pallas_call x3, Pallas kernels, prepare(): pl.pallas_call(functools.partial(prepare_kernel, cells_of), out_shape=sha...  2.1 us
    another operation x4, other arithmetic  1.45 us
  transfers between devices with their start and end apart: 13, of which 6 were waited for; matrix products, arithmetic and copies ran while one was open for 11% of the time, Pallas kernels for 18%

profile of v5, /device:TPU:0, one launch (start us, length us, event | category | flops | bytes accessed | tf_op | source)
XLA Modules:
  0.0 62.9 jit_solution(2572656854039663440)
XLA Ops:
  0.0 1.0 %dynamic-slice_bitcast_fusion.7 = bf16[128,1024]{1,0:T(8,128)(2,1)S(1)} fusion(bf16[16,1,128,1024]{3,2,1,0:T(8,128)(2,1)} %param.4, s32[]{:T(128)S(6)} %select_n.63), kind=kLoop, calls=%fused_computation.8 | loop fusion | bytes 524292 | tf_op jit(solution)/shard_map/reshape | solution.py:399
  1.0 4.1 %collective-permute-start = (bf16[128,1024]{1,0:T(8,128)(2,1)S(1)}, bf16[128,1024]{1,0:T(8,128)(2,1)S(1)}, u32[]{:S(2)}, u32[]{:S(2)}) collective-permute-start(bf16[128,1024]{1,0:T(8,128)(2,1)S(1)} %dynamic-slice_bitcast_fusion.7), channel_id=1, source_target_pairs={{0,8},{4,12},{8,0},{12,4},{1,9},{5,13},{9,1},{13,5},{2,10},{6,14},... | collective-permute-start | bytes 786440 | tf_op jit(solution)/shard_map/ppermute | solution.py:392
  5.1 1.4 %dynamic-slice_bitcast_fusion.5 = (bf16[128,1024]{1,0:T(8,128)(2,1)S(1)}, bf16[128,1024]{1,0:T(8,128)(2,1)S(1)}) fusion(bf16[16,1,128,1024]{3,2,1,0:T(8,128)(2,1)} %param.4, s32[]{:T(128)S(6)} %select_n.69, s32[]{:T(128)S(6)} %select_n.68), kind=kLoop, calls=%fused_computation.6 | loop fusion | bytes 1048584 | tf_op jit(solution)/shard_map/reshape | solution.py:399
  6.5 0.6 prepare.3
  7.1 2.3 %dynamic-slice_bitcast_fusion = (bf16[128,1024]{1,0:T(8,128)(2,1)S(1)}, bf16[128,1024]{1,0:T(8,128)(2,1)S(1)}, bf16[128,1024]{1,0:T(8,128)(2,1)S(1)}, bf16[128,1024]{1,0:T(8,128)(2,1)S(1)}, bf16[128,1024]{1,0:T(8,128)(2,1)S(1)}) fusion(bf16[16,1,128,1024]{3,2,1,0:T(8,128)(2,1)} %param.4, s32[]{:T(128)S(6)} %select_n.74, s32[]{:T(128)S(6)} %select_n.72, ...), kind=kLoop, calls=%fused_computation.1 | loop fusion | bytes 2621460 | tf_op jit(solution)/shard_map/reshape | solution.py:399
  9.4 1.1 %prepare.4 = (bf16[128,1024]{1,0:T(8,128)(2,1)S(1)}, bf16[64,1024]{1,0:T(8,128)(2,1)S(1)}, bf16[64,1024]{1,0:T(8,128)(2,1)S(1)}, bf16[64,1024]{1,0:T(8,128)(2,1)...) custom-call(bf16[128,1024]{1,0:T(8,128)(2,1)S(1)} %get-tuple-element, ...), custom_call_target="tpu_custom_call" | custom-call | tf_op jit(solution)/shard_map/prepare/pallas_call | solution.py:115
  10.5 1.6 %collective-permute-start.5 = (bf16[128,1024]{1,0:T(8,128)(2,1)S(1)}, bf16[128,1024]{1,0:T(8,128)(2,1)S(1)}, u32[]{:S(2)}, u32[]{:S(2)}) collective-permute-start(bf16[128,1024]{1,0:T(8,128)(2,1)S(1)} %get-tuple-element.70), channel_id=1, source_target_pairs={{0,4},{4,0},{8,12},{12,8},{1,5},{5,1},{9,13},{13,9},{2,6},{6,2},{1... | collective-permute-start | bytes 786440 | tf_op jit(solution)/shard_map/ppermute | solution.py:392
  12.1 0.0 collective-permute-start.1
  12.1 0.1 eq.40
  12.2 0.1 iota_compare_fusion.3
  12.3 0.1 lt.47
  12.4 0.1 convert_reduce_fusion
  12.5 0.2 reduce-window.10
  12.7 1.2 %reduce-window.11 = s32[4,2,128]{2,1,0:T(2,128)S(1)} reduce-window(s32[4,2,128]{2,1,0:T(2,128)S(1)} %reshape.204, s32[]{:T(128)} %constant.103.clone.1), window={size=1x1x128 pad=0_0x0_0x127_0}, to_apply=%region_2.3 | reduce-window | flops 130048 | bytes 8196 | tf_op jit(solution)/shard_map/reduce-window.1
  14.0 0.1 slice.36
  14.0 0.1 copy.10
  14.2 0.1 copy.11
  14.3 0.1 add_bitcast_fusion
  14.4 0.1 fusion.10
  14.5 0.1 iota_compare_fusion
  14.6 0.1 reshape.196
  14.7 0.1 select_reduce_fusion
  14.8 0.6 slice.27
  18.0 0.7 %collective-permute-done.refs_0_ = bf16[128,1024]{1,0:T(8,128)(2,1)S(1)} collective-permute-done((bf16[128,1024]{1,0:T(8,128)(2,1)S(1)}, bf16[128,1024]{1,0:T(8,128)(2,1)S(1)}, u32[]{:S(2)}, u32[]{:S(2)}) %collective-permute-start) | collective-permute-done | bytes 262176 | tf_op jit(solution)/shard_map/ppermute | solution.py:392
  18.8 0.4 prepare.5.refs_2_
  19.2 1.1 %table.1.refs_4_ = bf16[1024,512]{1,0:T(8,128)(2,1)S(1)} custom-call(s32[1]{0:T(128)S(6)} %select_n.62.used_ref), custom_call_target="tpu_custom_call" | custom-call | tf_op jit(solution)/shard_map/table/pallas_call | solution.py:61
  20.4 0.2 collective-permute-start.6
  20.6 0.1 convert_reduce_fusion.1
  20.7 3.5 %collective-permute-start.7 = (bf16[64,1024]{1,0:T(8,128)(2,1)S(1)}, bf16[64,1024]{1,0:T(8,128)(2,1)S(1)}, u32[]{:S(2)}, u32[]{:S(2)}) collective-permute-start(bf16[64,1024]{1,0:T(8,128)(2,1)S(1)} %get-tuple-element.73), channel_id=1, source_target_pairs={{0,8},{4,12},{8,0},{12,4},{1,9},{5,13},{9,1},{13,5},{2,10},{6,14},... | collective-permute-start | bytes 393224 | tf_op jit(solution)/shard_map/ppermute | solution.py:392
  24.2 0.7 %collective-permute-start.8 = (bf16[64,1024]{1,0:T(8,128)(2,1)S(1)}, bf16[64,1024]{1,0:T(8,128)(2,1)S(1)}, u32[]{:S(2)}, u32[]{:S(2)}) collective-permute-start(bf16[64,1024]{1,0:T(8,128)(2,1)S(1)} %get-tuple-element.74), channel_id=1, source_target_pairs={{0,12},{4,8},{8,4},{12,0},{1,13},{5,9},{9,5},{13,1},{2,14},{6,10},... | collective-permute-start | bytes 393224 | tf_op jit(solution)/shard_map/ppermute | solution.py:392
  24.9 0.0 collective-permute-done.1.refs_3_
  24.9 10.4 %collective-permute-start.2 = (bf16[64,1024]{1,0:T(8,128)(2,1)S(1)}, bf16[64,1024]{1,0:T(8,128)(2,1)S(1)}, u32[]{:S(2)}, u32[]{:S(2)}) collective-permute-start(bf16[64,1024]{1,0:T(8,128)(2,1)S(1)} %get-tuple-element.58), channel_id=1, source_target_pairs={{0,4},{4,0},{8,12},{12,8},{1,5},{5,1},{9,13},{13,9},{2,6},{6,2},{1... | collective-permute-start | bytes 393224 | tf_op jit(solution)/shard_map/ppermute | solution.py:392
  35.3 1.3 %collective-permute-start.3 = (bf16[64,1024]{1,0:T(8,128)(2,1)S(1)}, bf16[64,1024]{1,0:T(8,128)(2,1)S(1)}, u32[]{:S(2)}, u32[]{:S(2)}) collective-permute-start(bf16[64,1024]{1,0:T(8,128)(2,1)S(1)} %get-tuple-element.59), channel_id=1, source_target_pairs={{0,8},{4,12},{8,0},{12,4},{1,9},{5,13},{9,1},{13,5},{2,10},{6,14},... | collective-permute-start | bytes 393224 | tf_op jit(solution)/shard_map/ppermute | solution.py:392
  36.7 0.0 collective-permute-done.6.refs_1_
  36.7 1.5 %collective-permute-start.4 = (bf16[64,1024]{1,0:T(8,128)(2,1)S(1)}, bf16[64,1024]{1,0:T(8,128)(2,1)S(1)}, u32[]{:S(2)}, u32[]{:S(2)}) collective-permute-start(bf16[64,1024]{1,0:T(8,128)(2,1)S(1)} %get-tuple-element.60), channel_id=1, source_target_pairs={{0,12},{4,8},{8,4},{12,0},{1,13},{5,9},{9,5},{13,1},{2,14},{6,10},... | collective-permute-start | bytes 393224 | tf_op jit(solution)/shard_map/ppermute | solution.py:392
  38.2 4.5 %stack.15.refs_6_ = f32[4,8,1024]{2,1,0:T(8,128)S(1)} custom-call(s32[1]{0:T(128)S(6)} %select_n.64.tiles_ref, s32[2,208]{1,0:T(2,128)S(1)} %broadcast_add_fusion.place_ref, s32[52]{0:T(128)S(1)} %broadcast_minimum_fusion.groups_ref, f32[4]{0:T(128)S(1)} %convert_rsqrt_fusion.norm_ref, bf16[128,1024]{1,0:T(8,128)(2,1)S(1)} %get-tuple-element.67.refs_0_, ...), custom_call_target="tpu_custom_call" | custom-call | tf_op jit(solution)/shard_map/stack/pallas_call | solution.py:381
  42.8 3.4 %stack.16.refs_7_ = f32[4,4,1024]{2,1,0:T(4,128)S(1)} custom-call(s32[1]{0:T(128)S(6)} %select_n.64.tiles_ref, s32[2,208]{1,0:T(2,128)S(1)} %broadcast_add_fusion.place_ref, s32[52]{0:T(128)S(1)} %broadcast_minimum_fusion.groups_ref, f32[4]{0:T(128)S(1)} %convert_rsqrt_fusion.norm_ref, bf16[64,1024]{1,0:T(8,128)(2,1)S(1)} %get-tuple-element.71.refs_0_, ...), custom_call_target="tpu_custom_call" | custom-call | tf_op jit(solution)/shard_map/stack/pallas_call | solution.py:381
  46.2 2.7 %collective-permute-done.3.refs_2_ = bf16[64,1024]{1,0:T(8,128)(2,1)S(1)} collective-permute-done((bf16[64,1024]{1,0:T(8,128)(2,1)S(1)}, bf16[64,1024]{1,0:T(8,128)(2,1)S(1)}, u32[]{:S(2)}, u32[]{:S(2)}) %collective-permute-start.3) | collective-permute-done | bytes 131104 | tf_op jit(solution)/shard_map/ppermute | solution.py:392
  48.8 3.3 %stack.17 = (bf16[4,64,128]{2,1,0:T(8,128)(2,1)S(1)}, bf16[4,64,128]{2,1,0:T(8,128)(2,1)S(1)}) custom-call(s32[1]{0:T(128)S(6)} %select_n.64.tiles_ref, s32[2,208]{1,0:T(2,128)S(1)} %broadcast_add_fusion.place_ref, s32[52]{0:T(128)S(1)} %broadcast_minimum_fusion.groups_ref, f32[4]{0:T(128)S(1)} %convert_rsqrt_fusion.norm_ref, ...), custom_call_target="tpu_custom_call" | custom-call | tf_op jit(solution)/shard_map/stack/pallas_call | solution.py:381
  52.2 0.1 collective-permute-start.9
  52.2 1.2 %collective-permute-done.9 = bf16[4,64,128]{2,1,0:T(8,128)(2,1)S(1)} collective-permute-done((bf16[4,64,128]{2,1,0:T(8,128)(2,1)S(1)}, bf16[4,64,128]{2,1,0:T(8,128)(2,1)S(1)}, u32[]{:S(2)}, u32[]{:S(2)}) %collective-permute-start.9) | collective-permute-done | bytes 65568 | tf_op jit(solution)/shard_map/ppermute | solution.py:447
  53.5 2.9 %collective-permute-start.10 = (bf16[2,64,128]{2,1,0:T(8,128)(2,1)S(1)}, bf16[2,64,128]{2,1,0:T(8,128)(2,1)S(1)}, u32[]{:S(2)}, u32[]{:S(2)}) collective-permute-start(bf16[2,64,128]{2,1,0:T(8,128)(2,1)S(1)} %get-tuple-element.85), channel_id=1, source_target_pairs={{0,12},{4,8},{8,4},{12,0},{1,13},{5,9},{9,5},{13,1},{2,14},{6,10},... | collective-permute-start | bytes 98312 | tf_op jit(solution)/shard_map/ppermute | solution.py:392
  56.4 1.9 %collective-permute-start.11 = (bf16[2,64,128]{2,1,0:T(8,128)(2,1)S(1)}, bf16[2,64,128]{2,1,0:T(8,128)(2,1)S(1)}, u32[]{:S(2)}, u32[]{:S(2)}) collective-permute-start(bf16[2,64,128]{2,1,0:T(8,128)(2,1)S(1)} %get-tuple-element.86), channel_id=1, source_target_pairs={{0,8},{4,12},{8,0},{12,4},{1,9},{5,13},{9,1},{13,5},{2,10},{6,14},... | collective-permute-start | bytes 98312 | tf_op jit(solution)/shard_map/ppermute | solution.py:392
  58.3 0.5 collective-permute-start.12
  58.8 0.5 collective-permute-done.10.refs_0_
  59.3 2.0 %collective-permute-done.11.refs_1_ = bf16[2,64,128]{2,1,0:T(8,128)(2,1)S(1)} collective-permute-done((bf16[2,64,128]{2,1,0:T(8,128)(2,1)S(1)}, bf16[2,64,128]{2,1,0:T(8,128)(2,1)S(1)}, u32[]{:S(2)}, u32[]{:S(2)}) %collective-permute-start.11) | collective-permute-done | bytes 32800 | tf_op jit(solution)/shard_map/ppermute | solution.py:392
  61.3 0.9 %collective-permute-done.12.refs_2_ = bf16[2,64,128]{2,1,0:T(8,128)(2,1)S(1)} collective-permute-done((bf16[2,64,128]{2,1,0:T(8,128)(2,1)S(1)}, bf16[2,64,128]{2,1,0:T(8,128)(2,1)S(1)}, u32[]{:S(2)}, u32[]{:S(2)}) %collective-permute-start.12) | collective-permute-done | bytes 32800 | tf_op jit(solution)/shard_map/ppermute | solution.py:392
  62.2 0.7 %place.1 = f32[4,128,128]{2,1,0:T(8,128)} custom-call(s32[1]{0:T(128)} %bitcast.refs_5_.piece_ref, bf16[2,64,128]{2,1,0:T(8,128)(2,1)S(1)} %collective-permute-done.10.refs_0_, bf16[2,64,128]{2,1,0:T(8,128)(2,1)S(1)} %collective-permute-done.11.refs_1_, bf16[2,64,128]{2,1,0:T(8,128)(2,1)S(1)} %collective-permute-done.12.refs_2_, ...), custom_call_target="tpu_custom_call" | custom-call | tf_op jit(solution)/shard_map/place/pallas_call | solution.py:450
  (27 shorter events, 0.2 us)
Async XLA Ops:
  0.0 12.1 %copy-start.1 = (s32[4,40]{1,0:T(4,128)S(1)}, s32[4,40]{1,0:T(4,128)}, u32[]{:S(2)}) copy-start(s32[4,40]{1,0:T(4,128)} %param.7) | copy-start | bytes 1924
  0.0 12.2 %copy-start.2 = (s32[4]{0:T(128)S(1)}, s32[4]{0:T(128)}, u32[]{:S(2)}) copy-start(s32[4]{0:T(128)} %param.6) | copy-start | bytes 52
  0.0 14.6 %copy-start = (s32[4,40,2]{1,2,0:T(2,128)S(1)}, s32[4,40,2]{1,2,0:T(2,128)}, u32[]{:S(2)}) copy-start(s32[4,40,2]{1,2,0:T(2,128)} %param.5) | copy-start | bytes 3844
  1.0 17.7 %collective-permute-start = (bf16[128,1024]{1,0:T(8,128)(2,1)S(1)}, bf16[128,1024]{1,0:T(8,128)(2,1)S(1)}, u32[]{:S(2)}, u32[]{:S(2)}) collective-permute-start(bf16[128,1024]{1,0:T(8,128)(2,1)S(1)} %dynamic-slice_bitcast_fusion.7), channel_id=1, source_target_pairs={{0,8},{4,12},{8,0},{12,4},{1,9},{5,13},{9,1},{13,5},{2,10},{6,14},... | collective-permute-start | bytes 786440 | tf_op jit(solution)/shard_map/ppermute | solution.py:392
  10.5 24.9 %collective-permute-start.5 = (bf16[128,1024]{1,0:T(8,128)(2,1)S(1)}, bf16[128,1024]{1,0:T(8,128)(2,1)S(1)}, u32[]{:S(2)}, u32[]{:S(2)}) collective-permute-start(bf16[128,1024]{1,0:T(8,128)(2,1)S(1)} %get-tuple-element.70), channel_id=1, source_target_pairs={{0,4},{4,0},{8,12},{12,8},{1,5},{5,1},{9,13},{13,9},{2,6},{6,2},{1... | collective-permute-start | bytes 786440 | tf_op jit(solution)/shard_map/ppermute | solution.py:392
  12.1 12.8 %collective-permute-start.1 = (bf16[128,1024]{1,0:T(8,128)(2,1)S(1)}, bf16[128,1024]{1,0:T(8,128)(2,1)S(1)}, u32[]{:S(2)}, u32[]{:S(2)}) collective-permute-start(bf16[128,1024]{1,0:T(8,128)(2,1)S(1)} %get-tuple-element.57), channel_id=1, source_target_pairs={{0,12},{4,8},{8,4},{12,0},{1,13},{5,9},{9,5},{13,1},{2,14},{6,10},... | collective-permute-start | bytes 786440 | tf_op jit(solution)/shard_map/ppermute | solution.py:392
  20.4 16.3 %collective-permute-start.6 = (bf16[64,1024]{1,0:T(8,128)(2,1)S(1)}, bf16[64,1024]{1,0:T(8,128)(2,1)S(1)}, u32[]{:S(2)}, u32[]{:S(2)}) collective-permute-start(bf16[64,1024]{1,0:T(8,128)(2,1)S(1)} %get-tuple-element.72), channel_id=1, source_target_pairs={{0,4},{4,0},{8,12},{12,8},{1,5},{5,1},{9,13},{13,9},{2,6},{6,2},{1... | collective-permute-start | bytes 393224 | tf_op jit(solution)/shard_map/ppermute | solution.py:392
  20.7 22.1 %collective-permute-start.7 = (bf16[64,1024]{1,0:T(8,128)(2,1)S(1)}, bf16[64,1024]{1,0:T(8,128)(2,1)S(1)}, u32[]{:S(2)}, u32[]{:S(2)}) collective-permute-start(bf16[64,1024]{1,0:T(8,128)(2,1)S(1)} %get-tuple-element.73), channel_id=1, source_target_pairs={{0,8},{4,12},{8,0},{12,4},{1,9},{5,13},{9,1},{13,5},{2,10},{6,14},... | collective-permute-start | bytes 393224 | tf_op jit(solution)/shard_map/ppermute | solution.py:392
  24.2 18.6 %collective-permute-start.8 = (bf16[64,1024]{1,0:T(8,128)(2,1)S(1)}, bf16[64,1024]{1,0:T(8,128)(2,1)S(1)}, u32[]{:S(2)}, u32[]{:S(2)}) collective-permute-start(bf16[64,1024]{1,0:T(8,128)(2,1)S(1)} %get-tuple-element.74), channel_id=1, source_target_pairs={{0,12},{4,8},{8,4},{12,0},{1,13},{5,9},{9,5},{13,1},{2,14},{6,10},... | collective-permute-start | bytes 393224 | tf_op jit(solution)/shard_map/ppermute | solution.py:392
  24.9 21.2 %collective-permute-start.2 = (bf16[64,1024]{1,0:T(8,128)(2,1)S(1)}, bf16[64,1024]{1,0:T(8,128)(2,1)S(1)}, u32[]{:S(2)}, u32[]{:S(2)}) collective-permute-start(bf16[64,1024]{1,0:T(8,128)(2,1)S(1)} %get-tuple-element.58), channel_id=1, source_target_pairs={{0,4},{4,0},{8,12},{12,8},{1,5},{5,1},{9,13},{13,9},{2,6},{6,2},{1... | collective-permute-start | bytes 393224 | tf_op jit(solution)/shard_map/ppermute | solution.py:392
  35.3 13.5 %collective-permute-start.3 = (bf16[64,1024]{1,0:T(8,128)(2,1)S(1)}, bf16[64,1024]{1,0:T(8,128)(2,1)S(1)}, u32[]{:S(2)}, u32[]{:S(2)}) collective-permute-start(bf16[64,1024]{1,0:T(8,128)(2,1)S(1)} %get-tuple-element.59), channel_id=1, source_target_pairs={{0,8},{4,12},{8,0},{12,4},{1,9},{5,13},{9,1},{13,5},{2,10},{6,14},... | collective-permute-start | bytes 393224 | tf_op jit(solution)/shard_map/ppermute | solution.py:392
  36.7 12.1 %collective-permute-start.4 = (bf16[64,1024]{1,0:T(8,128)(2,1)S(1)}, bf16[64,1024]{1,0:T(8,128)(2,1)S(1)}, u32[]{:S(2)}, u32[]{:S(2)}) collective-permute-start(bf16[64,1024]{1,0:T(8,128)(2,1)S(1)} %get-tuple-element.60), channel_id=1, source_target_pairs={{0,12},{4,8},{8,4},{12,0},{1,13},{5,9},{9,5},{13,1},{2,14},{6,10},... | collective-permute-start | bytes 393224 | tf_op jit(solution)/shard_map/ppermute | solution.py:392
  52.2 1.3 %collective-permute-start.9 = (bf16[4,64,128]{2,1,0:T(8,128)(2,1)S(1)}, bf16[4,64,128]{2,1,0:T(8,128)(2,1)S(1)}, u32[]{:S(2)}, u32[]{:S(2)}) collective-permute-start(bf16[4,64,128]{2,1,0:T(8,128)(2,1)S(1)} %get-tuple-element.76), channel_id=1, source_target_pairs={{0,1},{1,0},{2,3},{3,2},{4,5},{5,4},{6,7},{7,6},{8,9},{9,8},{10,11... | collective-permute-start | bytes 196616 | tf_op jit(solution)/shard_map/ppermute | solution.py:447
  53.5 5.8 %collective-permute-start.10 = (bf16[2,64,128]{2,1,0:T(8,128)(2,1)S(1)}, bf16[2,64,128]{2,1,0:T(8,128)(2,1)S(1)}, u32[]{:S(2)}, u32[]{:S(2)}) collective-permute-start(bf16[2,64,128]{2,1,0:T(8,128)(2,1)S(1)} %get-tuple-element.85), channel_id=1, source_target_pairs={{0,12},{4,8},{8,4},{12,0},{1,13},{5,9},{9,5},{13,1},{2,14},{6,10},... | collective-permute-start | bytes 98312 | tf_op jit(solution)/shard_map/ppermute | solution.py:392
  56.4 4.9 %collective-permute-start.11 = (bf16[2,64,128]{2,1,0:T(8,128)(2,1)S(1)}, bf16[2,64,128]{2,1,0:T(8,128)(2,1)S(1)}, u32[]{:S(2)}, u32[]{:S(2)}) collective-permute-start(bf16[2,64,128]{2,1,0:T(8,128)(2,1)S(1)} %get-tuple-element.86), channel_id=1, source_target_pairs={{0,8},{4,12},{8,0},{12,4},{1,9},{5,13},{9,1},{13,5},{2,10},{6,14},... | collective-permute-start | bytes 98312 | tf_op jit(solution)/shard_map/ppermute | solution.py:392
  58.3 3.9 %collective-permute-start.12 = (bf16[2,64,128]{2,1,0:T(8,128)(2,1)S(1)}, bf16[2,64,128]{2,1,0:T(8,128)(2,1)S(1)}, u32[]{:S(2)}, u32[]{:S(2)}) collective-permute-start(bf16[2,64,128]{2,1,0:T(8,128)(2,1)S(1)} %get-tuple-element.87), channel_id=1, source_target_pairs={{0,4},{4,0},{8,12},{12,8},{1,5},{5,1},{9,13},{13,9},{2,6},{6,2},{1... | collective-permute-start | bytes 98312 | tf_op jit(solution)/shard_map/ppermute | solution.py:392

commit v6 on v5

--- a/solution.py
+++ b/solution.py
@@ -349,7 +349,7 @@
     unit_pairs = PACK_ROWS // min(chunks[-1])
     pieces = parts * cores
     here = (me * cores + core).reshape(1)
-    tile_units = [max(1, rows // chunk_rows(cells, unit_pairs)) for cells, rows in zip(chunks, (256, 128, 128))]
+    tile_units = [max(1, rows // chunk_rows(cells, unit_pairs)) for cells, rows in zip(chunks, (256, 160, 160))]
 
     used, taken, unit_group, norm = pair_order(
         pair_blocks, live_pairs, stack_group, parts, part_blocks, unit_pairs, max(tile_units)

time: 62.9 us -> 62.9 us (level)
  Pallas kernels: 15.2 us -> 14 us
  waiting for transfers between devices: 8.07 us -> 9.06 us
    pallas_call x3, Pallas kernels: 11.2 us -> 10 us  [stack_call(): pl.pallas_call(functools.partial(stack_kernel, len(received), cells, unit...]
    ppermute x12, waiting for transfers between devices: 6.83 us -> 7.82 us  [move(): return lax.ppermute(value, 'pair', [(i, i ^ shift) for i in range(parts)])]
  transfers between devices with their start and end apart: 13 -> 13, of which waited for: 6 -> 6; matrix products, arithmetic and copies ran while one was open for 11% -> 11% of each run, Pallas kernels for 18% -> 16%
where the time goes in v6:
time: 62.9 us; the launch traced here: 62.7 us
  starting transfers between devices  28.8 us (46%)
  Pallas kernels  14 us (22%)
  waiting for transfers between devices  9.06 us (14%)
  local copies, waits for them, and re-layouts  5.81 us (9%)
  between operations  2.82 us (4%)
  other arithmetic  2.19 us (3%)
    ppermute x12, starting transfers between devices, move(): return lax.ppermute(value, 'pair', [(i, i ^ shift) for i in range(parts)])  28.8 us
    pallas_call x3, Pallas kernels, stack_call(): pl.pallas_call(functools.partial(stack_kernel, len(received), cells, unit...  10 us
    ppermute x12, waiting for transfers between devices, move(): return lax.ppermute(value, 'pair', [(i, i ^ shift) for i in range(parts)])  7.82 us
    reshape x3, local copies, waits for them, and re-layouts, raw(): return piece.reshape(part_blocks * SUB_ROWS, width)  4.67 us
    pallas_call x3, Pallas kernels, prepare(): pl.pallas_call(functools.partial(prepare_kernel, cells_of), out_shape=sha...  2.1 us
    another operation x4, other arithmetic  1.45 us
  transfers between devices with their start and end apart: 13, of which 6 were waited for; matrix products, arithmetic and copies ran while one was open for 11% of the time, Pallas kernels for 16%

profile of v6, /device:TPU:0, one launch (start us, length us, event | category | flops | bytes accessed | tf_op | source)
XLA Modules:
  0.0 62.7 jit_solution(8708519344931028043)
XLA Ops:
  0.0 1.0 %dynamic-slice_bitcast_fusion.7 = bf16[128,1024]{1,0:T(8,128)(2,1)S(1)} fusion(bf16[16,1,128,1024]{3,2,1,0:T(8,128)(2,1)} %param.4, s32[]{:T(128)S(6)} %select_n.65), kind=kLoop, calls=%fused_computation.8 | loop fusion | bytes 524292 | tf_op jit(solution)/shard_map/reshape | solution.py:399
  1.0 4.1 %collective-permute-start = (bf16[128,1024]{1,0:T(8,128)(2,1)S(1)}, bf16[128,1024]{1,0:T(8,128)(2,1)S(1)}, u32[]{:S(2)}, u32[]{:S(2)}) collective-permute-start(bf16[128,1024]{1,0:T(8,128)(2,1)S(1)} %dynamic-slice_bitcast_fusion.7), channel_id=1, source_target_pairs={{0,8},{4,12},{8,0},{12,4},{1,9},{5,13},{9,1},{13,5},{2,10},{6,14},... | collective-permute-start | bytes 786440 | tf_op jit(solution)/shard_map/ppermute | solution.py:392
  5.1 1.4 %dynamic-slice_bitcast_fusion.5 = (bf16[128,1024]{1,0:T(8,128)(2,1)S(1)}, bf16[128,1024]{1,0:T(8,128)(2,1)S(1)}) fusion(bf16[16,1,128,1024]{3,2,1,0:T(8,128)(2,1)} %param.4, s32[]{:T(128)S(6)} %select_n.71, s32[]{:T(128)S(6)} %select_n.70), kind=kLoop, calls=%fused_computation.6 | loop fusion | bytes 1048584 | tf_op jit(solution)/shard_map/reshape | solution.py:399
  6.5 0.6 prepare.3
  7.1 2.3 %dynamic-slice_bitcast_fusion = (bf16[128,1024]{1,0:T(8,128)(2,1)S(1)}, bf16[128,1024]{1,0:T(8,128)(2,1)S(1)}, bf16[128,1024]{1,0:T(8,128)(2,1)S(1)}, bf16[128,1024]{1,0:T(8,128)(2,1)S(1)}, bf16[128,1024]{1,0:T(8,128)(2,1)S(1)}) fusion(bf16[16,1,128,1024]{3,2,1,0:T(8,128)(2,1)} %param.4, s32[]{:T(128)S(6)} %select_n.76, s32[]{:T(128)S(6)} %select_n.74, ...), kind=kLoop, calls=%fused_computation.1 | loop fusion | bytes 2621460 | tf_op jit(solution)/shard_map/reshape | solution.py:399
  9.4 1.1 %prepare.4 = (bf16[128,1024]{1,0:T(8,128)(2,1)S(1)}, bf16[64,1024]{1,0:T(8,128)(2,1)S(1)}, bf16[64,1024]{1,0:T(8,128)(2,1)S(1)}, bf16[64,1024]{1,0:T(8,128)(2,1)...) custom-call(bf16[128,1024]{1,0:T(8,128)(2,1)S(1)} %get-tuple-element, ...), custom_call_target="tpu_custom_call" | custom-call | tf_op jit(solution)/shard_map/prepare/pallas_call | solution.py:115
  10.5 1.6 %collective-permute-start.5 = (bf16[128,1024]{1,0:T(8,128)(2,1)S(1)}, bf16[128,1024]{1,0:T(8,128)(2,1)S(1)}, u32[]{:S(2)}, u32[]{:S(2)}) collective-permute-start(bf16[128,1024]{1,0:T(8,128)(2,1)S(1)} %get-tuple-element.70), channel_id=1, source_target_pairs={{0,4},{4,0},{8,12},{12,8},{1,5},{5,1},{9,13},{13,9},{2,6},{6,2},{1... | collective-permute-start | bytes 786440 | tf_op jit(solution)/shard_map/ppermute | solution.py:392
  12.1 0.0 collective-permute-start.1
  12.1 0.1 eq.40
  12.2 0.1 iota_compare_fusion.3
  12.3 0.1 lt.47
  12.4 0.1 convert_reduce_fusion
  12.5 0.2 reduce-window.10
  12.7 1.2 %reduce-window.11 = s32[4,2,128]{2,1,0:T(2,128)S(1)} reduce-window(s32[4,2,128]{2,1,0:T(2,128)S(1)} %reshape.204, s32[]{:T(128)} %constant.111.clone.1), window={size=1x1x128 pad=0_0x0_0x127_0}, to_apply=%region_2.3 | reduce-window | flops 130048 | bytes 8196 | tf_op jit(solution)/shard_map/reduce-window.1
  14.0 0.1 slice.36
  14.0 0.1 copy.10
  14.2 0.1 copy.11
  14.3 0.1 add_bitcast_fusion
  14.4 0.1 fusion.10
  14.5 0.1 iota_compare_fusion
  14.6 0.1 reshape.196
  14.7 0.1 select_reduce_fusion
  14.8 0.6 slice.27
  18.0 0.7 %collective-permute-done.refs_0_ = bf16[128,1024]{1,0:T(8,128)(2,1)S(1)} collective-permute-done((bf16[128,1024]{1,0:T(8,128)(2,1)S(1)}, bf16[128,1024]{1,0:T(8,128)(2,1)S(1)}, u32[]{:S(2)}, u32[]{:S(2)}) %collective-permute-start) | collective-permute-done | bytes 262176 | tf_op jit(solution)/shard_map/ppermute | solution.py:392
  18.8 0.4 prepare.5.refs_2_
  19.2 1.1 %table.1.refs_4_ = bf16[1024,512]{1,0:T(8,128)(2,1)S(1)} custom-call(s32[1]{0:T(128)S(6)} %select_n.64.used_ref), custom_call_target="tpu_custom_call" | custom-call | tf_op jit(solution)/shard_map/table/pallas_call | solution.py:61
  20.4 0.2 collective-permute-start.6
  20.6 0.1 convert_reduce_fusion.1
  20.7 3.5 %collective-permute-start.7 = (bf16[64,1024]{1,0:T(8,128)(2,1)S(1)}, bf16[64,1024]{1,0:T(8,128)(2,1)S(1)}, u32[]{:S(2)}, u32[]{:S(2)}) collective-permute-start(bf16[64,1024]{1,0:T(8,128)(2,1)S(1)} %get-tuple-element.73), channel_id=1, source_target_pairs={{0,8},{4,12},{8,0},{12,4},{1,9},{5,13},{9,1},{13,5},{2,10},{6,14},... | collective-permute-start | bytes 393224 | tf_op jit(solution)/shard_map/ppermute | solution.py:392
  24.2 0.7 %collective-permute-start.8 = (bf16[64,1024]{1,0:T(8,128)(2,1)S(1)}, bf16[64,1024]{1,0:T(8,128)(2,1)S(1)}, u32[]{:S(2)}, u32[]{:S(2)}) collective-permute-start(bf16[64,1024]{1,0:T(8,128)(2,1)S(1)} %get-tuple-element.74), channel_id=1, source_target_pairs={{0,12},{4,8},{8,4},{12,0},{1,13},{5,9},{9,5},{13,1},{2,14},{6,10},... | collective-permute-start | bytes 393224 | tf_op jit(solution)/shard_map/ppermute | solution.py:392
  24.9 0.0 collective-permute-done.1.refs_3_
  24.9 10.4 %collective-permute-start.2 = (bf16[64,1024]{1,0:T(8,128)(2,1)S(1)}, bf16[64,1024]{1,0:T(8,128)(2,1)S(1)}, u32[]{:S(2)}, u32[]{:S(2)}) collective-permute-start(bf16[64,1024]{1,0:T(8,128)(2,1)S(1)} %get-tuple-element.58), channel_id=1, source_target_pairs={{0,4},{4,0},{8,12},{12,8},{1,5},{5,1},{9,13},{13,9},{2,6},{6,2},{1... | collective-permute-start | bytes 393224 | tf_op jit(solution)/shard_map/ppermute | solution.py:392
  35.3 1.3 %collective-permute-start.3 = (bf16[64,1024]{1,0:T(8,128)(2,1)S(1)}, bf16[64,1024]{1,0:T(8,128)(2,1)S(1)}, u32[]{:S(2)}, u32[]{:S(2)}) collective-permute-start(bf16[64,1024]{1,0:T(8,128)(2,1)S(1)} %get-tuple-element.59), channel_id=1, source_target_pairs={{0,8},{4,12},{8,0},{12,4},{1,9},{5,13},{9,1},{13,5},{2,10},{6,14},... | collective-permute-start | bytes 393224 | tf_op jit(solution)/shard_map/ppermute | solution.py:392
  36.7 0.0 collective-permute-done.6.refs_1_
  36.7 1.5 %collective-permute-start.4 = (bf16[64,1024]{1,0:T(8,128)(2,1)S(1)}, bf16[64,1024]{1,0:T(8,128)(2,1)S(1)}, u32[]{:S(2)}, u32[]{:S(2)}) collective-permute-start(bf16[64,1024]{1,0:T(8,128)(2,1)S(1)} %get-tuple-element.60), channel_id=1, source_target_pairs={{0,12},{4,8},{8,4},{12,0},{1,13},{5,9},{9,5},{13,1},{2,14},{6,10},... | collective-permute-start | bytes 393224 | tf_op jit(solution)/shard_map/ppermute | solution.py:392
  38.2 3.7 %stack.15.refs_6_ = f32[4,8,1024]{2,1,0:T(8,128)S(1)} custom-call(s32[1]{0:T(128)S(6)} %select_n.77.tiles_ref, s32[2,216]{1,0:T(2,128)S(1)} %broadcast_add_fusion.place_ref, s32[54]{0:T(128)S(1)} %broadcast_minimum_fusion.groups_ref, f32[4]{0:T(128)S(1)} %convert_rsqrt_fusion.norm_ref, bf16[128,1024]{1,0:T(8,128)(2,1)S(1)} %get-tuple-element.67.refs_0_, ...), custom_call_target="tpu_custom_call" | custom-call | tf_op jit(solution)/shard_map/stack/pallas_call | solution.py:381
  42.0 3.2 %stack.16.refs_7_ = f32[4,4,1024]{2,1,0:T(4,128)S(1)} custom-call(s32[1]{0:T(128)S(6)} %select_n.66.tiles_ref, s32[2,216]{1,0:T(2,128)S(1)} %broadcast_add_fusion.place_ref, s32[54]{0:T(128)S(1)} %broadcast_minimum_fusion.groups_ref, f32[4]{0:T(128)S(1)} %convert_rsqrt_fusion.norm_ref, bf16[64,1024]{1,0:T(8,128)(2,1)S(1)} %get-tuple-element.71.refs_0_, ...), custom_call_target="tpu_custom_call" | custom-call | tf_op jit(solution)/shard_map/stack/pallas_call | solution.py:381
  45.2 3.6 %collective-permute-done.3.refs_2_ = bf16[64,1024]{1,0:T(8,128)(2,1)S(1)} collective-permute-done((bf16[64,1024]{1,0:T(8,128)(2,1)S(1)}, bf16[64,1024]{1,0:T(8,128)(2,1)S(1)}, u32[]{:S(2)}, u32[]{:S(2)}) %collective-permute-start.3) | collective-permute-done | bytes 131104 | tf_op jit(solution)/shard_map/ppermute | solution.py:392
  48.8 3.1 %stack.17 = (bf16[4,64,128]{2,1,0:T(8,128)(2,1)S(1)}, bf16[4,64,128]{2,1,0:T(8,128)(2,1)S(1)}) custom-call(s32[1]{0:T(128)S(6)} %select_n.66.tiles_ref, s32[2,216]{1,0:T(2,128)S(1)} %broadcast_add_fusion.place_ref, s32[54]{0:T(128)S(1)} %broadcast_minimum_fusion.groups_ref, f32[4]{0:T(128)S(1)} %convert_rsqrt_fusion.norm_ref, ...), custom_call_target="tpu_custom_call" | custom-call | tf_op jit(solution)/shard_map/stack/pallas_call | solution.py:381
  52.0 0.1 collective-permute-start.9
  52.0 1.2 %collective-permute-done.9 = bf16[4,64,128]{2,1,0:T(8,128)(2,1)S(1)} collective-permute-done((bf16[4,64,128]{2,1,0:T(8,128)(2,1)S(1)}, bf16[4,64,128]{2,1,0:T(8,128)(2,1)S(1)}, u32[]{:S(2)}, u32[]{:S(2)}) %collective-permute-start.9) | collective-permute-done | bytes 65568 | tf_op jit(solution)/shard_map/ppermute | solution.py:447
  53.3 2.9 %collective-permute-start.10 = (bf16[2,64,128]{2,1,0:T(8,128)(2,1)S(1)}, bf16[2,64,128]{2,1,0:T(8,128)(2,1)S(1)}, u32[]{:S(2)}, u32[]{:S(2)}) collective-permute-start(bf16[2,64,128]{2,1,0:T(8,128)(2,1)S(1)} %get-tuple-element.85), channel_id=1, source_target_pairs={{0,12},{4,8},{8,4},{12,0},{1,13},{5,9},{9,5},{13,1},{2,14},{6,10},... | collective-permute-start | bytes 98312 | tf_op jit(solution)/shard_map/ppermute | solution.py:392
  56.2 1.9 %collective-permute-start.11 = (bf16[2,64,128]{2,1,0:T(8,128)(2,1)S(1)}, bf16[2,64,128]{2,1,0:T(8,128)(2,1)S(1)}, u32[]{:S(2)}, u32[]{:S(2)}) collective-permute-start(bf16[2,64,128]{2,1,0:T(8,128)(2,1)S(1)} %get-tuple-element.86), channel_id=1, source_target_pairs={{0,8},{4,12},{8,0},{12,4},{1,9},{5,13},{9,1},{13,5},{2,10},{6,14},... | collective-permute-start | bytes 98312 | tf_op jit(solution)/shard_map/ppermute | solution.py:392
  58.1 0.5 collective-permute-start.12
  58.6 0.5 collective-permute-done.10.refs_0_
  59.1 2.0 %collective-permute-done.11.refs_1_ = bf16[2,64,128]{2,1,0:T(8,128)(2,1)S(1)} collective-permute-done((bf16[2,64,128]{2,1,0:T(8,128)(2,1)S(1)}, bf16[2,64,128]{2,1,0:T(8,128)(2,1)S(1)}, u32[]{:S(2)}, u32[]{:S(2)}) %collective-permute-start.11) | collective-permute-done | bytes 32800 | tf_op jit(solution)/shard_map/ppermute | solution.py:392
  61.1 0.9 %collective-permute-done.12.refs_2_ = bf16[2,64,128]{2,1,0:T(8,128)(2,1)S(1)} collective-permute-done((bf16[2,64,128]{2,1,0:T(8,128)(2,1)S(1)}, bf16[2,64,128]{2,1,0:T(8,128)(2,1)S(1)}, u32[]{:S(2)}, u32[]{:S(2)}) %collective-permute-start.12) | collective-permute-done | bytes 32800 | tf_op jit(solution)/shard_map/ppermute | solution.py:392
  62.0 0.7 %place.1 = f32[4,128,128]{2,1,0:T(8,128)} custom-call(s32[1]{0:T(128)} %bitcast.refs_5_.piece_ref, bf16[2,64,128]{2,1,0:T(8,128)(2,1)S(1)} %collective-permute-done.10.refs_0_, bf16[2,64,128]{2,1,0:T(8,128)(2,1)S(1)} %collective-permute-done.11.refs_1_, bf16[2,64,128]{2,1,0:T(8,128)(2,1)S(1)} %collective-permute-done.12.refs_2_, ...), custom_call_target="tpu_custom_call" | custom-call | tf_op jit(solution)/shard_map/place/pallas_call | solution.py:450
  (27 shorter events, 0.2 us)
Async XLA Ops:
  0.0 12.1 %copy-start.1 = (s32[4,40]{1,0:T(4,128)S(1)}, s32[4,40]{1,0:T(4,128)}, u32[]{:S(2)}) copy-start(s32[4,40]{1,0:T(4,128)} %param.7) | copy-start | bytes 1924
  0.0 12.2 %copy-start.2 = (s32[4]{0:T(128)S(1)}, s32[4]{0:T(128)}, u32[]{:S(2)}) copy-start(s32[4]{0:T(128)} %param.6) | copy-start | bytes 52
  0.0 14.6 %copy-start = (s32[4,40,2]{1,2,0:T(2,128)S(1)}, s32[4,40,2]{1,2,0:T(2,128)}, u32[]{:S(2)}) copy-start(s32[4,40,2]{1,2,0:T(2,128)} %param.5) | copy-start | bytes 3844
  1.0 17.7 %collective-permute-start = (bf16[128,1024]{1,0:T(8,128)(2,1)S(1)}, bf16[128,1024]{1,0:T(8,128)(2,1)S(1)}, u32[]{:S(2)}, u32[]{:S(2)}) collective-permute-start(bf16[128,1024]{1,0:T(8,128)(2,1)S(1)} %dynamic-slice_bitcast_fusion.7), channel_id=1, source_target_pairs={{0,8},{4,12},{8,0},{12,4},{1,9},{5,13},{9,1},{13,5},{2,10},{6,14},... | collective-permute-start | bytes 786440 | tf_op jit(solution)/shard_map/ppermute | solution.py:392
  10.5 24.9 %collective-permute-start.5 = (bf16[128,1024]{1,0:T(8,128)(2,1)S(1)}, bf16[128,1024]{1,0:T(8,128)(2,1)S(1)}, u32[]{:S(2)}, u32[]{:S(2)}) collective-permute-start(bf16[128,1024]{1,0:T(8,128)(2,1)S(1)} %get-tuple-element.70), channel_id=1, source_target_pairs={{0,4},{4,0},{8,12},{12,8},{1,5},{5,1},{9,13},{13,9},{2,6},{6,2},{1... | collective-permute-start | bytes 786440 | tf_op jit(solution)/shard_map/ppermute | solution.py:392
  12.1 12.8 %collective-permute-start.1 = (bf16[128,1024]{1,0:T(8,128)(2,1)S(1)}, bf16[128,1024]{1,0:T(8,128)(2,1)S(1)}, u32[]{:S(2)}, u32[]{:S(2)}) collective-permute-start(bf16[128,1024]{1,0:T(8,128)(2,1)S(1)} %get-tuple-element.57), channel_id=1, source_target_pairs={{0,12},{4,8},{8,4},{12,0},{1,13},{5,9},{9,5},{13,1},{2,14},{6,10},... | collective-permute-start | bytes 786440 | tf_op jit(solution)/shard_map/ppermute | solution.py:392
  20.4 16.3 %collective-permute-start.6 = (bf16[64,1024]{1,0:T(8,128)(2,1)S(1)}, bf16[64,1024]{1,0:T(8,128)(2,1)S(1)}, u32[]{:S(2)}, u32[]{:S(2)}) collective-permute-start(bf16[64,1024]{1,0:T(8,128)(2,1)S(1)} %get-tuple-element.72), channel_id=1, source_target_pairs={{0,4},{4,0},{8,12},{12,8},{1,5},{5,1},{9,13},{13,9},{2,6},{6,2},{1... | collective-permute-start | bytes 393224 | tf_op jit(solution)/shard_map/ppermute | solution.py:392
  20.7 21.3 %collective-permute-start.7 = (bf16[64,1024]{1,0:T(8,128)(2,1)S(1)}, bf16[64,1024]{1,0:T(8,128)(2,1)S(1)}, u32[]{:S(2)}, u32[]{:S(2)}) collective-permute-start(bf16[64,1024]{1,0:T(8,128)(2,1)S(1)} %get-tuple-element.73), channel_id=1, source_target_pairs={{0,8},{4,12},{8,0},{12,4},{1,9},{5,13},{9,1},{13,5},{2,10},{6,14},... | collective-permute-start | bytes 393224 | tf_op jit(solution)/shard_map/ppermute | solution.py:392
  24.2 17.8 %collective-permute-start.8 = (bf16[64,1024]{1,0:T(8,128)(2,1)S(1)}, bf16[64,1024]{1,0:T(8,128)(2,1)S(1)}, u32[]{:S(2)}, u32[]{:S(2)}) collective-permute-start(bf16[64,1024]{1,0:T(8,128)(2,1)S(1)} %get-tuple-element.74), channel_id=1, source_target_pairs={{0,12},{4,8},{8,4},{12,0},{1,13},{5,9},{9,5},{13,1},{2,14},{6,10},... | collective-permute-start | bytes 393224 | tf_op jit(solution)/shard_map/ppermute | solution.py:392
  24.9 20.2 %collective-permute-start.2 = (bf16[64,1024]{1,0:T(8,128)(2,1)S(1)}, bf16[64,1024]{1,0:T(8,128)(2,1)S(1)}, u32[]{:S(2)}, u32[]{:S(2)}) collective-permute-start(bf16[64,1024]{1,0:T(8,128)(2,1)S(1)} %get-tuple-element.58), channel_id=1, source_target_pairs={{0,4},{4,0},{8,12},{12,8},{1,5},{5,1},{9,13},{13,9},{2,6},{6,2},{1... | collective-permute-start | bytes 393224 | tf_op jit(solution)/shard_map/ppermute | solution.py:392
  35.3 13.5 %collective-permute-start.3 = (bf16[64,1024]{1,0:T(8,128)(2,1)S(1)}, bf16[64,1024]{1,0:T(8,128)(2,1)S(1)}, u32[]{:S(2)}, u32[]{:S(2)}) collective-permute-start(bf16[64,1024]{1,0:T(8,128)(2,1)S(1)} %get-tuple-element.59), channel_id=1, source_target_pairs={{0,8},{4,12},{8,0},{12,4},{1,9},{5,13},{9,1},{13,5},{2,10},{6,14},... | collective-permute-start | bytes 393224 | tf_op jit(solution)/shard_map/ppermute | solution.py:392
  36.7 12.1 %collective-permute-start.4 = (bf16[64,1024]{1,0:T(8,128)(2,1)S(1)}, bf16[64,1024]{1,0:T(8,128)(2,1)S(1)}, u32[]{:S(2)}, u32[]{:S(2)}) collective-permute-start(bf16[64,1024]{1,0:T(8,128)(2,1)S(1)} %get-tuple-element.60), channel_id=1, source_target_pairs={{0,12},{4,8},{8,4},{12,0},{1,13},{5,9},{9,5},{13,1},{2,14},{6,10},... | collective-permute-start | bytes 393224 | tf_op jit(solution)/shard_map/ppermute | solution.py:392
  52.0 1.3 %collective-permute-start.9 = (bf16[4,64,128]{2,1,0:T(8,128)(2,1)S(1)}, bf16[4,64,128]{2,1,0:T(8,128)(2,1)S(1)}, u32[]{:S(2)}, u32[]{:S(2)}) collective-permute-start(bf16[4,64,128]{2,1,0:T(8,128)(2,1)S(1)} %get-tuple-element.76), channel_id=1, source_target_pairs={{0,1},{1,0},{2,3},{3,2},{4,5},{5,4},{6,7},{7,6},{8,9},{9,8},{10,11... | collective-permute-start | bytes 196616 | tf_op jit(solution)/shard_map/ppermute | solution.py:447
  53.3 5.8 %collective-permute-start.10 = (bf16[2,64,128]{2,1,0:T(8,128)(2,1)S(1)}, bf16[2,64,128]{2,1,0:T(8,128)(2,1)S(1)}, u32[]{:S(2)}, u32[]{:S(2)}) collective-permute-start(bf16[2,64,128]{2,1,0:T(8,128)(2,1)S(1)} %get-tuple-element.85), channel_id=1, source_target_pairs={{0,12},{4,8},{8,4},{12,0},{1,13},{5,9},{9,5},{13,1},{2,14},{6,10},... | collective-permute-start | bytes 98312 | tf_op jit(solution)/shard_map/ppermute | solution.py:392
  56.2 4.9 %collective-permute-start.11 = (bf16[2,64,128]{2,1,0:T(8,128)(2,1)S(1)}, bf16[2,64,128]{2,1,0:T(8,128)(2,1)S(1)}, u32[]{:S(2)}, u32[]{:S(2)}) collective-permute-start(bf16[2,64,128]{2,1,0:T(8,128)(2,1)S(1)} %get-tuple-element.86), channel_id=1, source_target_pairs={{0,8},{4,12},{8,0},{12,4},{1,9},{5,13},{9,1},{13,5},{2,10},{6,14},... | collective-permute-start | bytes 98312 | tf_op jit(solution)/shard_map/ppermute | solution.py:392
  58.1 3.9 %collective-permute-start.12 = (bf16[2,64,128]{2,1,0:T(8,128)(2,1)S(1)}, bf16[2,64,128]{2,1,0:T(8,128)(2,1)S(1)}, u32[]{:S(2)}, u32[]{:S(2)}) collective-permute-start(bf16[2,64,128]{2,1,0:T(8,128)(2,1)S(1)} %get-tuple-element.87), channel_id=1, source_target_pairs={{0,4},{4,0},{8,12},{12,8},{1,5},{5,1},{9,13},{13,9},{2,6},{6,2},{1... | collective-permute-start | bytes 98312 | tf_op jit(solution)/shard_map/ppermute | solution.py:392
